TPU v7x, 32 devices: a whole 2x2x4 slice. The times are simulated.
32 devices in a mesh: tm: 4 (over z), src: 4 (over x, core), rcv: 2 (over y).
Axes of the slice: x: 2, y: 2, z: 4, core: 2. Of those that a mesh axis runs over, the one named last changes fastest.
Arguments:
- src_real: bfloat16 [5, 1024, 2048], P(None, 'tm', 'src'), may hold values from -6 to 6
- src_imag: bfloat16 [5, 1024, 2048], P(None, 'tm', 'src'), may hold values from -6 to 6
- rcv_real: bfloat16 [5, 1024, 2048], P(None, 'tm', 'rcv'), may hold values from -6 to 6
- rcv_imag: bfloat16 [5, 1024, 2048], P(None, 'tm', 'rcv'), may hold values from -6 to 6
- src_pos: float32 [2048], replicated, may hold values from -1 to 1
- rcv_pos: float32 [2048], replicated, may hold values from -1 to 1
- freqs: float32 [5], replicated, may hold values from 60 to 120
Outputs:
- beam: float32 [2048, 2, 5, 2048], P('src', None, None, ('tm', 'rcv'))
All inputs are finite; a program needn't handle non-finite values.
Results may differ from a plain program's by a relative error of at most 0.0052.
Values may be sent and summed in bfloat16 or wider, within the bound.
No kernel may reach another device: no remote copies, remote signals or barrier semaphores. Data moves between devices by JAX's collectives and lax.ppermute only.
A program may use at most 128 MiB of HBM per device.

v0:
```python
import jax
import jax.numpy as jnp
from jax import lax
from jax.sharding import PartitionSpec as P

SRC_ST = 2048
RCV_ST = 2048
SRC_SL = 2048
RCV_SL = 2048


TWO_PI = 6.283185307179586


def grid_points(first, count, total):
    index = (first + jnp.arange(count, dtype=jnp.int32)).astype(jnp.float32)
    return (2.0 * index + 1.0) / total - 1.0


def phases(freqs, slowness, positions):
    return (TWO_PI * freqs)[:, None, None] * slowness[None, :, None] * positions[None, None, :]


def mixed(form, first, second):
    return jnp.einsum(form, first, second, preferred_element_type=jnp.float32)


def receiver_fold(freqs, slow_rcv, locate, piece, start):
    part_real, part_imag = piece
    where = locate(start, part_real.shape[2])
    angle = phases(freqs, slow_rcv, where)
    steer_real = jnp.cos(angle).astype(jnp.bfloat16)
    steer_imag = jnp.sin(angle).astype(jnp.bfloat16)
    new_real = mixed("fab,fqb->faq", part_real, steer_real) - mixed(
        "fab,fqb->faq", part_imag, steer_imag
    )
    new_imag = mixed("fab,fqb->faq", part_real, steer_imag) + mixed(
        "fab,fqb->faq", part_imag, steer_real
    )
    return (new_real, new_imag)


def source_terms(freqs, slow_src, positions, focus_real, focus_imag):
    angle = phases(freqs, slow_src, positions)
    steer_real = jnp.cos(angle).astype(jnp.bfloat16)
    steer_imag = (-jnp.sin(angle)).astype(jnp.bfloat16)
    term_real = mixed("fpa,faq->pfq", steer_real, focus_real) - mixed(
        "fpa,faq->pfq", steer_imag, focus_imag
    )
    term_imag = mixed("fpa,faq->pfq", steer_real, focus_imag) + mixed(
        "fpa,faq->pfq", steer_imag, focus_real
    )
    return (term_real, term_imag)


def shards(src_real, src_imag, rcv_real, rcv_imag, src_pos, rcv_pos, freqs):
    n_time = lax.axis_size("tm")
    n_recv = lax.axis_size("rcv")
    n_source = lax.axis_size("src")
    src_block = src_real.shape[2]
    rcv_block = rcv_real.shape[2]
    windows = src_real.shape[1] * n_time
    q_block = RCV_SL // (n_time * n_recv)
    p_block = SRC_SL // n_source
    src_both = jnp.concatenate([src_real, src_imag], 1)
    rcv_plain = jnp.concatenate([rcv_real, rcv_imag], 1)
    rcv_turned = jnp.concatenate([-rcv_imag, rcv_real], 1)
    part_real = mixed("fwa,fwb->fab", src_both, rcv_plain)
    part_imag = mixed("fwa,fwb->fab", src_both, rcv_turned)
    q_first = (lax.axis_index("tm") * n_recv + lax.axis_index("rcv")) * q_block
    slow_rcv = grid_points(q_first, q_block, RCV_SL)
    sum_real, sum_imag = (
        lax.psum_scatter(part_real, "tm", scatter_dimension=2, tiled=True),
        lax.psum_scatter(part_imag, "tm", scatter_dimension=2, tiled=True),
    )
    sub_width = rcv_block // n_time

    def mapped(start, count):
        column = jnp.arange(count, dtype=jnp.int32)
        block = column // sub_width
        natural = block % n_recv * rcv_block + block // n_recv * sub_width + column % sub_width
        return jnp.take(rcv_pos, natural)

    cross = (sum_real.astype(jnp.bfloat16), sum_imag.astype(jnp.bfloat16))
    focus_real, focus_imag = receiver_fold(
        freqs,
        slow_rcv,
        mapped,
        (
            lax.all_gather(cross[0], ("tm", "rcv"), axis=2, tiled=True),
            lax.all_gather(cross[1], ("tm", "rcv"), axis=2, tiled=True),
        ),
        jnp.int32(0),
    )
    focus_scale = 1.0 / jnp.sqrt(jnp.float32(windows * RCV_ST))
    focus_real = (focus_real * focus_scale).astype(jnp.bfloat16)
    focus_imag = (focus_imag * focus_scale).astype(jnp.bfloat16)
    beam_scale = 1.0 / jnp.sqrt(jnp.float32(SRC_ST))
    own_pos = lax.dynamic_slice_in_dim(src_pos, lax.axis_index("src") * src_block, src_block)
    slow_src = grid_points(jnp.int32(0), p_block * lax.axis_size("src"), SRC_SL)
    term_real, term_imag = source_terms(freqs, slow_src, own_pos, focus_real, focus_imag)
    return lax.psum_scatter(
        jnp.stack([term_real, term_imag], 1) * beam_scale, "src", scatter_dimension=0, tiled=True
    )


def solution(mesh):
    in_specs = (
        P(None, "tm", "src"),
        P(None, "tm", "src"),
        P(None, "tm", "rcv"),
        P(None, "tm", "rcv"),
        P(),
        P(),
        P(),
    )
    out_specs = P("src", None, None, ("tm", "rcv"))
    return jax.shard_map(shards, mesh=mesh, in_specs=in_specs, out_specs=out_specs, check_vma=False)
```

profile of v0, /device:TPU:0, one launch (start us, length us, event | category | flops | bytes accessed | tf_op | source)
XLA Modules:
  0.0 1190.9 jit_solution(2243607770041998882)
XLA Ops:
  6.5 0.0 copy-start
  6.5 0.0 reduce-scatter.6.cloned.1.call-start
  6.5 2.6 copy.15
  9.1 2.4 copy.16
  11.6 0.0 copy-done.2
  11.6 0.7 neg.6
  12.3 9.5 fusion.33
  21.7 0.0 reduce-scatter.6.cloned.1.call-update
  21.8 0.0 reduce-scatter.4.cloned.1.call-start
  21.8 9.9 fusion.29
  31.7 0.0 reduce-scatter.4.cloned.1.call-update
  31.7 0.0 all-gather.5.cloned.1.call-start
  31.8 170.8 %reduce-scatter.6.cloned.1.call-done = f32[5,512,256]{2,1,0:T(8,128)} async-done(((f32[5,512,1024]{2,1,0:T(8,128)}), f32[5,512,256]{2,1,0:T(8,128)}) %reduce-scatter.6.cloned.1.call-update) | async-done | bytes 2621456 | tf_op jit(solution)/shard_map/reduce_scatter | solution.py:74
  202.6 3.0 convert_element_type.41
  205.6 0.0 all-gather.5.cloned.1.call-update
  205.6 0.0 all-gather.3.cloned.1.call-start
  205.7 178.4 %reduce-scatter.4.cloned.1.call-done = f32[5,512,256]{2,1,0:T(8,128)} async-done(((f32[5,512,1024]{2,1,0:T(8,128)}), f32[5,512,256]{2,1,0:T(8,128)}) %reduce-scatter.4.cloned.1.call-update) | async-done | bytes 2621456 | tf_op jit(solution)/shard_map/reduce_scatter | solution.py:73
  384.0 2.9 convert_element_type.38
  387.0 0.0 all-gather.3.cloned.1.call-update
  387.0 0.3 reduce-scatter.8.cloned.1.call-start
  387.4 0.0 copy-done
  387.4 11.8 gather_fusion
  399.2 0.8 dynamic_slice.3
  400.0 0.0 copy-done.3
  400.0 0.1 broadcast_multiply_fusion.1
  400.1 0.1 broadcast_multiply_fusion
  400.2 36.0 %fusion.104 = bf16[5,256,2048]{2,1,0:T(8,128)(2,1)} fusion(f32[2048]{0:T(1024)S(1)} %and_select_fusion.4, f32[5,256]{1,0:T(8,128)S(1)} %broadcast_multiply_fusion.1), kind=kLoop, calls=%fused_computation.14.clone.1.clone | loop fusion | flops 5242880 | bytes 5256192 | tf_op jit(solution)/shard_map/fab,fqb->faq/dot_general | solution.py:25
  436.2 35.6 %fusion.108 = bf16[5,256,2048]{2,1,0:T(8,128)(2,1)} fusion(f32[2048]{0:T(1024)S(1)} %and_select_fusion.4, f32[5,256]{1,0:T(8,128)S(1)} %broadcast_multiply_fusion.1), kind=kLoop, calls=%fused_computation.13.clone.1.clone.clone.clone.1 | loop fusion | flops 5242880 | bytes 5256192 | tf_op jit(solution)/shard_map/fab,fqb->faq/dot_general | solution.py:25
  471.7 35.9 %fusion.102 = bf16[5,256,2048]{2,1,0:T(8,128)(2,1)} fusion(f32[2048]{0:T(1024)S(1)} %and_select_fusion.4, f32[5,256]{1,0:T(8,128)S(1)} %broadcast_multiply_fusion.1), kind=kLoop, calls=%fused_computation.14.clone.clone.1 | loop fusion | flops 5242880 | bytes 5256192 | tf_op jit(solution)/shard_map/fab,fqb->faq/dot_general | solution.py:25
  507.6 35.6 %fusion.106 = bf16[5,256,2048]{2,1,0:T(8,128)(2,1)} fusion(f32[2048]{0:T(1024)S(1)} %and_select_fusion.4, f32[5,256]{1,0:T(8,128)S(1)} %broadcast_multiply_fusion.1), kind=kLoop, calls=%fused_computation.13.clone.clone.clone.clone.1 | loop fusion | flops 5242880 | bytes 5256192 | tf_op jit(solution)/shard_map/fab,fqb->faq/dot_general | solution.py:25
  543.2 8.7 fusion.23
  551.9 137.5 %all-gather.3.cloned.1.call-done = bf16[5,512,2048]{2,1,0:T(8,128)(2,1)} async-done(((bf16[5,512,256]{2,1,0:T(8,128)(2,1)}), bf16[5,512,2048]{2,1,0:T(8,128)(2,1)}) %all-gather.3.cloned.1.call-update) | async-done | bytes 10485776 | tf_op jit(solution)/shard_map/all_gather | solution.py:90
  689.4 8.4 multiply_convert_fusion.1
  697.9 0.0 slice-start
  697.9 80.6 %fusion.5 = f32[5,256,2048]{2,1,0:T(8,128)} fusion(bf16[5,512,256]{2,1,0:T(8,128)(2,1)S(1)} %multiply_convert_fusion.1, f32[512]{0:T(512)S(1)} %dynamic_slice.3, f32[5,2048]{1,0:T(8,128)S(1)} %broadcast_multiply_fusion), kind=kOutput, calls=%fused_computation.10 | convolution fusion | flops 2694840320 | bytes 11839488 | tf_op jit(solution)/shard_map/fpa,faq->pfq/dot_general | solution.py:25
  778.4 7.3 fusion.21
  785.7 0.0 slice-done
  785.7 0.0 slice-done.1
  785.7 7.4 multiply_convert_fusion
  793.2 0.0 copy-start.4
  793.2 70.2 %fusion.3 = f32[5,256,2048]{2,1,0:T(8,128)S(1)} fusion(bf16[5,512,256]{2,1,0:T(8,128)(2,1)S(1)} %multiply_convert_fusion, f32[512]{0:T(512)S(1)} %dynamic_slice.3, f32[5,2048]{1,0:T(8,128)S(1)} %broadcast_multiply_fusion), kind=kOutput, calls=%fused_computation.9 | convolution fusion | flops 2694840320 | bytes 11839488 | tf_op jit(solution)/shard_map/fpa,faq->pfq/dot_general | solution.py:25
  863.3 76.5 %subtract_bitcast_fusion = f32[2048,1,5,256]{0,3,2,1:T(8,128)S(1)} fusion(f32[5,256,2048]{2,1,0:T(8,128)S(1)} %copy-done.4, bf16[5,512,256]{2,1,0:T(8,128)(2,1)S(1)} %multiply_convert_fusion, f32[512]{0:T(512)S(1)} %dynamic_slice.3, f32[5,2048]{1,0:T(8,128)S(1)} %broadcast_multiply_fusion), kind=kOutput, calls=%fused_computation.16 | convolution fusion | flops 2702704640 | bytes 22325248 | tf_op jit(solution)/shard_map/fpa,faq->pfq/dot_general | solution.py:25
  939.9 76.5 %add_bitcast_fusion = f32[2048,1,5,256]{0,3,2,1:T(8,128)S(1)} fusion(f32[5,256,2048]{2,1,0:T(8,128)S(1)} %fusion.3, bf16[5,512,256]{2,1,0:T(8,128)(2,1)S(1)} %multiply_convert_fusion.1, f32[512]{0:T(512)S(1)} %dynamic_slice.3, f32[5,2048]{1,0:T(8,128)S(1)} %broadcast_multiply_fusion), kind=kOutput, calls=%fused_computation.15 | convolution fusion | flops 2702704640 | bytes 22325248 | tf_op jit(solution)/shard_map/fpa,faq->pfq/dot_general | solution.py:25
  1016.4 7.5 maximum_multiply_fusion
  1023.9 0.0 reduce-scatter.8.cloned.1.call-update
  1023.9 0.0 copy-start.1
  1024.0 151.4 %reduce-scatter.8.cloned.1.call-done = f32[512,2,5,256]{0,3,2,1:T(8,128)} async-done(((f32[2048,2,5,256]{0,3,2,1:T(8,128)}), f32[512,2,5,256]{0,3,2,1:T(8,128)}) %reduce-scatter.8.cloned.1.call-update) | async-done | bytes 5242896 | tf_op jit(solution)/shard_map/reduce_scatter | solution.py:102
  1175.4 8.7 copy.21
  (13 shorter events, 0.1 us)
Async XLA Ops:
  6.5 380.9 %copy-start = (f32[2048]{0:T(1024)S(1)}, f32[2048]{0:T(1024)}, u32[]{:S(2)}) copy-start(f32[2048]{0:T(1024)} %param.12) | copy-start | bytes 24580
  6.5 5.0 copy-start.2
  6.5 196.1 %reduce-scatter.6.cloned.1.call-start = ((), (), s32[]{:S(2)}) async-start(), calls=%async_computation.5 | async-start | bytes 13107200 | tf_op jit(solution)/shard_map/reduce_scatter | solution.py:74
  21.8 362.3 %reduce-scatter.4.cloned.1.call-start = ((), (), s32[]{:S(2)}) async-start(), calls=%async_computation.3 | async-start | bytes 13107200 | tf_op jit(solution)/shard_map/reduce_scatter | solution.py:73
  31.7 511.5 %all-gather.5.cloned.1.call-start = ((), (), s32[]{:S(2)}) async-start(), calls=%async_computation.6 | async-start | bytes 11796480 | tf_op jit(solution)/shard_map/all_gather | solution.py:91
  205.6 483.8 %all-gather.3.cloned.1.call-start = ((), (), s32[]{:S(2)}) async-start(), calls=%async_computation.4 | async-start | bytes 11796480 | tf_op jit(solution)/shard_map/all_gather | solution.py:90
  387.0 13.0 %copy-start.3 = (f32[5]{0:T(128)S(1)}, f32[5]{0:T(128)}, u32[]{:S(2)}) copy-start(f32[5]{0:T(128)} %param.13) | copy-start | bytes 64
  387.0 788.4 %reduce-scatter.8.cloned.1.call-start = ((), (), s32[]{:S(2)}) async-start(), calls=%async_computation.7 | async-start | bytes 26214400 | tf_op jit(solution)/shard_map/reduce_scatter | solution.py:102
  697.9 87.8 %slice-start = ((s8[5242880]{0:T(1024)(128)(4,1)}), s8[4194304]{0:T(1024)(128)(4,1)S(1)}, s32[]{:S(2)}) async-start(s8[5242880]{0:T(1024)(128)(4,1)} %bitcast.29), calls=%async_computation.8 | async-start | bytes 8388608
  778.4 7.3 slice-start.1
  793.2 70.2 %copy-start.4 = (f32[5,256,2048]{2,1,0:T(8,128)S(1)}, f32[5,256,2048]{2,1,0:T(8,128)}, u32[]{:S(2)}) copy-start(f32[5,256,2048]{2,1,0:T(8,128)} %fusion.5) | copy-start | bytes 31457284
  1023.9 160.2 %copy-start.1 = (f32[2048]{0:T(1024)S(1)}, f32[2048]{0:T(1024)}, u32[]{:S(2)}) copy-start(f32[2048]{0:T(1024)} %param.12) | copy-start | bytes 24580
Sparse Core Ops, SparseCore 0:
  21.9 180.6 reduce-scatter.5
  205.0 179.0 reduce-scatter.3
  386.1 152.0 all-gather.4
  540.1 149.2 all-gather.2
  1024.1 151.2 reduce-scatter.7
where the time goes:
time: 1200 us; the launch traced here: 1190 us
  waiting for transfers between devices  638 us (53%)
  matrix products  355 us (30%)
  other arithmetic  157 us (13%)
  local copies, waits for them, and re-layouts  26.3 us (2%)
  between operations  13.5 us (1%)
    dot_general x10, matrix products, mixed(): return jnp.einsum(form, first, second, preferred_element_type=jnp.float32)  355 us
    reduce_scatter x1, waiting for transfers between devices, shards(): lax.psum_scatter(part_real, 'tm', scatter_dimension=2, tiled=True)  178 us
    reduce_scatter x1, waiting for transfers between devices, shards(): lax.psum_scatter(part_imag, 'tm', scatter_dimension=2, tiled=True)  171 us
    reduce_scatter x1, waiting for transfers between devices, shards(): lax.psum_scatter(jnp.stack([term_real, term_imag], 1) * beam_scale, 'src'...  151 us
    dot_general x4, other arithmetic, mixed(): return jnp.einsum(form, first, second, preferred_element_type=jnp.float32)  143 us
    all_gather x1, waiting for transfers between devices, shards(): lax.all_gather(cross[0], ('tm', 'rcv'), axis=2, tiled=True)  137 us
  transfers between devices with their start and end apart: 5, of which 4 were waited for; matrix products, arithmetic and copies ran while one was open for 15% of the time, Pallas kernels for 0%

commit v1 on v0

--- a/solution.py
+++ b/solution.py
@@ -1,6 +1,8 @@
 import jax
 import jax.numpy as jnp
 from jax import lax
+from jax.experimental import pallas as pl
+from jax.experimental.pallas import tpu as pltpu
 from jax.sharding import PartitionSpec as P
 
 SRC_ST = 2048
@@ -53,7 +55,7 @@
     return (term_real, term_imag)
 
 
-def shards(src_real, src_imag, rcv_real, rcv_imag, src_pos, rcv_pos, freqs):
+def shards_any(src_real, src_imag, rcv_real, rcv_imag, src_pos, rcv_pos, freqs):
     n_time = lax.axis_size("tm")
     n_recv = lax.axis_size("rcv")
     n_source = lax.axis_size("src")
@@ -104,7 +106,241 @@
     )
 
 
+FINE = 32
+CHUNKS = 4
+VMEM = 48 * 1024 * 1024
+
+
+def waves(freq, slowness, positions):
+    angle = ((TWO_PI * freq) * slowness)[:, None] * positions[None, :]
+    return jnp.cos(angle), jnp.sin(angle)
+
+
+def tables(freq, starts, total, positions):
+    coarse = (2.0 * starts.astype(jnp.float32) + 1.0) / total - 1.0
+    fine = 2.0 * jnp.arange(FINE, dtype=jnp.float32) / total
+    return waves(freq, coarse, positions) + waves(freq, fine, positions)
+
+
+def runs(first, count):
+    return first + FINE * jnp.arange(count // FINE, dtype=jnp.int32)
+
+
+def nt(first, second):
+    return lax.dot_general(first, second, (((1,), (1,)), ((), ())), preferred_element_type=jnp.float32)
+
+
+def steered_kernel(sign, scale, n_parts, cos_c, sin_c, cos_f, sin_f, *refs):
+    parts, outs, (steer, spectra) = refs[:n_parts], refs[n_parts:-2], refs[-2:]
+    step = pl.program_id(0)
+    group = cos_c.shape[0]
+    rows = group * FINE
+
+    @pl.when(step == 0)
+    def _():
+        first = 0
+        for part in parts:
+            spectra[:, first : first + part.shape[1]] = part[...]
+            first += part.shape[1]
+
+    for i in range(group):
+        cc, sc = cos_c[i : i + 1, :], sin_c[i : i + 1, :]
+        steer[i * FINE : (i + 1) * FINE, :] = (cc * cos_f[...] - sc * sin_f[...]).astype(jnp.bfloat16)
+        steer[rows + i * FINE : rows + (i + 1) * FINE, :] = (sc * cos_f[...] + cc * sin_f[...]).astype(
+            jnp.bfloat16
+        )
+    found = nt(steer[...], spectra[...])
+    half = found.shape[1] // 2
+    real = (found[:rows, :half] + found[rows:, half:]) * scale
+    imag = (found[:rows, half:] - found[rows:, :half]) * (sign * scale)
+    for k, out in enumerate(outs):
+
+        @pl.when(step == k)
+        def _(out=out):
+            if out.ndim == 2:
+                out[:, :half] = real.astype(out.dtype)
+                out[:, half:] = imag.astype(out.dtype)
+            else:
+                out[:, 0, :] = real
+                out[:, 1, :] = imag
+
+
+def steered(table, parts, steps, sign=1.0, scale=1.0, paired=False):
+    coarse, depth = table[0].shape
+    wide = parts[0].shape[0]
+    group = coarse // steps
+    rows = group * FINE
+    whole = lambda v: pl.BlockSpec(v.shape, lambda i: (0, 0))
+    if paired:
+        shape, spec = jax.ShapeDtypeStruct((rows, 2, wide // 2), jnp.float32), pl.BlockSpec(
+            (rows, 2, wide // 2), lambda i: (0, 0, 0)
+        )
+    else:
+        shape, spec = jax.ShapeDtypeStruct((rows, wide), jnp.bfloat16), pl.BlockSpec((rows, wide), lambda i: (0, 0))
+    return pl.pallas_call(
+        lambda *refs: steered_kernel(sign, scale, len(parts), *refs),
+        grid=(steps,),
+        in_specs=[pl.BlockSpec((group, depth), lambda i: (i, 0))] * 2
+        + [whole(v) for v in table[2:]]
+        + [whole(v) for v in parts],
+        out_specs=[spec] * steps,
+        out_shape=[shape] * steps,
+        scratch_shapes=[pltpu.VMEM((2 * rows, depth), jnp.bfloat16), pltpu.VMEM((wide, depth), jnp.bfloat16)],
+        compiler_params=pltpu.CompilerParams(vmem_limit_bytes=VMEM),
+        cost_estimate=pl.CostEstimate(
+            flops=4 * coarse * FINE * wide * depth, bytes_accessed=2 * wide * depth, transcendentals=0
+        ),
+    )(*table, *parts)
+
+
+def product_kernel(scale, own, near, mid, far, keep, send, here, over_y, over_x, over_xy, both):
+    rows, wide = own.shape
+    half = wide // 2
+    first = 0
+    for part in (own[...], near[...], mid[...] + far[...]):
+        for at in range(0, part.shape[1], wide):
+            real, imag = part[:, at : at + half], part[:, at + half : at + wide]
+            both[:rows, first : first + half] = real
+            both[:rows, first + half : first + wide] = -imag
+            both[rows:, first : first + half] = imag
+            both[rows:, first + half : first + wide] = real
+            first += wide
+    middle = rows // 2
+    for side, one, two in ((keep, here, over_x), (send, over_y, over_xy)):
+        total = nt(both[...], side[...]) * scale
+        for t in range(2):
+            one[:, t, :] = total[t * rows : t * rows + middle]
+            two[:, t, :] = total[t * rows + middle : (t + 1) * rows]
+
+
+def product(scale, own, near, mid, far, keep, send):
+    rows = own.shape[0]
+    shape = jax.ShapeDtypeStruct((rows // 2, 2, keep.shape[0]), jnp.float32)
+    return pl.pallas_call(
+        lambda *refs: product_kernel(scale, *refs),
+        out_shape=[shape] * 4,
+        in_specs=[pl.BlockSpec(memory_space=pltpu.VMEM)] * 6,
+        out_specs=[pl.BlockSpec(memory_space=pltpu.VMEM)] * 4,
+        scratch_shapes=[pltpu.VMEM((2 * rows, keep.shape[1]), jnp.bfloat16)],
+        compiler_params=pltpu.CompilerParams(vmem_limit_bytes=VMEM),
+        cost_estimate=pl.CostEstimate(
+            flops=8 * rows * keep.shape[0] * keep.shape[1], bytes_accessed=4 * keep.size, transcendentals=0
+        ),
+    )(own, near, mid, far, keep, send)
+
+
+def shards_plane(src_real, src_imag, rcv_real, rcv_imag, src_pos, rcv_pos, freqs):
+    n_z = lax.axis_size("tm")
+    bins, wide, a_block = src_real.shape
+    b_block = rcv_real.shape[2]
+    half = wide // 2
+    p_block = SRC_SL // lax.axis_size("src")
+    q_plane = RCV_SL // n_z
+    q_block = q_plane // 2
+    q_sub = q_block // lax.axis_size("src")
+    z, s, y = (lax.axis_index(name) for name in ("tm", "src", "rcv"))
+    x, c = s // 2, s % 2
+    mine = 2 * x + y
+    last = bins - 1
+    inner = (z == 1) | (z == 2)
+    core = lambda v: lax.ppermute(v, "src", [(i, i ^ 1) for i in range(4)])
+    over_x = lambda v: lax.ppermute(v, "src", [(i, i ^ 2) for i in range(4)])
+    over_y = lambda v: lax.ppermute(v, "rcv", [(0, 1), (1, 0)])
+    over_xy = lambda v: lax.ppermute(v, ("src", "rcv"), [(i, i ^ 5) for i in range(8)])
+    over_z = lambda v, d: lax.ppermute(v, "tm", [(i, i ^ d) for i in range(n_z)])
+
+    def chain(v):
+        near = over_z(v, 1)
+        mid = lax.ppermute(jnp.concatenate([v, near], 1), "tm", [(1, 2), (2, 1)])
+        far = lax.ppermute(mid, "tm", [(1, 0), (2, 3)])
+        return v, near, mid, far
+
+    def bin_of(real, imag, which):
+        return jnp.stack([lax.dynamic_index_in_dim(part, which, 0, False) for part in (real, imag)])
+
+    raw_last = lax.dynamic_slice_in_dim(jnp.stack([src_real[last], src_imag[last]]), y * half, half, 1)
+    raw_last = chain(raw_last.reshape(2 * half, a_block))
+
+    flat = lambda v: v.reshape(-1, v.shape[-1])
+    given = over_x(flat(bin_of(src_real, src_imag, 2 * (1 - x) + y)))
+    own = flat(bin_of(src_real, src_imag, mine))
+    x_mine = [own, given, core(own), core(given)]
+    theirs = jnp.stack([bin_of(rcv_real, rcv_imag, 2 * x + 1 - y), jnp.stack([rcv_real[last], rcv_imag[last]])])
+    given = over_y(lax.dynamic_slice_in_dim(theirs, c * half, half, 2))
+    other = core(given)
+    given, other = jnp.where(c == 0, given, other), jnp.where(c == 0, other, given)
+    given = jnp.concatenate([given, other], 2)
+    y_mine = [flat(bin_of(rcv_real, rcv_imag, mine)), flat(given[0])]
+    y_last = [flat(jnp.stack([rcv_real[last], rcv_imag[last]])), flat(given[1])]
+
+    take = lambda v, block, size: lax.dynamic_slice_in_dim(v, block * size, size)
+    at_src = jnp.concatenate([take(src_pos, block, a_block) for block in (s, s ^ 2, s ^ 1, s ^ 3)])
+    at_rcv = jnp.concatenate([take(rcv_pos, block, b_block) for block in (y, 1 - y)])
+    f_mine, f_last = lax.dynamic_index_in_dim(freqs, mine, 0, False), freqs[last]
+
+    chunk = p_block // CHUNKS
+    here, there = s * p_block, (s ^ 2) * p_block
+    starts = jnp.concatenate(
+        [runs(first + k * chunk, chunk) for k in range(CHUNKS) for first in (here, there)]
+    )
+    pieces = [chain(v) for v in steered(tables(f_mine, starts, SRC_SL, at_src), x_mine, CHUNKS)]
+
+    planes = [z ^ d for d in range(n_z)]
+    r_mine = tables(
+        f_mine, jnp.concatenate([runs(to * q_plane + c * q_block, q_block) for to in planes]), RCV_SL, at_rcv
+    )
+    r_last = tables(
+        f_last,
+        jnp.concatenate([runs(to * q_plane + y * q_block + s * q_sub, q_sub) for to in planes]),
+        RCV_SL,
+        at_rcv,
+    )
+    yr_mine = steered(r_mine, y_mine, n_z, sign=-1.0)
+    yr_last = steered(r_last, y_last, 1, sign=-1.0)[0].reshape(n_z, q_sub, -1)
+    got = [jnp.concatenate([yr_mine[d], yr_last[d]], 0) for d in range(n_z)]
+    got = [got[0]] + [over_z(got[d], d) for d in range(1, n_z)]
+    got = [got[0], got[1], jnp.where(inner, got[3], got[2]), jnp.where(inner, got[2], got[3])]
+    yr_mine = jnp.concatenate([v[:q_block] for v in got], 1)
+    yr_last = jnp.concatenate([v[q_block:] for v in got], 1)
+
+    yr_other = core(yr_mine)
+    keep_mine = jnp.where(c == y, yr_mine, yr_other)
+    send_mine = jnp.where(c == y, yr_other, yr_mine)
+    yr_last = lax.all_gather(yr_last, "src", axis=0, tiled=True).reshape(q_block, n_z, 2, wide)
+
+    focus_scale = 1.0 / float(wide * n_z * RCV_ST) ** 0.5
+    beam_scale = 1.0 / float(SRC_ST) ** 0.5
+    whole = jnp.zeros((p_block, bins, 2, q_block), jnp.float32)
+
+    own, near, mid, far = raw_last
+    slots = jnp.stack([own, near, (mid + far)[:, :a_block], (mid + far)[:, a_block:]])
+    slots = slots.reshape(n_z, 2, half, a_block)
+    other = over_y(slots)
+    slots = jnp.concatenate([jnp.where(y == 0, slots, other), jnp.where(y == 0, other, slots)], 2)
+    parts = jnp.einsum("qzuw,ztwa->utqa", yr_last, slots, preferred_element_type=jnp.float32) * focus_scale
+    focus = jnp.concatenate([parts[0, 0] - parts[1, 1], parts[0, 1] + parts[1, 0]], 0).astype(jnp.bfloat16)
+    table = tables(
+        f_last,
+        jnp.concatenate([runs(block * p_block, p_block) for block in (s, s ^ 2, s ^ 1, s ^ 3)]),
+        SRC_SL,
+        take(src_pos, s, a_block),
+    )
+    shares = steered(table, [focus], 4, scale=beam_scale, paired=True)
+    shares = [shares[0] + core(shares[2]), shares[1] + core(shares[3])]
+    shares = shares[0] + over_x(shares[1])
+    whole = lax.dynamic_update_slice(whole, shares[:, None], (0, last, 0, 0))
+
+    for k in range(CHUNKS):
+        found = product(focus_scale * beam_scale, *pieces[k], keep_mine, send_mine)
+        found = [found[0], over_y(found[1]), over_x(found[2]), over_xy(found[3])]
+        for d in range(4):
+            whole = lax.dynamic_update_slice(whole, found[d][:, None], (k * chunk, mine ^ d, 0, 0))
+    return whole.transpose(0, 2, 1, 3)
+
+
 def solution(mesh):
+    plane = (mesh.shape["tm"], mesh.shape["src"], mesh.shape["rcv"]) == (4, 4, 2)
+    shards = shards_plane if plane else shards_any
     in_specs = (
         P(None, "tm", "src"),
         P(None, "tm", "src"),

time: 1200 us -> 271 us (0.23)
  waiting for transfers between devices: 638 us -> 110 us
  matrix products: 355 us -> 2.79 us
  other arithmetic: 157 us -> 36.9 us
  starting transfers between devices: 0.46 us -> 53.7 us
  Pallas kernels: 0 us -> 29.3 us
    reduce_scatter x3 -> x0, waiting for transfers between devices: 501 us -> none  [the longest x1 178 us: shards(): lax.psum_scatter(part_real, 'tm', scatter_dimension=2, tiled=True)]
    dot_general x10 -> x1, matrix products: 355 us -> 2.79 us  [shards_plane(): jnp.einsum('qzuw,ztwa->utqa', yr_last, slots, preferred_element_type=jnp....]
    dot_general x4 -> x0, other arithmetic: 143 us -> none  [mixed(): return jnp.einsum(form, first, second, preferred_element_type=jnp.float32)]
    all_gather x2 -> x1, waiting for transfers between devices: 137 us -> 0.01 us  [shards_plane(): lax.all_gather(yr_last, 'src', axis=0, tiled=True)]
    ppermute x0 -> x40, waiting for transfers between devices: none -> 110 us  [the longest x5 47.4 us: chain(): far = lax.ppermute(mid, 'tm', [(1, 0), (2, 3)])]
    ppermute x0 -> x40, starting transfers between devices: none -> 53.7 us  [the longest x8 19 us: shards_plane(): lax.ppermute(v, 'tm', [(i, i ^ d) for i in range(n_z)])]
    pallas_call x0 -> x8, Pallas kernels: none -> 29.3 us  [the longest x4 18.8 us: steered(): pl.pallas_call(lambda *refs: steered_kernel(sign, scale, len(parts), *ref...]
  transfers between devices with their start and end apart: 5 -> 41, of which waited for: 4 -> 17; matrix products, arithmetic and copies ran while one was open for 15% -> 19% of each run, Pallas kernels for 0% -> 11%
where the time goes in v1:
time: 271 us; the launch traced here: 270 us
  waiting for transfers between devices  110 us (41%)
  starting transfers between devices  53.7 us (20%)
  other arithmetic  36.9 us (14%)
  Pallas kernels  29.3 us (11%)
  local copies, waits for them, and re-layouts  21.1 us (8%)
  between operations  16.6 us (6%)
  matrix products  2.79 us (1%)
    ppermute x5, waiting for transfers between devices, chain(): far = lax.ppermute(mid, 'tm', [(1, 0), (2, 3)])  47.4 us
    ppermute x6, waiting for transfers between devices, shards_plane(): over_y = lambda v: lax.ppermute(v, 'rcv', [(0, 1), (1, 0)])  31.3 us
    ppermute x8, waiting for transfers between devices, shards_plane(): lax.ppermute(v, 'tm', [(i, i ^ d) for i in range(n_z)])  26.3 us
    ppermute x8, starting transfers between devices, shards_plane(): lax.ppermute(v, 'tm', [(i, i ^ d) for i in range(n_z)])  19 us
    pallas_call x4, Pallas kernels, steered(): pl.pallas_call(lambda *refs: steered_kernel(sign, scale, len(parts), *ref...  18.8 us
    pallas_call x4, Pallas kernels, product(): pl.pallas_call(lambda *refs: product_kernel(scale, *refs), out_shape=[sha...  10.5 us
    ppermute x6, starting transfers between devices, shards_plane(): over_y = lambda v: lax.ppermute(v, 'rcv', [(0, 1), (1, 0)])  7.91 us
    ppermute x5, starting transfers between devices, chain(): mid = lax.ppermute(jnp.concatenate([v, near], 1), 'tm', [(1, 2), (2, 1)])  7.32 us
  transfers between devices with their start and end apart: 41, of which 17 were waited for; matrix products, arithmetic and copies ran while one was open for 19% of the time, Pallas kernels for 11%

profile of v1, /device:TPU:0, one launch (start us, length us, event | category | flops | bytes accessed | tf_op | source)
XLA Modules:
  0.0 270.0 jit_solution(2290703239365756)
XLA Ops:
  6.5 2.4 constant_dynamic-slice_fusion
  9.6 3.0 %collective-permute-start = (bf16[256,512]{1,0:T(8,128)(2,1)}, bf16[256,512]{1,0:T(8,128)(2,1)S(1)}, u32[]{:S(2)}, u32[]{:S(2)}) collective-permute-start(bf16[256,512]{1,0:T(8,128)(2,1)} %bitcast.3), channel_id=1, source_target_pairs={{0,8},{8,0},{16,24},{24,16},{1,9},{9,1},{17,25},{25,17},{2,10},{10... | collective-permute-start | bytes 786440 | tf_op jit(solution)/shard_map/ppermute | solution.py:250
  12.7 3.2 %constant_dynamic-slice_fusion.4 = (bf16[1,256,1024]{2,1,0:T(8,128)(2,1)}, bf16[1,256,1024]{2,1,0:T(8,128)(2,1)S(1)}, bf16[1,256,1024]{2,1,0:T(8,128)(2,1)S(1)},...) fusion(bf16[5,256,1024]{2,1,0:T(8,128)(2,1)} %param.10, ...), kind=kLoop, calls=%fused_computation.87 | loop fusion | bytes 6291464 | tf_op jit(solution)/shard_map/jit(dynamic_index_in_dim)/dynamic_slice | solution.py:259
  18.3 1.5 collective-permute-start.4
  20.6 1.5 collective-permute-start.12
  29.0 14.2 %collective-permute-done.4 = bf16[2,2,128,1024]{3,2,1,0:T(8,128)(2,1)} collective-permute-done((bf16[2,2,128,1024]{3,2,1,0:T(8,128)(2,1)}, bf16[2,2,128,1024]{3,2,1,0:T(8,128)(2,1)}, u32[]{:S(2)}, u32[]{:S(2)}) %collective-permute-start.4) | collective-permute-done | bytes 1048608 | tf_op jit(solution)/shard_map/ppermute | solution.py:248
  44.4 1.9 pad_maximum_fusion.5
  48.4 6.1 %multiply_sine_fusion = (f32[32,2048]{1,0:T(8,128)S(1)}, f32[32,2048]{1,0:T(8,128)S(1)}, f32[32,2048]{1,0:T(8,128)}, f32[32,2048]{1,0:T(8,128)}, f32[32,2048]{1,...) fusion(f32[2048]{0:T(1024)} %get-tuple-element.156, ...), kind=kLoop, calls=%fused_computation.40 | loop fusion | flops 327680 | bytes 2638336 | tf_op jit(solution)/shard_map/sin | solution.py:116
  55.8 1.7 broadcast_select_fusion.2
  59.0 5.5 %shard_map.74 = (bf16[256,512]{1,0:T(8,128)(2,1)S(1)}, bf16[256,512]{1,0:T(8,128)(2,1)S(1)}, bf16[256,512]{1,0:T(8,128)(2,1)S(1)}, bf16[256,512]{1,0:T(8,128)(2,1)S(1)}) custom-call(f32[32,2048]{1,0:T(8,128)S(1)} %get-tuple-element.124.refs_0_, f32[32,2048]{1,0:T(8,128)S(1)} %get-tuple-element.123.refs_1_, f32[32,2048]{1,0:T(8,128)S(1)} %get-tuple-element.125.refs_2_, ...), custom_call_target="tpu_custom_call" | custom-call | flops 4294967296 | bytes 2097152 | tf_op jit(solution)/shard_map/pallas_call | solution.py:180
  64.5 2.5 collective-permute-start.7
  67.1 8.9 %collective-permute-start.8 = (bf16[320,512]{1,0:T(8,128)(2,1)S(1)}, bf16[320,512]{1,0:T(8,128)(2,1)S(1)}, u32[]{:S(2)}, u32[]{:S(2)}) collective-permute-start(bf16[320,512]{1,0:T(8,128)(2,1)S(1)} %pad_maximum_fusion.15), channel_id=1, source_target_pairs={{0,16},{8,24},{16,0},{24,8},{1,17},{9,25},{17,1},{25,9},{2,18},{10... | collective-permute-start | bytes 983048 | tf_op jit(solution)/shard_map/ppermute | solution.py:250
  76.5 9.0 %collective-permute-done.2 = bf16[256,1024]{1,0:T(8,128)(2,1)S(1)} collective-permute-done((bf16[256,1024]{1,0:T(8,128)(2,1)}, bf16[256,1024]{1,0:T(8,128)(2,1)S(1)}, u32[]{:S(2)}, u32[]{:S(2)}) %collective-permute-start.2) | collective-permute-done | bytes 524320 | tf_op jit(solution)/shard_map/ppermute | solution.py:255
  85.5 2.0 add.373
  87.5 10.2 %collective-permute-done.8 = bf16[320,512]{1,0:T(8,128)(2,1)S(1)} collective-permute-done((bf16[320,512]{1,0:T(8,128)(2,1)S(1)}, bf16[320,512]{1,0:T(8,128)(2,1)S(1)}, u32[]{:S(2)}, u32[]{:S(2)}) %collective-permute-start.8) | collective-permute-done | bytes 327712 | tf_op jit(solution)/shard_map/ppermute | solution.py:250
  102.5 1.5 collective-permute-start.3
  105.9 6.5 %shard_map.76 = (bf16[256,512]{1,0:T(8,128)(2,1)S(1)}, bf16[256,512]{1,0:T(8,128)(2,1)S(1)}, bf16[256,512]{1,0:T(8,128)(2,1)S(1)}, bf16[256,512]{1,0:T(8,128)(2,1)S(1)}) custom-call(f32[32,2048]{1,0:T(8,128)S(1)} %copy-done, f32[32,2048]{1,0:T(8,128)S(1)} %copy-done.1, f32[32,2048]{1,0:T(8,128)S(1)} %get-tuple-element.94.refs_2_, ...), custom_call_target="tpu_custom_call" | custom-call | flops 4294967296 | bytes 2097152 | tf_op jit(solution)/shard_map/pallas_call | solution.py:180
  113.1 2.1 collective-permute-start.22
  115.6 6.2 %collective-permute-done.15.refs_1_ = bf16[256,512]{1,0:T(8,128)(2,1)S(1)} collective-permute-done((bf16[256,512]{1,0:T(8,128)(2,1)S(1)}, bf16[256,512]{1,0:T(8,128)(2,1)S(1)}, u32[]{:S(2)}, u32[]{:S(2)}) %collective-permute-start.15) | collective-permute-done | bytes 262176 | tf_op jit(solution)/shard_map/ppermute | solution.py:250
  124.2 3.3 %collective-permute-done.22.refs_1_ = bf16[256,512]{1,0:T(8,128)(2,1)S(1)} collective-permute-done((bf16[256,512]{1,0:T(8,128)(2,1)S(1)}, bf16[256,512]{1,0:T(8,128)(2,1)S(1)}, u32[]{:S(2)}, u32[]{:S(2)}) %collective-permute-start.22) | collective-permute-done | bytes 262176 | tf_op jit(solution)/shard_map/ppermute | solution.py:250
  129.8 3.0 %broadcast_select_fusion.5 = (bf16[4,2,128,512]{3,2,0,1:T(8,128)(2,1)}, bf16[4,2,128,512]{3,2,0,1:T(8,128)(2,1)}) fusion(bf16[4,2,128,512]{3,2,0,1:T(8,128)(2,1)} %collective-permute-done.3, pred[]{:T(512)S(6)} %eq.20, bf16[1,2,128,512]{3,2,0,1:T(8,128)(2,1)} %bitcast.83, bf16[1,2,128,512]{3,2,0,1:T(8,128)(2,1)} %bitcast.81, ...), kind=kLoop, calls=%fused_computation.25 | loop fusion | flops 2621440 | bytes 4194305 | tf_op jit(solution)/shard_map/jit(_where)/select_n | solution.py:319
  135.0 1.8 reshape.206
  136.8 2.8 %fusion.3 = f32[2,2,256,512]{3,2,1,0:T(8,128)S(1)} fusion(bf16[4,2,128,512]{3,2,0,1:T(8,128)(2,1)} %get-tuple-element.76, bf16[4,2,128,512]{3,2,0,1:T(8,128)(2,1)} %get-tuple-element.75, bf16[256,4,2,256,1]{3,2,1,0,4:T(2,128)(2,1)S(1)} %bitcast.84), kind=kOutput, calls=%fused_computation.9 | convolution fusion | flops 1078460416 | bytes 5242880 | tf_op jit(solution)/shard_map/qzuw,ztwa->utqa/dot_general | solution.py:320
  139.9 5.5 %shard_map.75 = (f32[512,2,256]{2,1,0:T(2,128)S(1)}, f32[512,2,256]{2,1,0:T(2,128)S(1)}, f32[512,2,256]{2,1,0:T(2,128)}, f32[512,2,256]{2,1,0:T(2,128)S(1)}) custom-call(f32[64,512]{1,0:T(8,128)S(1)} %get-tuple-element.120.refs_0_, f32[64,512]{1,0:T(8,128)S(1)} %get-tuple-element.119.refs_1_, f32[32,512]{1,0:T(8,128)S(1)} %get-tuple-element.118.refs_2_, ...), custom_call_target="tpu_custom_call" | custom-call | flops 2147483648 | bytes 524288 | tf_op jit(solution)/shard_map/pallas_call | solution.py:180
  147.0 2.0 collective-permute-start.34
  149.1 6.5 %collective-permute-done.34.refs_1_ = bf16[256,512]{1,0:T(8,128)(2,1)S(1)} collective-permute-done((bf16[256,512]{1,0:T(8,128)(2,1)S(1)}, bf16[256,512]{1,0:T(8,128)(2,1)S(1)}, u32[]{:S(2)}, u32[]{:S(2)}) %collective-permute-start.34) | collective-permute-done | bytes 262176 | tf_op jit(solution)/shard_map/ppermute | solution.py:250
  155.5 1.5 collective-permute-start.29
  157.9 1.5 collective-permute-start.35
  160.8 1.5 add.415
  165.1 11.3 %collective-permute-done.17.refs_3_ = bf16[256,1024]{1,0:T(8,128)(2,1)} collective-permute-done((bf16[256,1024]{1,0:T(8,128)(2,1)}, bf16[256,1024]{1,0:T(8,128)(2,1)}, u32[]{:S(2)}, u32[]{:S(2)}) %collective-permute-start.17) | collective-permute-done | bytes 524320 | tf_op jit(solution)/shard_map/ppermute | solution.py:255
  179.0 1.9 broadcast_select_fusion
  180.9 2.7 %shard_map.77 = (f32[128,2,256]{2,1,0:T(2,128)S(1)}, f32[128,2,256]{2,1,0:T(2,128)S(1)}, f32[128,2,256]{2,1,0:T(2,128)S(1)}, f32[128,2,256]{2,1,0:T(2,128)S(1)}) custom-call(bf16[256,512]{1,0:T(8,128)(2,1)S(1)} %copy-done.5, bf16[256,512]{1,0:T(8,128)(2,1)S(1)} %collective-permute-done.15.refs_1_, bf16[256,1024]{1,0:T(8,128)(2,1)} %collective-permute-done.16.refs_2_, ...), custom_call_target="tpu_custom_call" | custom-call | flops 1073741824 | bytes 2097152 | tf_op jit(solution)/shard_map/pallas_call | solution.py:219
  183.6 14.3 %collective-permute-done.24.refs_3_ = bf16[256,1024]{1,0:T(8,128)(2,1)S(1)} collective-permute-done((bf16[256,1024]{1,0:T(8,128)(2,1)}, bf16[256,1024]{1,0:T(8,128)(2,1)S(1)}, u32[]{:S(2)}, u32[]{:S(2)}) %collective-permute-start.24) | collective-permute-done | bytes 524320 | tf_op jit(solution)/shard_map/ppermute | solution.py:255
  198.4 2.6 shard_map.78
  201.0 8.2 %collective-permute-done.30.refs_3_ = bf16[256,1024]{1,0:T(8,128)(2,1)S(1)} collective-permute-done((bf16[256,1024]{1,0:T(8,128)(2,1)}, bf16[256,1024]{1,0:T(8,128)(2,1)S(1)}, u32[]{:S(2)}, u32[]{:S(2)}) %collective-permute-start.30) | collective-permute-done | bytes 524320 | tf_op jit(solution)/shard_map/ppermute | solution.py:255
  210.6 2.6 shard_map.79
  213.2 4.7 %collective-permute-done.36.refs_3_ = bf16[256,1024]{1,0:T(8,128)(2,1)S(1)} collective-permute-done((bf16[256,1024]{1,0:T(8,128)(2,1)}, bf16[256,1024]{1,0:T(8,128)(2,1)S(1)}, u32[]{:S(2)}, u32[]{:S(2)}) %collective-permute-start.36) | collective-permute-done | bytes 524320 | tf_op jit(solution)/shard_map/ppermute | solution.py:255
  219.3 2.6 shard_map.80
  221.9 1.6 collective-permute-start.25
  224.1 2.3 add_bitcast_fusion
  229.4 1.6 collective-permute-start.31
  231.7 5.2 %collective-permute-done.25 = f32[128,2,256]{2,1,0:T(2,128)S(1)} collective-permute-done((f32[128,2,256]{2,1,0:T(2,128)S(1)}, f32[128,2,256]{2,1,0:T(2,128)S(1)}, u32[]{:S(2)}, u32[]{:S(2)}) %collective-permute-start.25) | collective-permute-done | bytes 262176 | tf_op jit(solution)/shard_map/ppermute | solution.py:248
  236.9 1.5 collective-permute-start.33
  240.7 7.4 %collective-permute-done.31 = f32[128,2,256]{2,1,0:T(2,128)S(1)} collective-permute-done((f32[128,2,256]{2,1,0:T(2,128)S(1)}, f32[128,2,256]{2,1,0:T(2,128)S(1)}, u32[]{:S(2)}, u32[]{:S(2)}) %collective-permute-start.31) | collective-permute-done | bytes 262176 | tf_op jit(solution)/shard_map/ppermute | solution.py:248
  248.0 1.5 collective-permute-start.39
  249.9 4.5 %collective-permute-done.37 = f32[128,2,256]{2,1,0:T(2,128)S(1)} collective-permute-done((f32[128,2,256]{2,1,0:T(2,128)S(1)}, f32[128,2,256]{2,1,0:T(2,128)S(1)}, u32[]{:S(2)}, u32[]{:S(2)}) %collective-permute-start.37) | collective-permute-done | bytes 262176 | tf_op jit(solution)/shard_map/ppermute | solution.py:248
  255.1 3.9 %collective-permute-done.39 = f32[128,2,256]{2,1,0:T(2,128)S(1)} collective-permute-done((f32[128,2,256]{2,1,0:T(2,128)S(1)}, f32[128,2,256]{2,1,0:T(2,128)S(1)}, u32[]{:S(2)}, u32[]{:S(2)}) %collective-permute-start.39) | collective-permute-done | bytes 262176 | tf_op jit(solution)/shard_map/ppermute | solution.py:249
  259.0 4.2 %copy.10 = f32[512,2,5,256]{3,1,2,0:T(2,128)} copy(f32[512,2,5,256]{3,1,0,2:T(2,128)S(1)} %bitcast.77) | data formatting | bytes 10485760 | tf_op jit(solution)/shard_map/transpose | solution.py:338
  (186 shorter events, 49.8 us)
Async XLA Ops:
  6.5 128.5 %all-gather.2.cloned.1.call-start = ((), (), s32[]{:S(2)}) async-start(), calls=%async_computation | async-start | bytes 1310720 | tf_op jit(solution)/shard_map/all_gather | solution.py:309
  9.6 34.7 %collective-permute-start = (bf16[256,512]{1,0:T(8,128)(2,1)}, bf16[256,512]{1,0:T(8,128)(2,1)S(1)}, u32[]{:S(2)}, u32[]{:S(2)}) collective-permute-start(bf16[256,512]{1,0:T(8,128)(2,1)} %bitcast.3), channel_id=1, source_target_pairs={{0,8},{8,0},{16,24},{24,16},{1,9},{9,1},{17,25},{25,17},{2,10},{10... | collective-permute-start | bytes 786440 | tf_op jit(solution)/shard_map/ppermute | solution.py:250
  18.3 24.9 %collective-permute-start.4 = (bf16[2,2,128,1024]{3,2,1,0:T(8,128)(2,1)}, bf16[2,2,128,1024]{3,2,1,0:T(8,128)(2,1)}, u32[]{:S(2)}, u32[]{:S(2)}) collective-permute-start(bf16[2,2,128,1024]{3,2,1,0:T(8,128)(2,1)} %fusion.5), channel_id=1, source_target_pairs={{0,1},{1,0},{2,3},{3,2},{4,5},{5,4},{6,7},{7,6},{8,9},{9,8},{10,11... | collective-permute-start | bytes 3145736 | tf_op jit(solution)/shard_map/ppermute | solution.py:248
  20.6 55.8 %collective-permute-start.12 = (bf16[512,512]{1,0:T(8,128)(2,1)}, bf16[512,512]{1,0:T(8,128)(2,1)}, u32[]{:S(2)}, u32[]{:S(2)}) collective-permute-start(bf16[512,512]{1,0:T(8,128)(2,1)} %bitcast.23), channel_id=1, source_target_pairs={{0,4},{2,6},{4,0},{6,2},{1,5},{3,7},{5,1},{7,3},{8,12},{10,14},{12... | collective-permute-start | bytes 1572872 | tf_op jit(solution)/shard_map/ppermute | solution.py:247
  43.2 12.6 %collective-permute-start.5 = (bf16[2,2,128,1024]{3,2,1,0:T(8,128)(2,1)}, bf16[2,2,128,1024]{3,2,1,0:T(8,128)(2,1)}, u32[]{:S(2)}, u32[]{:S(2)}) collective-permute-start(bf16[2,2,128,1024]{3,2,1,0:T(8,128)(2,1)} %collective-permute-done.4), channel_id=1, source_target_pairs={{0,2},{2,0},{4,6},{6,4},{1,3},{3,1},{5,7},{7,5},{8,10},{10,8},{12,... | collective-permute-start | bytes 3145736 | tf_op jit(solution)/shard_map/ppermute | solution.py:246
  44.4 57.0 %copy-start.11 = (bf16[256,512]{1,0:T(8,128)(2,1)}, bf16[256,512]{1,0:T(8,128)(2,1)S(1)}, u32[]{:S(2)}) copy-start(bf16[256,512]{1,0:T(8,128)(2,1)S(1)} %collective-permute-done) | copy-start | bytes 786436
  46.3 8.2 %collective-permute-start.1 = (bf16[256,1024]{1,0:T(8,128)(2,1)}, bf16[256,1024]{1,0:T(8,128)(2,1)}, u32[]{:S(2)}, u32[]{:S(2)}) collective-permute-start(bf16[256,1024]{1,0:T(8,128)(2,1)} %pad_maximum_fusion.5), channel_id=1, source_target_pairs={{8,16},{16,8},{9,17},{17,9},{10,18},{18,10},{11,19},{19,11},{12,20... | collective-permute-start | bytes 1572872 | tf_op jit(solution)/shard_map/ppermute | solution.py:254
  54.5 31.0 %collective-permute-start.2 = (bf16[256,1024]{1,0:T(8,128)(2,1)}, bf16[256,1024]{1,0:T(8,128)(2,1)S(1)}, u32[]{:S(2)}, u32[]{:S(2)}) collective-permute-start(bf16[256,1024]{1,0:T(8,128)(2,1)} %collective-permute-done.1), channel_id=1, source_target_pairs={{8,0},{16,24},{9,1},{17,25},{10,2},{18,26},{11,3},{19,27},{12,4},{... | collective-permute-start | bytes 1572872 | tf_op jit(solution)/shard_map/ppermute | solution.py:255
  64.5 36.9 %copy-start.12 = (bf16[1,2,128,512]{3,2,0,1:T(8,128)(2,1)S(1)}, bf16[1,2,128,512]{3,2,0,1:T(8,128)(2,1)}, u32[]{:S(2)}) copy-start(bf16[1,2,128,512]{3,2,0,1:T(8,128)(2,1)} %fusion.45) | copy-start | bytes 786436
  64.5 40.4 %copy-start = (f32[32,2048]{1,0:T(8,128)S(1)}, f32[32,2048]{1,0:T(8,128)}, u32[]{:S(2)}) copy-start(f32[32,2048]{1,0:T(8,128)} %get-tuple-element.105.refs_0_) | copy-start | bytes 786436
  64.5 40.4 %copy-start.1 = (f32[32,2048]{1,0:T(8,128)S(1)}, f32[32,2048]{1,0:T(8,128)}, u32[]{:S(2)}) copy-start(f32[32,2048]{1,0:T(8,128)} %get-tuple-element.106.refs_1_) | copy-start | bytes 786436
  64.5 23.0 %collective-permute-start.7 = (bf16[320,512]{1,0:T(8,128)(2,1)S(1)}, bf16[320,512]{1,0:T(8,128)(2,1)S(1)}, u32[]{:S(2)}, u32[]{:S(2)}) collective-permute-start(bf16[320,512]{1,0:T(8,128)(2,1)S(1)} %pad_maximum_fusion.14), channel_id=1, source_target_pairs={{0,24},{8,16},{16,8},{24,0},{1,25},{9,17},{17,9},{25,1},{2,26},{10... | collective-permute-start | bytes 983048 | tf_op jit(solution)/shard_map/ppermute | solution.py:250
  67.1 30.6 %collective-permute-start.8 = (bf16[320,512]{1,0:T(8,128)(2,1)S(1)}, bf16[320,512]{1,0:T(8,128)(2,1)S(1)}, u32[]{:S(2)}, u32[]{:S(2)}) collective-permute-start(bf16[320,512]{1,0:T(8,128)(2,1)S(1)} %pad_maximum_fusion.15), channel_id=1, source_target_pairs={{0,16},{8,24},{16,0},{24,8},{1,17},{9,25},{17,1},{25,9},{2,18},{10... | collective-permute-start | bytes 983048 | tf_op jit(solution)/shard_map/ppermute | solution.py:250
  76.0 22.8 %collective-permute-start.6 = (bf16[320,512]{1,0:T(8,128)(2,1)S(1)}, bf16[320,512]{1,0:T(8,128)(2,1)S(1)}, u32[]{:S(2)}, u32[]{:S(2)}) collective-permute-start(bf16[320,512]{1,0:T(8,128)(2,1)S(1)} %pad_maximum_fusion.13), channel_id=1, source_target_pairs={{0,8},{8,0},{16,24},{24,16},{1,9},{9,1},{17,25},{25,17},{2,10},{10... | collective-permute-start | bytes 983048 | tf_op jit(solution)/shard_map/ppermute | solution.py:250
  76.4 27.6 %collective-permute-start.13 = (bf16[512,512]{1,0:T(8,128)(2,1)S(1)}, bf16[512,512]{1,0:T(8,128)(2,1)S(1)}, u32[]{:S(2)}, u32[]{:S(2)}) collective-permute-start(bf16[512,512]{1,0:T(8,128)(2,1)S(1)} %bitcast.75), channel_id=1, source_target_pairs={{0,2},{2,0},{4,6},{6,4},{1,3},{3,1},{5,7},{7,5},{8,10},{10,8},{12,... | collective-permute-start | bytes 1572872 | tf_op jit(solution)/shard_map/ppermute | solution.py:246
  85.5 18.6 %collective-permute-start.14 = (bf16[512,512]{1,0:T(8,128)(2,1)}, bf16[512,512]{1,0:T(8,128)(2,1)S(1)}, u32[]{:S(2)}, u32[]{:S(2)}) collective-permute-start(bf16[512,512]{1,0:T(8,128)(2,1)} %collective-permute-done.12.refs_5_), channel_id=1, source_target_pairs={{0,2},{2,0},{4,6},{6,4},{1,3},{3,1},{5,7},{7,5},{8,10},{10,8},{12,... | collective-permute-start | bytes 1572872 | tf_op jit(solution)/shard_map/ppermute | solution.py:246
  102.5 27.2 %collective-permute-start.3 = (bf16[4,2,128,512]{3,2,0,1:T(8,128)(2,1)}, bf16[4,2,128,512]{3,2,0,1:T(8,128)(2,1)}, u32[]{:S(2)}, u32[]{:S(2)}) collective-permute-start(bf16[4,2,128,512]{3,2,0,1:T(8,128)(2,1)} %pad_maximum_fusion.1), channel_id=1, source_target_pairs={{0,1},{1,0},{2,3},{3,2},{4,5},{5,4},{6,7},{7,6},{8,9},{9,8},{10,11... | collective-permute-start | bytes 3145736 | tf_op jit(solution)/shard_map/ppermute | solution.py:248
  112.5 27.2 %copy-start.2 = (bf16[256,512]{1,0:T(8,128)(2,1)}, bf16[256,512]{1,0:T(8,128)(2,1)S(1)}, u32[]{:S(2)}) copy-start(bf16[256,512]{1,0:T(8,128)(2,1)S(1)} %get-tuple-element.46.refs_0_) | copy-start | bytes 786436
  112.5 9.3 %collective-permute-start.15 = (bf16[256,512]{1,0:T(8,128)(2,1)S(1)}, bf16[256,512]{1,0:T(8,128)(2,1)S(1)}, u32[]{:S(2)}, u32[]{:S(2)}) collective-permute-start(bf16[256,512]{1,0:T(8,128)(2,1)S(1)} %get-tuple-element.40.refs_0_), channel_id=1, source_target_pairs={{0,8},{8,0},{16,24},{24,16},{1,9},{9,1},{17,25},{25,17},{2,10},{10... | collective-permute-start | bytes 786440 | tf_op jit(solution)/shard_map/ppermute | solution.py:250
  113.1 14.3 %collective-permute-start.22 = (bf16[256,512]{1,0:T(8,128)(2,1)S(1)}, bf16[256,512]{1,0:T(8,128)(2,1)S(1)}, u32[]{:S(2)}, u32[]{:S(2)}) collective-permute-start(bf16[256,512]{1,0:T(8,128)(2,1)S(1)} %get-tuple-element.46.refs_0_), channel_id=1, source_target_pairs={{0,8},{8,0},{16,24},{24,16},{1,9},{9,1},{17,25},{25,17},{2,10},{10... | collective-permute-start | bytes 786440 | tf_op jit(solution)/shard_map/ppermute | solution.py:250
  115.5 31.5 %collective-permute-start.28 = (bf16[256,512]{1,0:T(8,128)(2,1)S(1)}, bf16[256,512]{1,0:T(8,128)(2,1)S(1)}, u32[]{:S(2)}, u32[]{:S(2)}) collective-permute-start(bf16[256,512]{1,0:T(8,128)(2,1)S(1)} %get-tuple-element.51.refs_0_), channel_id=1, source_target_pairs={{0,8},{8,0},{16,24},{24,16},{1,9},{9,1},{17,25},{25,17},{2,10},{10... | collective-permute-start | bytes 786440 | tf_op jit(solution)/shard_map/ppermute | solution.py:250
  122.7 35.2 %collective-permute-start.16 = (bf16[256,1024]{1,0:T(8,128)(2,1)}, bf16[256,1024]{1,0:T(8,128)(2,1)}, u32[]{:S(2)}, u32[]{:S(2)}) collective-permute-start(bf16[256,1024]{1,0:T(8,128)(2,1)} %pad_maximum_fusion.9), channel_id=1, source_target_pairs={{8,16},{16,8},{9,17},{17,9},{10,18},{18,10},{11,19},{19,11},{12,20... | collective-permute-start | bytes 1572872 | tf_op jit(solution)/shard_map/ppermute | solution.py:254
  128.3 31.1 %collective-permute-start.23 = (bf16[256,1024]{1,0:T(8,128)(2,1)}, bf16[256,1024]{1,0:T(8,128)(2,1)}, u32[]{:S(2)}, u32[]{:S(2)}) collective-permute-start(bf16[256,1024]{1,0:T(8,128)(2,1)} %pad_maximum_fusion.10), channel_id=1, source_target_pairs={{8,16},{16,8},{9,17},{17,9},{10,18},{18,10},{11,19},{19,11},{12,20... | collective-permute-start | bytes 1572872 | tf_op jit(solution)/shard_map/ppermute | solution.py:254
  145.3 15.4 %collective-permute-start.10 = (f32[512,2,256]{2,1,0:T(2,128)S(1)}, f32[512,2,256]{2,1,0:T(2,128)S(1)}, u32[]{:S(2)}, u32[]{:S(2)}) collective-permute-start(f32[512,2,256]{2,1,0:T(2,128)S(1)} %get-tuple-element.39), channel_id=1, source_target_pairs={{0,2},{2,0},{4,6},{6,4},{1,3},{3,1},{5,7},{7,5},{8,10},{10,8},{12,... | collective-permute-start | bytes 3145736 | tf_op jit(solution)/shard_map/ppermute | solution.py:246
  146.5 34.4 %copy-start.5 = (bf16[256,512]{1,0:T(8,128)(2,1)S(1)}, bf16[256,512]{1,0:T(8,128)(2,1)}, u32[]{:S(2)}) copy-start(bf16[256,512]{1,0:T(8,128)(2,1)} %copy-done.4) | copy-start | bytes 786436
  146.5 31.2 %collective-permute-start.18 = (bf16[256,2048]{1,0:T(8,128)(2,1)}, bf16[256,2048]{1,0:T(8,128)(2,1)}, u32[]{:S(2)}, u32[]{:S(2)}) collective-permute-start(bf16[256,2048]{1,0:T(8,128)(2,1)} %pad_maximum_fusion.4), channel_id=1, source_target_pairs={{0,2},{2,0},{4,6},{6,4},{1,3},{3,1},{5,7},{7,5},{8,10},{10,8},{12,... | collective-permute-start | bytes 3145736 | tf_op jit(solution)/shard_map/ppermute | solution.py:246
  147.0 8.5 %collective-permute-start.34 = (bf16[256,512]{1,0:T(8,128)(2,1)S(1)}, bf16[256,512]{1,0:T(8,128)(2,1)S(1)}, u32[]{:S(2)}, u32[]{:S(2)}) collective-permute-start(bf16[256,512]{1,0:T(8,128)(2,1)S(1)} %get-tuple-element.56.refs_0_), channel_id=1, source_target_pairs={{0,8},{8,0},{16,24},{24,16},{1,9},{9,1},{17,25},{25,17},{2,10},{10... | collective-permute-start | bytes 786440 | tf_op jit(solution)/shard_map/ppermute | solution.py:250
  155.5 6.8 %collective-permute-start.29 = (bf16[256,1024]{1,0:T(8,128)(2,1)S(1)}, bf16[256,1024]{1,0:T(8,128)(2,1)}, u32[]{:S(2)}, u32[]{:S(2)}) collective-permute-start(bf16[256,1024]{1,0:T(8,128)(2,1)S(1)} %pad_maximum_fusion.11), channel_id=1, source_target_pairs={{8,16},{16,8},{9,17},{17,9},{10,18},{18,10},{11,19},{19,11},{12,20... | collective-permute-start | bytes 1572872 | tf_op jit(solution)/shard_map/ppermute | solution.py:254
  157.9 5.9 %collective-permute-start.35 = (bf16[256,1024]{1,0:T(8,128)(2,1)}, bf16[256,1024]{1,0:T(8,128)(2,1)}, u32[]{:S(2)}, u32[]{:S(2)}) collective-permute-start(bf16[256,1024]{1,0:T(8,128)(2,1)} %pad_maximum_fusion.12), channel_id=1, source_target_pairs={{8,16},{16,8},{9,17},{17,9},{10,18},{18,10},{11,19},{19,11},{12,20... | collective-permute-start | bytes 1572872 | tf_op jit(solution)/shard_map/ppermute | solution.py:254
  159.4 17.0 %collective-permute-start.17 = (bf16[256,1024]{1,0:T(8,128)(2,1)}, bf16[256,1024]{1,0:T(8,128)(2,1)}, u32[]{:S(2)}, u32[]{:S(2)}) collective-permute-start(bf16[256,1024]{1,0:T(8,128)(2,1)} %collective-permute-done.16.refs_2_), channel_id=1, source_target_pairs={{8,0},{16,24},{9,1},{17,25},{10,2},{18,26},{11,3},{19,27},{12,4},{... | collective-permute-start | bytes 1572872 | tf_op jit(solution)/shard_map/ppermute | solution.py:255
  160.7 61.2 %collective-permute-start.9 = (f32[512,2,256]{2,1,0:T(2,128)}, f32[512,2,256]{2,1,0:T(2,128)}, u32[]{:S(2)}, u32[]{:S(2)}) collective-permute-start(f32[512,2,256]{2,1,0:T(2,128)} %get-tuple-element.37), channel_id=1, source_target_pairs={{0,2},{2,0},{4,6},{6,4},{1,3},{3,1},{5,7},{7,5},{8,10},{10,8},{12,... | collective-permute-start | bytes 3145736 | tf_op jit(solution)/shard_map/ppermute | solution.py:246
  160.8 37.6 %copy-start.3 = (bf16[256,512]{1,0:T(8,128)(2,1)S(1)}, bf16[256,512]{1,0:T(8,128)(2,1)}, u32[]{:S(2)}) copy-start(bf16[256,512]{1,0:T(8,128)(2,1)} %copy-done.2) | copy-start | bytes 786436
  162.3 61.2 %collective-permute-start.11 = (f32[512,2,256]{2,1,0:T(2,128)}, f32[512,2,256]{2,1,0:T(2,128)}, u32[]{:S(2)}, u32[]{:S(2)}) collective-permute-start(f32[512,2,256]{2,1,0:T(2,128)} %add.415), channel_id=1, source_target_pairs={{0,4},{2,6},{4,0},{6,2},{1,5},{3,7},{5,1},{7,3},{8,12},{10,14},{12... | collective-permute-start | bytes 3145736 | tf_op jit(solution)/shard_map/ppermute | solution.py:247
  163.8 34.1 %collective-permute-start.24 = (bf16[256,1024]{1,0:T(8,128)(2,1)}, bf16[256,1024]{1,0:T(8,128)(2,1)S(1)}, u32[]{:S(2)}, u32[]{:S(2)}) collective-permute-start(bf16[256,1024]{1,0:T(8,128)(2,1)} %collective-permute-done.23.refs_2_), channel_id=1, source_target_pairs={{8,0},{16,24},{9,1},{17,25},{10,2},{18,26},{11,3},{19,27},{12,4},{... | collective-permute-start | bytes 1572872 | tf_op jit(solution)/shard_map/ppermute | solution.py:255
  176.4 32.8 %collective-permute-start.30 = (bf16[256,1024]{1,0:T(8,128)(2,1)}, bf16[256,1024]{1,0:T(8,128)(2,1)S(1)}, u32[]{:S(2)}, u32[]{:S(2)}) collective-permute-start(bf16[256,1024]{1,0:T(8,128)(2,1)} %collective-permute-done.29.refs_2_), channel_id=1, source_target_pairs={{8,0},{16,24},{9,1},{17,25},{10,2},{18,26},{11,3},{19,27},{12,4},{... | collective-permute-start | bytes 1572872 | tf_op jit(solution)/shard_map/ppermute | solution.py:255
  177.7 40.2 %collective-permute-start.36 = (bf16[256,1024]{1,0:T(8,128)(2,1)}, bf16[256,1024]{1,0:T(8,128)(2,1)S(1)}, u32[]{:S(2)}, u32[]{:S(2)}) collective-permute-start(bf16[256,1024]{1,0:T(8,128)(2,1)} %collective-permute-done.35.refs_2_), channel_id=1, source_target_pairs={{8,0},{16,24},{9,1},{17,25},{10,2},{18,26},{11,3},{19,27},{12,4},{... | collective-permute-start | bytes 1572872 | tf_op jit(solution)/shard_map/ppermute | solution.py:255
  197.9 29.9 %collective-permute-start.19 = (f32[128,2,256]{2,1,0:T(2,128)S(1)}, f32[128,2,256]{2,1,0:T(2,128)S(1)}, u32[]{:S(2)}, u32[]{:S(2)}) collective-permute-start(f32[128,2,256]{2,1,0:T(2,128)S(1)} %get-tuple-element.43), channel_id=1, source_target_pairs={{0,1},{1,0},{2,3},{3,2},{4,5},{5,4},{6,7},{7,6},{8,9},{9,8},{10,11... | collective-permute-start | bytes 786440 | tf_op jit(solution)/shard_map/ppermute | solution.py:248
  209.1 20.2 %collective-permute-start.20 = (f32[128,2,256]{2,1,0:T(2,128)S(1)}, f32[128,2,256]{2,1,0:T(2,128)S(1)}, u32[]{:S(2)}, u32[]{:S(2)}) collective-permute-start(f32[128,2,256]{2,1,0:T(2,128)S(1)} %get-tuple-element.44), channel_id=1, source_target_pairs={{0,4},{2,6},{4,0},{6,2},{1,5},{3,7},{5,1},{7,3},{8,12},{10,14},{12... | collective-permute-start | bytes 786440 | tf_op jit(solution)/shard_map/ppermute | solution.py:247
  217.9 13.1 %collective-permute-start.21 = (f32[128,2,256]{2,1,0:T(2,128)S(1)}, f32[128,2,256]{2,1,0:T(2,128)S(1)}, u32[]{:S(2)}, u32[]{:S(2)}) collective-permute-start(f32[128,2,256]{2,1,0:T(2,128)S(1)} %get-tuple-element.45), channel_id=1, source_target_pairs={{0,5},{1,4},{2,7},{3,6},{4,1},{5,0},{6,3},{7,2},{8,13},{9,12},{10,... | collective-permute-start | bytes 786440 | tf_op jit(solution)/shard_map/ppermute | solution.py:249
  221.9 14.9 %collective-permute-start.25 = (f32[128,2,256]{2,1,0:T(2,128)S(1)}, f32[128,2,256]{2,1,0:T(2,128)S(1)}, u32[]{:S(2)}, u32[]{:S(2)}) collective-permute-start(f32[128,2,256]{2,1,0:T(2,128)S(1)} %get-tuple-element.48), channel_id=1, source_target_pairs={{0,1},{1,0},{2,3},{3,2},{4,5},{5,4},{6,7},{7,6},{8,9},{9,8},{10,11... | collective-permute-start | bytes 786440 | tf_op jit(solution)/shard_map/ppermute | solution.py:248
  223.5 14.9 %collective-permute-start.26 = (f32[128,2,256]{2,1,0:T(2,128)S(1)}, f32[128,2,256]{2,1,0:T(2,128)S(1)}, u32[]{:S(2)}, u32[]{:S(2)}) collective-permute-start(f32[128,2,256]{2,1,0:T(2,128)S(1)} %get-tuple-element.49), channel_id=1, source_target_pairs={{0,4},{2,6},{4,0},{6,2},{1,5},{3,7},{5,1},{7,3},{8,12},{10,14},{12... | collective-permute-start | bytes 786440 | tf_op jit(solution)/shard_map/ppermute | solution.py:247
  227.8 11.8 %collective-permute-start.27 = (f32[128,2,256]{2,1,0:T(2,128)S(1)}, f32[128,2,256]{2,1,0:T(2,128)S(1)}, u32[]{:S(2)}, u32[]{:S(2)}) collective-permute-start(f32[128,2,256]{2,1,0:T(2,128)S(1)} %get-tuple-element.50), channel_id=1, source_target_pairs={{0,5},{1,4},{2,7},{3,6},{4,1},{5,0},{6,3},{7,2},{8,13},{9,12},{10,... | collective-permute-start | bytes 786440 | tf_op jit(solution)/shard_map/ppermute | solution.py:249
  229.4 18.7 %collective-permute-start.31 = (f32[128,2,256]{2,1,0:T(2,128)S(1)}, f32[128,2,256]{2,1,0:T(2,128)S(1)}, u32[]{:S(2)}, u32[]{:S(2)}) collective-permute-start(f32[128,2,256]{2,1,0:T(2,128)S(1)} %get-tuple-element.53), channel_id=1, source_target_pairs={{0,1},{1,0},{2,3},{3,2},{4,5},{5,4},{6,7},{7,6},{8,9},{9,8},{10,11... | collective-permute-start | bytes 786440 | tf_op jit(solution)/shard_map/ppermute | solution.py:248
  231.0 18.6 %collective-permute-start.32 = (f32[128,2,256]{2,1,0:T(2,128)S(1)}, f32[128,2,256]{2,1,0:T(2,128)S(1)}, u32[]{:S(2)}, u32[]{:S(2)}) collective-permute-start(f32[128,2,256]{2,1,0:T(2,128)S(1)} %get-tuple-element.54), channel_id=1, source_target_pairs={{0,4},{2,6},{4,0},{6,2},{1,5},{3,7},{5,1},{7,3},{8,12},{10,14},{12... | collective-permute-start | bytes 786440 | tf_op jit(solution)/shard_map/ppermute | solution.py:247
  236.9 12.9 %collective-permute-start.33 = (f32[128,2,256]{2,1,0:T(2,128)S(1)}, f32[128,2,256]{2,1,0:T(2,128)S(1)}, u32[]{:S(2)}, u32[]{:S(2)}) collective-permute-start(f32[128,2,256]{2,1,0:T(2,128)S(1)} %get-tuple-element.55), channel_id=1, source_target_pairs={{0,5},{1,4},{2,7},{3,6},{4,1},{5,0},{6,3},{7,2},{8,13},{9,12},{10,... | collective-permute-start | bytes 786440 | tf_op jit(solution)/shard_map/ppermute | solution.py:249
  238.4 16.0 %collective-permute-start.37 = (f32[128,2,256]{2,1,0:T(2,128)S(1)}, f32[128,2,256]{2,1,0:T(2,128)S(1)}, u32[]{:S(2)}, u32[]{:S(2)}) collective-permute-start(f32[128,2,256]{2,1,0:T(2,128)S(1)} %get-tuple-element.58), channel_id=1, source_target_pairs={{0,1},{1,0},{2,3},{3,2},{4,5},{5,4},{6,7},{7,6},{8,9},{9,8},{10,11... | collective-permute-start | bytes 786440 | tf_op jit(solution)/shard_map/ppermute | solution.py:248
  239.7 15.3 %collective-permute-start.38 = (f32[128,2,256]{2,1,0:T(2,128)S(1)}, f32[128,2,256]{2,1,0:T(2,128)S(1)}, u32[]{:S(2)}, u32[]{:S(2)}) collective-permute-start(f32[128,2,256]{2,1,0:T(2,128)S(1)} %get-tuple-element.59), channel_id=1, source_target_pairs={{0,4},{2,6},{4,0},{6,2},{1,5},{3,7},{5,1},{7,3},{8,12},{10,14},{12... | collective-permute-start | bytes 786440 | tf_op jit(solution)/shard_map/ppermute | solution.py:247
  248.0 10.9 %collective-permute-start.39 = (f32[128,2,256]{2,1,0:T(2,128)S(1)}, f32[128,2,256]{2,1,0:T(2,128)S(1)}, u32[]{:S(2)}, u32[]{:S(2)}) collective-permute-start(f32[128,2,256]{2,1,0:T(2,128)S(1)} %get-tuple-element.60), channel_id=1, source_target_pairs={{0,5},{1,4},{2,7},{3,6},{4,1},{5,0},{6,3},{7,2},{8,13},{9,12},{10,... | collective-permute-start | bytes 786440 | tf_op jit(solution)/shard_map/ppermute | solution.py:249
  (23 other events, 208.1 us)
Sparse Core Ops, SparseCore 0:
  100.4 16.7 all-gather.1

commit v2 on v1

--- a/solution.py
+++ b/solution.py
@@ -2,6 +2,7 @@
 import jax.numpy as jnp
 from jax import lax
 from jax.experimental import pallas as pl
+from jax.experimental.layout import Layout, with_layout_constraint
 from jax.experimental.pallas import tpu as pltpu
 from jax.sharding import PartitionSpec as P
 
@@ -108,6 +109,8 @@
 
 FINE = 32
 CHUNKS = 4
+GROUPS = 2
+ROWS = Layout(major_to_minor=(0, 1, 2, 3))
 VMEM = 48 * 1024 * 1024
 
 
@@ -193,40 +196,40 @@
     )(*table, *parts)
 
 
-def product_kernel(scale, own, near, mid, far, keep, send, here, over_y, over_x, over_xy, both):
-    rows, wide = own.shape
+def product_kernel(scale, first, own, near, one, two, three, four, keep, send, *refs):
+    outs, both = refs[:-1], refs[-1]
+    rows = both.shape[0] // 2
+    wide = own.shape[1]
     half = wide // 2
-    first = 0
-    for part in (own[...], near[...], mid[...] + far[...]):
-        for at in range(0, part.shape[1], wide):
-            real, imag = part[:, at : at + half], part[:, at + half : at + wide]
-            both[:rows, first : first + half] = real
-            both[:rows, first + half : first + wide] = -imag
-            both[rows:, first : first + half] = imag
-            both[rows:, first + half : first + wide] = real
-            first += wide
+    here = pl.ds(first, rows)
+    for slot, part in enumerate((own[here, :], near[here, :], one[here, :] + two[here, :], three[here, :] + four[...])):
+        at = slot * wide
+        real, imag = part[:, :half], part[:, half:]
+        both[:rows, at : at + half] = real
+        both[:rows, at + half : at + wide] = -imag
+        both[rows:, at : at + half] = imag
+        both[rows:, at + half : at + wide] = real
     middle = rows // 2
-    for side, one, two in ((keep, here, over_x), (send, over_y, over_xy)):
+    for side, one, two in ((keep, outs[0], outs[2]), (send, outs[1], outs[3])):
         total = nt(both[...], side[...]) * scale
         for t in range(2):
-            one[:, t, :] = total[t * rows : t * rows + middle]
-            two[:, t, :] = total[t * rows + middle : (t + 1) * rows]
-
-
-def product(scale, own, near, mid, far, keep, send):
-    rows = own.shape[0]
-    shape = jax.ShapeDtypeStruct((rows // 2, 2, keep.shape[0]), jnp.float32)
+            one[:, t, :] = total[t * rows : t * rows + middle].astype(one.dtype)
+            two[:, t, :] = total[t * rows + middle : (t + 1) * rows].astype(two.dtype)
+
+
+def product(scale, first, rows, parts, keep, send):
+    shape = (rows // 2, 2, keep.shape[0])
     return pl.pallas_call(
-        lambda *refs: product_kernel(scale, *refs),
-        out_shape=[shape] * 4,
-        in_specs=[pl.BlockSpec(memory_space=pltpu.VMEM)] * 6,
+        lambda *refs: product_kernel(scale, first, *refs),
+        out_shape=[jax.ShapeDtypeStruct(shape, kind) for kind in (jnp.float32,) + (jnp.bfloat16,) * 3],
+        in_specs=[pl.BlockSpec(memory_space=pltpu.VMEM)] * 8,
         out_specs=[pl.BlockSpec(memory_space=pltpu.VMEM)] * 4,
         scratch_shapes=[pltpu.VMEM((2 * rows, keep.shape[1]), jnp.bfloat16)],
         compiler_params=pltpu.CompilerParams(vmem_limit_bytes=VMEM),
         cost_estimate=pl.CostEstimate(
             flops=8 * rows * keep.shape[0] * keep.shape[1], bytes_accessed=4 * keep.size, transcendentals=0
         ),
-    )(own, near, mid, far, keep, send)
+    )(*parts, keep, send)
 
 
 def shards_plane(src_real, src_imag, rcv_real, rcv_imag, src_pos, rcv_pos, freqs):
@@ -249,30 +252,45 @@
     over_xy = lambda v: lax.ppermute(v, ("src", "rcv"), [(i, i ^ 5) for i in range(8)])
     over_z = lambda v, d: lax.ppermute(v, "tm", [(i, i ^ d) for i in range(n_z)])
 
-    def chain(v):
-        near = over_z(v, 1)
-        mid = lax.ppermute(jnp.concatenate([v, near], 1), "tm", [(1, 2), (2, 1)])
-        far = lax.ppermute(mid, "tm", [(1, 0), (2, 3)])
-        return v, near, mid, far
+    turn = [freqs]
+
+    def after(v, *others):
+        return lax.optimization_barrier((v, others))[0]
+
+    def step(v):
+        v = after(v, turn[0])
+        turn[0] = v
+        return v
+
+    ends = lambda v: lax.ppermute(v, "tm", [(1, 0), (2, 3)])
+    middle = lambda v: lax.ppermute(v, "tm", [(1, 2), (2, 1)])
 
     def bin_of(real, imag, which):
         return jnp.stack([lax.dynamic_index_in_dim(part, which, 0, False) for part in (real, imag)])
 
+    flat = lambda v: v.reshape(-1, v.shape[-1])
+    given = step(flat(bin_of(src_real, src_imag, 2 * (1 - x) + y)))
+    given = over_x(given)
     raw_last = lax.dynamic_slice_in_dim(jnp.stack([src_real[last], src_imag[last]]), y * half, half, 1)
-    raw_last = chain(raw_last.reshape(2 * half, a_block))
-
-    flat = lambda v: v.reshape(-1, v.shape[-1])
-    given = over_x(flat(bin_of(src_real, src_imag, 2 * (1 - x) + y)))
-    own = flat(bin_of(src_real, src_imag, mine))
-    x_mine = [own, given, core(own), core(given)]
-    theirs = jnp.stack([bin_of(rcv_real, rcv_imag, 2 * x + 1 - y), jnp.stack([rcv_real[last], rcv_imag[last]])])
-    given = over_y(lax.dynamic_slice_in_dim(theirs, c * half, half, 2))
-    other = core(given)
-    given, other = jnp.where(c == 0, given, other), jnp.where(c == 0, other, given)
-    given = jnp.concatenate([given, other], 2)
-    y_mine = [flat(bin_of(rcv_real, rcv_imag, mine)), flat(given[0])]
-    y_last = [flat(jnp.stack([rcv_real[last], rcv_imag[last]])), flat(given[1])]
-
+    raw_last = step(raw_last.reshape(2 * half, a_block))
+    raw_near = over_z(raw_last, 1)
+    raw_one = middle(raw_last)
+
+    def half_bin(which):
+        at = (which, c * half, 0)
+        return jnp.concatenate([lax.dynamic_slice(v, at, (1, half, b_block))[0] for v in (rcv_real, rcv_imag)], 0)
+
+    y_given = [half_bin(2 * x + 1 - y), half_bin(last)]
+    y_given = [over_y(step(v)) for v in y_given]
+    own = step(flat(bin_of(src_real, src_imag, mine)))
+    x_mine = [own, given, core(own)]
+    raw_near = step(raw_near)
+    raw_two = middle(raw_near)
+    raw_three = ends(step(raw_one))
+    x_mine[1] = step(x_mine[1])
+    x_mine.append(core(x_mine[1]))
+    raw_two = step(raw_two)
+    raw_four = ends(raw_two)
     take = lambda v, block, size: lax.dynamic_slice_in_dim(v, block * size, size)
     at_src = jnp.concatenate([take(src_pos, block, a_block) for block in (s, s ^ 2, s ^ 1, s ^ 3)])
     at_rcv = jnp.concatenate([take(rcv_pos, block, b_block) for block in (y, 1 - y)])
@@ -283,7 +301,24 @@
     starts = jnp.concatenate(
         [runs(first + k * chunk, chunk) for k in range(CHUNKS) for first in (here, there)]
     )
-    pieces = [chain(v) for v in steered(tables(f_mine, starts, SRC_SL, at_src), x_mine, CHUNKS)]
+    pieces = steered(tables(f_mine, starts, SRC_SL, at_src), x_mine, GROUPS)
+    pieces = step(pieces)
+    near = [over_z(v, 1) for v in pieces]
+    one = [middle(v) for v in pieces]
+    raw_three, raw_four = step((raw_three, raw_four))
+    slots = jnp.stack([raw_last, raw_near, raw_one + raw_three, raw_two + raw_four])
+    slots = step(slots.reshape(n_z, 2, half, a_block))
+    other_slots = over_y(slots)
+    rcv_real, rcv_imag = after((rcv_real, rcv_imag), pieces[0])
+
+    def receivers(which, given):
+        given = step(given)
+        other = core(given)
+        pair = jnp.stack([jnp.where(c == 0, given, other), jnp.where(c == 0, other, given)])
+        pair = pair.reshape(2, 2, half, b_block).transpose(1, 0, 2, 3).reshape(2 * wide, b_block)
+        return [flat(bin_of(rcv_real, rcv_imag, which)), pair]
+
+    y_mine, y_last = receivers(mine, y_given[0]), receivers(last, y_given[1])
 
     planes = [z ^ d for d in range(n_z)]
     r_mine = tables(
@@ -297,26 +332,35 @@
     )
     yr_mine = steered(r_mine, y_mine, n_z, sign=-1.0)
     yr_last = steered(r_last, y_last, 1, sign=-1.0)[0].reshape(n_z, q_sub, -1)
-    got = [jnp.concatenate([yr_mine[d], yr_last[d]], 0) for d in range(n_z)]
+    got = step([jnp.concatenate([yr_mine[d], yr_last[d]], 0) for d in range(n_z)])
     got = [got[0]] + [over_z(got[d], d) for d in range(1, n_z)]
+    two, three, four = [], [], []
+    for k in range(GROUPS):
+        near[k] = step(near[k])
+        two.append(middle(near[k]))
+        one[k] = step(one[k])
+        three.append(ends(one[k]))
+    got = step(got)
     got = [got[0], got[1], jnp.where(inner, got[3], got[2]), jnp.where(inner, got[2], got[3])]
     yr_mine = jnp.concatenate([v[:q_block] for v in got], 1)
     yr_last = jnp.concatenate([v[q_block:] for v in got], 1)
-
+    yr_mine = step(yr_mine)
     yr_other = core(yr_mine)
     keep_mine = jnp.where(c == y, yr_mine, yr_other)
     send_mine = jnp.where(c == y, yr_other, yr_mine)
+    three = step(three)
     yr_last = lax.all_gather(yr_last, "src", axis=0, tiled=True).reshape(q_block, n_z, 2, wide)
+    per = CHUNKS // GROUPS
+    for k in range(GROUPS):
+        two[k] = step(two[k])
+        four.append([ends(two[k][i * 2 * chunk : (i + 1) * 2 * chunk]) for i in range(per)])
 
     focus_scale = 1.0 / float(wide * n_z * RCV_ST) ** 0.5
     beam_scale = 1.0 / float(SRC_ST) ** 0.5
-    whole = jnp.zeros((p_block, bins, 2, q_block), jnp.float32)
-
-    own, near, mid, far = raw_last
-    slots = jnp.stack([own, near, (mid + far)[:, :a_block], (mid + far)[:, a_block:]])
-    slots = slots.reshape(n_z, 2, half, a_block)
-    other = over_y(slots)
-    slots = jnp.concatenate([jnp.where(y == 0, slots, other), jnp.where(y == 0, other, slots)], 2)
+    whole = with_layout_constraint(jnp.zeros((p_block, bins, 2, q_block), jnp.float32), ROWS)
+
+    other_slots = step(other_slots)
+    slots = jnp.concatenate([jnp.where(y == 0, slots, other_slots), jnp.where(y == 0, other_slots, slots)], 2)
     parts = jnp.einsum("qzuw,ztwa->utqa", yr_last, slots, preferred_element_type=jnp.float32) * focus_scale
     focus = jnp.concatenate([parts[0, 0] - parts[1, 1], parts[0, 1] + parts[1, 0]], 0).astype(jnp.bfloat16)
     table = tables(
@@ -331,11 +375,14 @@
     whole = lax.dynamic_update_slice(whole, shares[:, None], (0, last, 0, 0))
 
     for k in range(CHUNKS):
-        found = product(focus_scale * beam_scale, *pieces[k], keep_mine, send_mine)
+        g, i = k // per, k % per
+        parts = [pieces[g], near[g], one[g], three[g], two[g], step(four[g][i])]
+        found = product(focus_scale * beam_scale, i * 2 * chunk, 2 * chunk, parts, keep_mine, send_mine)
+        found = step(found)
         found = [found[0], over_y(found[1]), over_x(found[2]), over_xy(found[3])]
         for d in range(4):
-            whole = lax.dynamic_update_slice(whole, found[d][:, None], (k * chunk, mine ^ d, 0, 0))
-    return whole.transpose(0, 2, 1, 3)
+            whole = lax.dynamic_update_slice(whole, found[d].astype(jnp.float32)[:, None], (k * chunk, mine ^ d, 0, 0))
+    return with_layout_constraint(whole, ROWS).transpose(0, 2, 1, 3)
 
 
 def solution(mesh):

time: 271 us -> 227 us (0.84)
  waiting for transfers between devices: 110 us -> 65.3 us
  other arithmetic: 36.9 us -> 28.5 us
  starting transfers between devices: 53.7 us -> 58.4 us
  local copies, waits for them, and re-layouts: 21.1 us -> 25 us
    ppermute x6 -> x7, waiting for transfers between devices: 31.3 us -> 2.87 us  [shards_plane(): over_y = lambda v: lax.ppermute(v, 'rcv', [(0, 1), (1, 0)])]
    ppermute x10 -> x14, waiting for transfers between devices: 47.4 us -> 35 us  [the longest x8 35 us: shards_plane(): ends = lambda v: lax.ppermute(v, 'tm', [(1, 0), (2, 3)])]
    unnamed x60 -> x34, local copies, waits for them, and re-layouts: 3.47 us -> 8.9 us
    transpose x1 -> x0, local copies, waits for them, and re-layouts: 4.16 us -> none  [shards_plane(): return whole.transpose(0, 2, 1, 3)]
    ppermute x8 -> x6, waiting for transfers between devices: 26.3 us -> 23 us  [shards_plane(): lax.ppermute(v, 'tm', [(i, i ^ d) for i in range(n_z)])]
    ppermute x10 -> x14, starting transfers between devices: 13.7 us -> 16.9 us  [the longest x8 10.3 us: shards_plane(): ends = lambda v: lax.ppermute(v, 'tm', [(1, 0), (2, 3)])]
    ppermute x4, starting transfers between devices: 5.93 us -> 2.99 us  [shards_plane(): lax.ppermute(v, ('src', 'rcv'), [(i, i ^ 5) for i in range(8)])]
    ppermute x8 -> x6, starting transfers between devices: 19 us -> 21.8 us  [shards_plane(): lax.ppermute(v, 'tm', [(i, i ^ d) for i in range(n_z)])]
  transfers between devices with their start and end apart: 41 -> 45, of which waited for: 17 -> 15; matrix products, arithmetic and copies ran while one was open for 19% -> 16% of each run, Pallas kernels for 11% -> 10%
where the time goes in v2:
time: 227 us; the launch traced here: 226 us
  waiting for transfers between devices  65.3 us (29%)
  starting transfers between devices  58.4 us (26%)
  other arithmetic  28.5 us (13%)
  Pallas kernels  28.5 us (13%)
  local copies, waits for them, and re-layouts  25 us (11%)
  between operations  16.7 us (7%)
  matrix products  3.1 us (1%)
    ppermute x8, waiting for transfers between devices, shards_plane(): ends = lambda v: lax.ppermute(v, 'tm', [(1, 0), (2, 3)])  35 us
    ppermute x6, waiting for transfers between devices, shards_plane(): lax.ppermute(v, 'tm', [(i, i ^ d) for i in range(n_z)])  23 us
    ppermute x6, starting transfers between devices, shards_plane(): lax.ppermute(v, 'tm', [(i, i ^ d) for i in range(n_z)])  21.8 us
    pallas_call x4, Pallas kernels, steered(): pl.pallas_call(lambda *refs: steered_kernel(sign, scale, len(parts), *ref...  17.3 us
    pallas_call x4, Pallas kernels, product(): pl.pallas_call(lambda *refs: product_kernel(scale, first, *refs), out_sha...  11.3 us
    ppermute x8, starting transfers between devices, shards_plane(): ends = lambda v: lax.ppermute(v, 'tm', [(1, 0), (2, 3)])  10.3 us
    ppermute x7, starting transfers between devices, shards_plane(): over_y = lambda v: lax.ppermute(v, 'rcv', [(0, 1), (1, 0)])  8.95 us
    unnamed x34, local copies, waits for them, and re-layouts  8.9 us
  transfers between devices with their start and end apart: 45, of which 15 were waited for; matrix products, arithmetic and copies ran while one was open for 16% of the time, Pallas kernels for 10%

profile of v2, /device:TPU:0, one launch (start us, length us, event | category | flops | bytes accessed | tf_op | source)
XLA Modules:
  0.0 225.5 jit_solution(17050750369672655691)
XLA Ops:
  10.5 3.0 %collective-permute-start = (bf16[256,512]{1,0:T(8,128)(2,1)}, bf16[256,512]{1,0:T(8,128)(2,1)}, u32[]{:S(2)}, u32[]{:S(2)}) collective-permute-start(bf16[256,512]{1,0:T(8,128)(2,1)} %bitcast.2), channel_id=1, source_target_pairs={{0,8},{8,0},{16,24},{24,16},{1,9},{9,1},{17,25},{25,17},{2,10},{10... | collective-permute-start | bytes 786440 | tf_op jit(solution)/shard_map/ppermute | solution.py:253
  13.5 1.3 collective-permute-start.1
  14.8 1.5 collective-permute-start.4
  19.3 1.5 collective-permute-start.12
  25.1 5.6 %multiply_sine_fusion.1 = (f32[32,2048]{1,0:T(8,128)S(1)}, f32[32,2048]{1,0:T(8,128)S(1)}, f32[32,2048]{1,0:T(8,128)S(1)}, f32[32,2048]{1,0:T(8,128)S(1)}, f32[3...) fusion(f32[2048]{0:T(1024)S(1)} %pad_maximum_fusion.17, ...), kind=kLoop, calls=%fused_computation.35 | loop fusion | flops 327680 | bytes 2638336 | tf_op jit(solution)/shard_map/sin | solution.py:119
  39.5 5.0 %shard_map.73 = (bf16[512,512]{1,0:T(8,128)(2,1)S(1)}, bf16[512,512]{1,0:T(8,128)(2,1)S(1)}) custom-call(f32[32,2048]{1,0:T(8,128)S(1)} %get-tuple-element.232.refs_0_, f32[32,2048]{1,0:T(8,128)S(1)} %get-tuple-element.231.refs_1_, f32[32,2048]{1,0:T(8,128)S(1)} %copy-done.4, f32[32,2048]{1,0:T(8,128)S(1)} %copy-done.5, bf16[512,512]{1,0:T(8,128)(2,1)S(1)} %bitcast.99, ...), custom_call_target="tpu_custom_call" | custom-call | flops 4294967296 | bytes 2097152 | tf_op jit(solution)/shard_map/pallas_call | solution.py:183
  44.5 13.3 %collective-permute-start.11 = (bf16[512,512]{1,0:T(8,128)(2,1)S(1)}, bf16[512,512]{1,0:T(8,128)(2,1)S(1)}, u32[]{:S(2)}, u32[]{:S(2)}) collective-permute-start(bf16[512,512]{1,0:T(8,128)(2,1)S(1)} %get-tuple-element.98.refs_0_), channel_id=1, source_target_pairs={{0,8},{8,0},{16,24},{24,16},{1,9},{9,1},{17,25},{25,17},{2,10},{10... | collective-permute-start | bytes 1572872 | tf_op jit(solution)/shard_map/ppermute | solution.py:253
  57.8 1.5 collective-permute-start.10
  59.2 2.1 collective-permute-done.5
  62.5 2.1 pad_maximum_fusion
  65.1 1.7 constant_dynamic-slice_fusion
  67.5 1.5 collective-permute-start.19
  69.0 1.3 broadcast_select_fusion.5
  70.6 5.5 %shard_map.74 = (bf16[256,512]{1,0:T(8,128)(2,1)S(1)}, bf16[256,512]{1,0:T(8,128)(2,1)S(1)}, bf16[256,512]{1,0:T(8,128)(2,1)S(1)}, bf16[256,512]{1,0:T(8,128)(2,1)S(1)}) custom-call(f32[32,2048]{1,0:T(8,128)S(1)} %get-tuple-element.217.refs_0_, f32[32,2048]{1,0:T(8,128)S(1)} %copy-done.3, f32[32,2048]{1,0:T(8,128)S(1)} %get-tuple-element.204.refs_2_, ...), custom_call_target="tpu_custom_call" | custom-call | flops 4294967296 | bytes 2097152 | tf_op jit(solution)/shard_map/pallas_call | solution.py:183
  76.1 1.3 shard_map.75
  78.2 2.7 %collective-permute-start.21 = (bf16[320,512]{1,0:T(8,128)(2,1)}, bf16[320,512]{1,0:T(8,128)(2,1)S(1)}, u32[]{:S(2)}, u32[]{:S(2)}) collective-permute-start(bf16[320,512]{1,0:T(8,128)(2,1)} %pad_maximum_fusion.12), channel_id=1, source_target_pairs={{0,8},{8,0},{16,24},{24,16},{1,9},{9,1},{17,25},{25,17},{2,10},{10... | collective-permute-start | bytes 983048 | tf_op jit(solution)/shard_map/ppermute | solution.py:253
  81.0 1.3 collective-permute-start.22
  82.3 1.4 collective-permute-start.23
  83.7 12.2 %collective-permute-done.21 = bf16[320,512]{1,0:T(8,128)(2,1)S(1)} collective-permute-done((bf16[320,512]{1,0:T(8,128)(2,1)}, bf16[320,512]{1,0:T(8,128)(2,1)S(1)}, u32[]{:S(2)}, u32[]{:S(2)}) %collective-permute-start.21) | collective-permute-done | bytes 327712 | tf_op jit(solution)/shard_map/ppermute | solution.py:253
  95.9 10.8 %collective-permute-done.22 = bf16[320,512]{1,0:T(8,128)(2,1)} collective-permute-done((bf16[320,512]{1,0:T(8,128)(2,1)S(1)}, bf16[320,512]{1,0:T(8,128)(2,1)}, u32[]{:S(2)}, u32[]{:S(2)}) %collective-permute-start.22) | collective-permute-done | bytes 327712 | tf_op jit(solution)/shard_map/ppermute | solution.py:253
  109.4 1.6 collective-permute-start.8
  121.2 11.5 %collective-permute-done.20.refs_3_ = bf16[512,512]{1,0:T(8,128)(2,1)} collective-permute-done((bf16[512,512]{1,0:T(8,128)(2,1)}, bf16[512,512]{1,0:T(8,128)(2,1)}, u32[]{:S(2)}, u32[]{:S(2)}) %collective-permute-start.20) | collective-permute-done | bytes 524320 | tf_op jit(solution)/shard_map/ppermute | solution.py:265
  132.7 9.6 %collective-permute-done.18.refs_3_ = bf16[512,512]{1,0:T(8,128)(2,1)} collective-permute-done((bf16[512,512]{1,0:T(8,128)(2,1)}, bf16[512,512]{1,0:T(8,128)(2,1)}, u32[]{:S(2)}, u32[]{:S(2)}) %collective-permute-start.18) | collective-permute-done | bytes 524320 | tf_op jit(solution)/shard_map/ppermute | solution.py:265
  142.3 3.0 %broadcast_select_fusion.3 = (bf16[4,2,128,512]{3,2,0,1:T(8,128)(2,1)}, bf16[4,2,128,512]{3,2,0,1:T(8,128)(2,1)}) fusion(bf16[4,2,128,512]{3,2,0,1:T(8,128)(2,1)} %pad_maximum_fusion, bf16[4,2,128,512]{3,2,0,1:T(8,128)(2,1)} %collective-permute-done.8, pred[]{:T(512)S(6)} %eq.22), kind=kLoop, calls=%fused_computation.17 | loop fusion | flops 1048576 | bytes 4194305 | tf_op jit(solution)/shard_map/jit(_where)/select_n | solution.py:363
  145.3 2.6 %reshape.226 = bf16[256,4,2,256]{3,2,1,0:T(2,128)(2,1)} reshape(bf16[256,2048]{1,0:T(8,128)(2,1)} %all-gather.2.cloned.1.call-done) | data formatting | bytes 2097152 | tf_op jit(solution)/shard_map/reshape | solution.py:352
  148.0 3.1 %fusion.3 = f32[2,2,256,512]{3,2,1,0:T(8,128)S(1)} fusion(bf16[4,2,128,512]{3,2,0,1:T(8,128)(2,1)} %get-tuple-element.182, bf16[4,2,128,512]{3,2,0,1:T(8,128)(2,1)} %get-tuple-element.181, bf16[256,4,2,256,1]{3,2,1,0,4:T(2,128)(2,1)} %bitcast.104), kind=kOutput, calls=%fused_computation.5 | convolution fusion | flops 1078460416 | bytes 5242880 | tf_op jit(solution)/shard_map/qzuw,ztwa->utqa/dot_general | solution.py:364
  151.3 5.5 %shard_map.76 = (f32[512,2,256]{2,1,0:T(2,128)S(1)}, f32[512,2,256]{2,1,0:T(2,128)S(1)}, f32[512,2,256]{2,1,0:T(2,128)S(1)}, f32[512,2,256]{2,1,0:T(2,128)}) custom-call(f32[64,512]{1,0:T(8,128)S(1)} %get-tuple-element.230.refs_0_, f32[64,512]{1,0:T(8,128)S(1)} %get-tuple-element.229.refs_1_, f32[32,512]{1,0:T(8,128)S(1)} %get-tuple-element.228.refs_2_, ...), custom_call_target="tpu_custom_call" | custom-call | flops 2147483648 | bytes 524288 | tf_op jit(solution)/shard_map/pallas_call | solution.py:183
  161.7 2.1 add.450
  164.5 1.3 collective-permute-start.32
  165.8 9.2 %collective-permute-done.27.refs_5_ = bf16[256,512]{1,0:T(8,128)(2,1)S(1)} collective-permute-done((bf16[256,512]{1,0:T(8,128)(2,1)}, bf16[256,512]{1,0:T(8,128)(2,1)S(1)}, u32[]{:S(2)}, u32[]{:S(2)}) %collective-permute-start.27) | collective-permute-done | bytes 262176 | tf_op jit(solution)/shard_map/ppermute | solution.py:265
  176.2 1.3 collective-permute-start.40
  177.5 1.7 broadcast_select_fusion
  179.2 2.8 %shard_map.77 = (f32[128,2,256]{2,1,0:T(2,128)S(1)}, bf16[128,2,256]{2,1,0:T(2,128)(2,1)S(1)}, bf16[128,2,256]{2,1,0:T(2,128)(2,1)S(1)}, bf16[128,2,256]{2,1,0:T(2,128)(2,1)S(1)}) custom-call(bf16[512,512]{1,0:T(8,128)(2,1)S(1)} %get-tuple-element.98.refs_0_, bf16[512,512]{1,0:T(8,128)(2,1)S(1)} %collective-permute-done.11.refs_1_, ...), custom_call_target="tpu_custom_call" | custom-call | flops 1073741824 | bytes 2097152 | tf_op jit(solution)/shard_map/pallas_call | solution.py:222
  182.6 2.8 %shard_map.78 = (f32[128,2,256]{2,1,0:T(2,128)S(1)}, bf16[128,2,256]{2,1,0:T(2,128)(2,1)S(1)}, bf16[128,2,256]{2,1,0:T(2,128)(2,1)S(1)}, bf16[128,2,256]{2,1,0:T(2,128)(2,1)S(1)}) custom-call(bf16[512,512]{1,0:T(8,128)(2,1)S(1)} %get-tuple-element.98.refs_0_, bf16[512,512]{1,0:T(8,128)(2,1)S(1)} %collective-permute-done.11.refs_1_, ...), custom_call_target="tpu_custom_call" | custom-call | flops 1073741824 | bytes 2097152 | tf_op jit(solution)/shard_map/pallas_call | solution.py:222
  186.4 2.8 %shard_map.79 = (f32[128,2,256]{2,1,0:T(2,128)S(1)}, bf16[128,2,256]{2,1,0:T(2,128)(2,1)S(1)}, bf16[128,2,256]{2,1,0:T(2,128)(2,1)S(1)}, bf16[128,2,256]{2,1,0:T(2,128)(2,1)S(1)}) custom-call(bf16[512,512]{1,0:T(8,128)(2,1)S(1)} %get-tuple-element.99.refs_0_, bf16[512,512]{1,0:T(8,128)(2,1)S(1)} %collective-permute-done.9.refs_1_, ...), custom_call_target="tpu_custom_call" | custom-call | flops 1073741824 | bytes 2097152 | tf_op jit(solution)/shard_map/pallas_call | solution.py:222
  189.3 1.9 collective-permute-done.40.refs_5_
  191.6 2.8 %shard_map.80 = (f32[128,2,256]{2,1,0:T(2,128)S(1)}, bf16[128,2,256]{2,1,0:T(2,128)(2,1)S(1)}, bf16[128,2,256]{2,1,0:T(2,128)(2,1)S(1)}, bf16[128,2,256]{2,1,0:T(2,128)(2,1)S(1)}) custom-call(bf16[512,512]{1,0:T(8,128)(2,1)S(1)} %get-tuple-element.99.refs_0_, bf16[512,512]{1,0:T(8,128)(2,1)S(1)} %collective-permute-done.9.refs_1_, ...), custom_call_target="tpu_custom_call" | custom-call | flops 1073741824 | bytes 2097152 | tf_op jit(solution)/shard_map/pallas_call | solution.py:222
  194.5 1.6 collective-permute-start.33
  196.0 1.5 collective-permute-start.34
  198.3 1.4 pad
  200.5 1.6 collective-permute-start.37
  202.2 1.6 collective-permute-start.38
  204.7 1.6 collective-permute-start.41
  208.2 1.6 collective-permute-done.37
  209.8 1.5 collective-permute-start.43
  211.5 1.3 collective-permute-done.39
  214.7 1.5 collective-permute-done.43
  216.3 2.3 %copy-done.9 = f32[512,5,2,256]{3,2,1,0:T(2,128)} copy-done((f32[512,5,2,256]{3,2,1,0:T(2,128)}, f32[512,5,2,256]{3,2,1,0:T(2,128)S(1)}, u32[]{:S(2)}) %copy-start.9) | copy-done | bytes 5242904
  (178 shorter events, 49.0 us)
Async XLA Ops:
  6.5 18.4 %copy-start.14 = (f32[2048]{0:T(1024)S(1)}, f32[2048]{0:T(1024)}, u32[]{:S(2)}) copy-start(f32[2048]{0:T(1024)} %param.12) | copy-start | bytes 24580
  6.5 18.5 %copy-start.15 = (f32[2048]{0:T(1024)S(1)}, f32[2048]{0:T(1024)}, u32[]{:S(2)}) copy-start(f32[2048]{0:T(1024)} %param.11) | copy-start | bytes 24580
  6.5 138.8 %all-gather.2.cloned.1.call-start = ((), (), s32[]{:S(2)}) async-start(), calls=%async_computation | async-start | bytes 1310720 | tf_op jit(solution)/shard_map/all_gather | solution.py:352
  10.5 21.0 %collective-permute-start = (bf16[256,512]{1,0:T(8,128)(2,1)}, bf16[256,512]{1,0:T(8,128)(2,1)}, u32[]{:S(2)}, u32[]{:S(2)}) collective-permute-start(bf16[256,512]{1,0:T(8,128)(2,1)} %bitcast.2), channel_id=1, source_target_pairs={{0,8},{8,0},{16,24},{24,16},{1,9},{9,1},{17,25},{25,17},{2,10},{10... | collective-permute-start | bytes 786440 | tf_op jit(solution)/shard_map/ppermute | solution.py:253
  13.5 18.0 %collective-permute-start.1 = (bf16[256,512]{1,0:T(8,128)(2,1)}, bf16[256,512]{1,0:T(8,128)(2,1)}, u32[]{:S(2)}, u32[]{:S(2)}) collective-permute-start(bf16[256,512]{1,0:T(8,128)(2,1)} %bitcast.2), channel_id=1, source_target_pairs={{8,16},{16,8},{9,17},{17,9},{10,18},{18,10},{11,19},{19,11},{12,20... | collective-permute-start | bytes 786440 | tf_op jit(solution)/shard_map/ppermute | solution.py:266
  14.8 16.7 %collective-permute-start.4 = (bf16[512,512]{1,0:T(8,128)(2,1)}, bf16[512,512]{1,0:T(8,128)(2,1)S(1)}, u32[]{:S(2)}, u32[]{:S(2)}) collective-permute-start(bf16[512,512]{1,0:T(8,128)(2,1)} %bitcast.3), channel_id=1, source_target_pairs={{0,4},{2,6},{4,0},{6,2},{1,5},{3,7},{5,1},{7,3},{8,12},{10,14},{12... | collective-permute-start | bytes 1572872 | tf_op jit(solution)/shard_map/ppermute | solution.py:250
  19.3 45.3 %collective-permute-start.12 = (bf16[256,1024]{1,0:T(8,128)(2,1)}, bf16[256,1024]{1,0:T(8,128)(2,1)}, u32[]{:S(2)}, u32[]{:S(2)}) collective-permute-start(bf16[256,1024]{1,0:T(8,128)(2,1)} %pad_maximum_fusion.9), channel_id=1, source_target_pairs={{0,1},{1,0},{2,3},{3,2},{4,5},{5,4},{6,7},{7,6},{8,9},{9,8},{10,11... | collective-permute-start | bytes 1572872 | tf_op jit(solution)/shard_map/ppermute | solution.py:251
  21.7 42.9 %collective-permute-start.14 = (bf16[256,1024]{1,0:T(8,128)(2,1)}, bf16[256,1024]{1,0:T(8,128)(2,1)}, u32[]{:S(2)}, u32[]{:S(2)}) collective-permute-start(bf16[256,1024]{1,0:T(8,128)(2,1)} %pad_maximum_fusion.8), channel_id=1, source_target_pairs={{0,1},{1,0},{2,3},{3,2},{4,5},{5,4},{6,7},{7,6},{8,9},{9,8},{10,11... | collective-permute-start | bytes 1572872 | tf_op jit(solution)/shard_map/ppermute | solution.py:251
  31.5 3.8 %collective-permute-start.6 = (bf16[512,512]{1,0:T(8,128)(2,1)S(1)}, bf16[512,512]{1,0:T(8,128)(2,1)S(1)}, u32[]{:S(2)}, u32[]{:S(2)}) collective-permute-start(bf16[512,512]{1,0:T(8,128)(2,1)S(1)} %bitcast.98), channel_id=1, source_target_pairs={{0,2},{2,0},{4,6},{6,4},{1,3},{3,1},{5,7},{7,5},{8,10},{10,8},{12,... | collective-permute-start | bytes 1572872 | tf_op jit(solution)/shard_map/ppermute | solution.py:249
  31.6 5.0 %collective-permute-start.7 = (bf16[512,512]{1,0:T(8,128)(2,1)S(1)}, bf16[512,512]{1,0:T(8,128)(2,1)S(1)}, u32[]{:S(2)}, u32[]{:S(2)}) collective-permute-start(bf16[512,512]{1,0:T(8,128)(2,1)S(1)} %collective-permute-done.4.refs_5_), channel_id=1, source_target_pairs={{0,2},{2,0},{4,6},{6,4},{1,3},{3,1},{5,7},{7,5},{8,10},{10,8},{12,... | collective-permute-start | bytes 1572872 | tf_op jit(solution)/shard_map/ppermute | solution.py:249
  32.9 1.0 collective-permute-start.3
  33.9 23.9 %collective-permute-start.2 = (bf16[256,512]{1,0:T(8,128)(2,1)}, bf16[256,512]{1,0:T(8,128)(2,1)S(1)}, u32[]{:S(2)}, u32[]{:S(2)}) collective-permute-start(bf16[256,512]{1,0:T(8,128)(2,1)} %collective-permute-done.1), channel_id=1, source_target_pairs={{8,0},{16,24},{9,1},{17,25},{10,2},{18,26},{11,3},{19,27},{12,4},{... | collective-permute-start | bytes 786440 | tf_op jit(solution)/shard_map/ppermute | solution.py:265
  35.2 26.2 %collective-permute-start.5 = (bf16[256,512]{1,0:T(8,128)(2,1)S(1)}, bf16[256,512]{1,0:T(8,128)(2,1)S(1)}, u32[]{:S(2)}, u32[]{:S(2)}) collective-permute-start(bf16[256,512]{1,0:T(8,128)(2,1)S(1)} %collective-permute-done.3), channel_id=1, source_target_pairs={{8,0},{16,24},{9,1},{17,25},{10,2},{18,26},{11,3},{19,27},{12,4},{... | collective-permute-start | bytes 786440 | tf_op jit(solution)/shard_map/ppermute | solution.py:265
  44.5 36.5 %collective-permute-start.11 = (bf16[512,512]{1,0:T(8,128)(2,1)S(1)}, bf16[512,512]{1,0:T(8,128)(2,1)S(1)}, u32[]{:S(2)}, u32[]{:S(2)}) collective-permute-start(bf16[512,512]{1,0:T(8,128)(2,1)S(1)} %get-tuple-element.98.refs_0_), channel_id=1, source_target_pairs={{0,8},{8,0},{16,24},{24,16},{1,9},{9,1},{17,25},{25,17},{2,10},{10... | collective-permute-start | bytes 1572872 | tf_op jit(solution)/shard_map/ppermute | solution.py:253
  57.8 24.5 %collective-permute-start.10 = (bf16[512,512]{1,0:T(8,128)(2,1)S(1)}, bf16[512,512]{1,0:T(8,128)(2,1)}, u32[]{:S(2)}, u32[]{:S(2)}) collective-permute-start(bf16[512,512]{1,0:T(8,128)(2,1)S(1)} %get-tuple-element.98.refs_0_), channel_id=1, source_target_pairs={{8,16},{16,8},{9,17},{17,9},{10,18},{18,10},{11,19},{19,11},{12,20... | collective-permute-start | bytes 1572872 | tf_op jit(solution)/shard_map/ppermute | solution.py:266
  61.4 22.4 %collective-permute-start.9 = (bf16[512,512]{1,0:T(8,128)(2,1)S(1)}, bf16[512,512]{1,0:T(8,128)(2,1)S(1)}, u32[]{:S(2)}, u32[]{:S(2)}) collective-permute-start(bf16[512,512]{1,0:T(8,128)(2,1)S(1)} %get-tuple-element.99.refs_0_), channel_id=1, source_target_pairs={{0,8},{8,0},{16,24},{24,16},{1,9},{9,1},{17,25},{25,17},{2,10},{10... | collective-permute-start | bytes 1572872 | tf_op jit(solution)/shard_map/ppermute | solution.py:253
  64.6 4.4 %collective-permute-start.13 = (bf16[256,1024]{1,0:T(8,128)(2,1)}, bf16[256,1024]{1,0:T(8,128)(2,1)S(1)}, u32[]{:S(2)}, u32[]{:S(2)}) collective-permute-start(bf16[256,1024]{1,0:T(8,128)(2,1)} %collective-permute-done.12), channel_id=1, source_target_pairs={{0,2},{2,0},{4,6},{6,4},{1,3},{3,1},{5,7},{7,5},{8,10},{10,8},{12,... | collective-permute-start | bytes 1572872 | tf_op jit(solution)/shard_map/ppermute | solution.py:249
  64.6 2.9 %collective-permute-start.15 = (bf16[256,1024]{1,0:T(8,128)(2,1)}, bf16[256,1024]{1,0:T(8,128)(2,1)S(1)}, u32[]{:S(2)}, u32[]{:S(2)}) collective-permute-start(bf16[256,1024]{1,0:T(8,128)(2,1)} %collective-permute-done.14), channel_id=1, source_target_pairs={{0,2},{2,0},{4,6},{6,4},{1,3},{3,1},{5,7},{7,5},{8,10},{10,8},{12,... | collective-permute-start | bytes 1572872 | tf_op jit(solution)/shard_map/ppermute | solution.py:249
  67.5 16.3 %collective-permute-start.19 = (bf16[512,512]{1,0:T(8,128)(2,1)S(1)}, bf16[512,512]{1,0:T(8,128)(2,1)}, u32[]{:S(2)}, u32[]{:S(2)}) collective-permute-start(bf16[512,512]{1,0:T(8,128)(2,1)S(1)} %get-tuple-element.99.refs_0_), channel_id=1, source_target_pairs={{8,16},{16,8},{9,17},{17,9},{10,18},{18,10},{11,19},{19,11},{12,20... | collective-permute-start | bytes 1572872 | tf_op jit(solution)/shard_map/ppermute | solution.py:266
  78.2 35.7 %copy-start.10 = (bf16[320,512]{1,0:T(8,128)(2,1)}, bf16[320,512]{1,0:T(8,128)(2,1)S(1)}, u32[]{:S(2)}) copy-start(bf16[320,512]{1,0:T(8,128)(2,1)S(1)} %pad_maximum_fusion.11) | copy-start | bytes 983044
  78.2 17.7 %collective-permute-start.21 = (bf16[320,512]{1,0:T(8,128)(2,1)}, bf16[320,512]{1,0:T(8,128)(2,1)S(1)}, u32[]{:S(2)}, u32[]{:S(2)}) collective-permute-start(bf16[320,512]{1,0:T(8,128)(2,1)} %pad_maximum_fusion.12), channel_id=1, source_target_pairs={{0,8},{8,0},{16,24},{24,16},{1,9},{9,1},{17,25},{25,17},{2,10},{10... | collective-permute-start | bytes 983048 | tf_op jit(solution)/shard_map/ppermute | solution.py:253
  81.0 25.7 %collective-permute-start.22 = (bf16[320,512]{1,0:T(8,128)(2,1)S(1)}, bf16[320,512]{1,0:T(8,128)(2,1)}, u32[]{:S(2)}, u32[]{:S(2)}) collective-permute-start(bf16[320,512]{1,0:T(8,128)(2,1)S(1)} %pad_maximum_fusion.13), channel_id=1, source_target_pairs={{0,16},{8,24},{16,0},{24,8},{1,17},{9,25},{17,1},{25,9},{2,18},{10... | collective-permute-start | bytes 983048 | tf_op jit(solution)/shard_map/ppermute | solution.py:253
  82.3 24.4 %collective-permute-start.23 = (bf16[320,512]{1,0:T(8,128)(2,1)S(1)}, bf16[320,512]{1,0:T(8,128)(2,1)}, u32[]{:S(2)}, u32[]{:S(2)}) collective-permute-start(bf16[320,512]{1,0:T(8,128)(2,1)S(1)} %pad_maximum_fusion.14), channel_id=1, source_target_pairs={{0,24},{8,16},{16,8},{24,0},{1,25},{9,17},{17,9},{25,1},{2,26},{10... | collective-permute-start | bytes 983048 | tf_op jit(solution)/shard_map/ppermute | solution.py:253
  109.4 32.8 %collective-permute-start.8 = (bf16[4,2,128,512]{3,2,0,1:T(8,128)(2,1)}, bf16[4,2,128,512]{3,2,0,1:T(8,128)(2,1)}, u32[]{:S(2)}, u32[]{:S(2)}) collective-permute-start(bf16[4,2,128,512]{3,2,0,1:T(8,128)(2,1)} %pad_maximum_fusion), channel_id=1, source_target_pairs={{0,1},{1,0},{2,3},{3,2},{4,5},{5,4},{6,7},{7,6},{8,9},{9,8},{10,11... | collective-permute-start | bytes 3145736 | tf_op jit(solution)/shard_map/ppermute | solution.py:251
  111.3 21.3 %collective-permute-start.20 = (bf16[512,512]{1,0:T(8,128)(2,1)}, bf16[512,512]{1,0:T(8,128)(2,1)}, u32[]{:S(2)}, u32[]{:S(2)}) collective-permute-start(bf16[512,512]{1,0:T(8,128)(2,1)} %collective-permute-done.19.refs_2_), channel_id=1, source_target_pairs={{8,0},{16,24},{9,1},{17,25},{10,2},{18,26},{11,3},{19,27},{12,4},{... | collective-permute-start | bytes 1572872 | tf_op jit(solution)/shard_map/ppermute | solution.py:265
  112.7 29.6 %collective-permute-start.18 = (bf16[512,512]{1,0:T(8,128)(2,1)}, bf16[512,512]{1,0:T(8,128)(2,1)}, u32[]{:S(2)}, u32[]{:S(2)}) collective-permute-start(bf16[512,512]{1,0:T(8,128)(2,1)} %collective-permute-done.10.refs_2_), channel_id=1, source_target_pairs={{8,0},{16,24},{9,1},{17,25},{10,2},{18,26},{11,3},{19,27},{12,4},{... | collective-permute-start | bytes 1572872 | tf_op jit(solution)/shard_map/ppermute | solution.py:265
  114.0 28.3 %collective-permute-start.17 = (bf16[512,512]{1,0:T(8,128)(2,1)S(1)}, bf16[512,512]{1,0:T(8,128)(2,1)S(1)}, u32[]{:S(2)}, u32[]{:S(2)}) collective-permute-start(bf16[512,512]{1,0:T(8,128)(2,1)S(1)} %collective-permute-done.11.refs_1_), channel_id=1, source_target_pairs={{8,16},{16,8},{9,17},{17,9},{10,18},{18,10},{11,19},{19,11},{12,20... | collective-permute-start | bytes 1572872 | tf_op jit(solution)/shard_map/ppermute | solution.py:266
  114.7 27.6 %collective-permute-start.16 = (bf16[512,512]{1,0:T(8,128)(2,1)S(1)}, bf16[512,512]{1,0:T(8,128)(2,1)S(1)}, u32[]{:S(2)}, u32[]{:S(2)}) collective-permute-start(bf16[512,512]{1,0:T(8,128)(2,1)S(1)} %collective-permute-done.9.refs_1_), channel_id=1, source_target_pairs={{8,16},{16,8},{9,17},{17,9},{10,18},{18,10},{11,19},{19,11},{12,20... | collective-permute-start | bytes 1572872 | tf_op jit(solution)/shard_map/ppermute | solution.py:266
  158.7 3.0 %collective-permute-start.25 = (f32[512,2,256]{2,1,0:T(2,128)}, f32[512,2,256]{2,1,0:T(2,128)}, u32[]{:S(2)}, u32[]{:S(2)}) collective-permute-start(f32[512,2,256]{2,1,0:T(2,128)} %get-tuple-element.132), channel_id=1, source_target_pairs={{0,2},{2,0},{4,6},{6,4},{1,3},{3,1},{5,7},{7,5},{8,10},{10,8},{12,... | collective-permute-start | bytes 3145736 | tf_op jit(solution)/shard_map/ppermute | solution.py:249
  158.7 17.5 %collective-permute-start.28 = (bf16[256,2048]{1,0:T(8,128)(2,1)}, bf16[256,2048]{1,0:T(8,128)(2,1)}, u32[]{:S(2)}, u32[]{:S(2)}) collective-permute-start(bf16[256,2048]{1,0:T(8,128)(2,1)} %pad_maximum_fusion.5), channel_id=1, source_target_pairs={{0,2},{2,0},{4,6},{6,4},{1,3},{3,1},{5,7},{7,5},{8,10},{10,8},{12,... | collective-permute-start | bytes 3145736 | tf_op jit(solution)/shard_map/ppermute | solution.py:249
  160.1 14.9 %collective-permute-start.27 = (bf16[256,512]{1,0:T(8,128)(2,1)}, bf16[256,512]{1,0:T(8,128)(2,1)S(1)}, u32[]{:S(2)}, u32[]{:S(2)}) collective-permute-start(bf16[256,512]{1,0:T(8,128)(2,1)} %get-tuple-element.198), channel_id=1, source_target_pairs={{8,0},{16,24},{9,1},{17,25},{10,2},{18,26},{11,3},{19,27},{12,4},{... | collective-permute-start | bytes 786440 | tf_op jit(solution)/shard_map/ppermute | solution.py:265
  161.4 33.1 %collective-permute-start.24 = (f32[512,2,256]{2,1,0:T(2,128)}, f32[512,2,256]{2,1,0:T(2,128)S(1)}, u32[]{:S(2)}, u32[]{:S(2)}) collective-permute-start(f32[512,2,256]{2,1,0:T(2,128)} %copy-done.6), channel_id=1, source_target_pairs={{0,2},{2,0},{4,6},{6,4},{1,3},{3,1},{5,7},{7,5},{8,10},{10,8},{12,... | collective-permute-start | bytes 3145736 | tf_op jit(solution)/shard_map/ppermute | solution.py:249
  163.8 32.2 %collective-permute-start.26 = (f32[512,2,256]{2,1,0:T(2,128)S(1)}, f32[512,2,256]{2,1,0:T(2,128)S(1)}, u32[]{:S(2)}, u32[]{:S(2)}) collective-permute-start(f32[512,2,256]{2,1,0:T(2,128)S(1)} %add.450), channel_id=1, source_target_pairs={{0,4},{2,6},{4,0},{6,2},{1,5},{3,7},{5,1},{7,3},{8,12},{10,14},{12... | collective-permute-start | bytes 3145736 | tf_op jit(solution)/shard_map/ppermute | solution.py:250
  164.5 17.6 %collective-permute-start.32 = (bf16[256,512]{1,0:T(8,128)(2,1)}, bf16[256,512]{1,0:T(8,128)(2,1)S(1)}, u32[]{:S(2)}, u32[]{:S(2)}) collective-permute-start(bf16[256,512]{1,0:T(8,128)(2,1)} %get-tuple-element.197), channel_id=1, source_target_pairs={{8,0},{16,24},{9,1},{17,25},{10,2},{18,26},{11,3},{19,27},{12,4},{... | collective-permute-start | bytes 786440 | tf_op jit(solution)/shard_map/ppermute | solution.py:265
  174.9 11.2 %collective-permute-start.36 = (bf16[256,512]{1,0:T(8,128)(2,1)S(1)}, bf16[256,512]{1,0:T(8,128)(2,1)S(1)}, u32[]{:S(2)}, u32[]{:S(2)}) collective-permute-start(bf16[256,512]{1,0:T(8,128)(2,1)S(1)} %get-tuple-element.196), channel_id=1, source_target_pairs={{8,0},{16,24},{9,1},{17,25},{10,2},{18,26},{11,3},{19,27},{12,4},{... | collective-permute-start | bytes 786440 | tf_op jit(solution)/shard_map/ppermute | solution.py:265
  176.2 14.9 %collective-permute-start.40 = (bf16[256,512]{1,0:T(8,128)(2,1)S(1)}, bf16[256,512]{1,0:T(8,128)(2,1)S(1)}, u32[]{:S(2)}, u32[]{:S(2)}) collective-permute-start(bf16[256,512]{1,0:T(8,128)(2,1)S(1)} %get-tuple-element.195), channel_id=1, source_target_pairs={{8,0},{16,24},{9,1},{17,25},{10,2},{18,26},{11,3},{19,27},{12,4},{... | collective-permute-start | bytes 786440 | tf_op jit(solution)/shard_map/ppermute | solution.py:265
  182.1 17.7 %collective-permute-start.29 = (bf16[128,2,256]{2,1,0:T(2,128)(2,1)S(1)}, bf16[128,2,256]{2,1,0:T(2,128)(2,1)S(1)}, u32[]{:S(2)}, u32[]{:S(2)}) collective-permute-start(bf16[128,2,256]{2,1,0:T(2,128)(2,1)S(1)} %get-tuple-element.139), channel_id=1, source_target_pairs={{0,1},{1,0},{2,3},{3,2},{4,5},{5,4},{6,7},{7,6},{8,9},{9,8},{10,11... | collective-permute-start | bytes 393224 | tf_op jit(solution)/shard_map/ppermute | solution.py:251
  186.2 14.3 %collective-permute-start.30 = (bf16[128,2,256]{2,1,0:T(2,128)(2,1)S(1)}, bf16[128,2,256]{2,1,0:T(2,128)(2,1)S(1)}, u32[]{:S(2)}, u32[]{:S(2)}) collective-permute-start(bf16[128,2,256]{2,1,0:T(2,128)(2,1)S(1)} %get-tuple-element.140), channel_id=1, source_target_pairs={{0,4},{2,6},{4,0},{6,2},{1,5},{3,7},{5,1},{7,3},{8,12},{10,14},{12... | collective-permute-start | bytes 393224 | tf_op jit(solution)/shard_map/ppermute | solution.py:250
  191.2 11.1 %collective-permute-start.31 = (bf16[128,2,256]{2,1,0:T(2,128)(2,1)S(1)}, bf16[128,2,256]{2,1,0:T(2,128)(2,1)S(1)}, u32[]{:S(2)}, u32[]{:S(2)}) collective-permute-start(bf16[128,2,256]{2,1,0:T(2,128)(2,1)S(1)} %get-tuple-element.141), channel_id=1, source_target_pairs={{0,5},{1,4},{2,7},{3,6},{4,1},{5,0},{6,3},{7,2},{8,13},{9,12},{10,... | collective-permute-start | bytes 393224 | tf_op jit(solution)/shard_map/ppermute | solution.py:252
  194.5 9.5 %collective-permute-start.33 = (bf16[128,2,256]{2,1,0:T(2,128)(2,1)S(1)}, bf16[128,2,256]{2,1,0:T(2,128)(2,1)S(1)}, u32[]{:S(2)}, u32[]{:S(2)}) collective-permute-start(bf16[128,2,256]{2,1,0:T(2,128)(2,1)S(1)} %get-tuple-element.148), channel_id=1, source_target_pairs={{0,1},{1,0},{2,3},{3,2},{4,5},{5,4},{6,7},{7,6},{8,9},{9,8},{10,11... | collective-permute-start | bytes 393224 | tf_op jit(solution)/shard_map/ppermute | solution.py:251
  196.0 8.6 %collective-permute-start.34 = (bf16[128,2,256]{2,1,0:T(2,128)(2,1)S(1)}, bf16[128,2,256]{2,1,0:T(2,128)(2,1)S(1)}, u32[]{:S(2)}, u32[]{:S(2)}) collective-permute-start(bf16[128,2,256]{2,1,0:T(2,128)(2,1)S(1)} %get-tuple-element.149), channel_id=1, source_target_pairs={{0,4},{2,6},{4,0},{6,2},{1,5},{3,7},{5,1},{7,3},{8,12},{10,14},{12... | collective-permute-start | bytes 393224 | tf_op jit(solution)/shard_map/ppermute | solution.py:250
  199.8 7.4 %collective-permute-start.35 = (bf16[128,2,256]{2,1,0:T(2,128)(2,1)S(1)}, bf16[128,2,256]{2,1,0:T(2,128)(2,1)S(1)}, u32[]{:S(2)}, u32[]{:S(2)}) collective-permute-start(bf16[128,2,256]{2,1,0:T(2,128)(2,1)S(1)} %get-tuple-element.150), channel_id=1, source_target_pairs={{0,5},{1,4},{2,7},{3,6},{4,1},{5,0},{6,3},{7,2},{8,13},{9,12},{10,... | collective-permute-start | bytes 393224 | tf_op jit(solution)/shard_map/ppermute | solution.py:252
  200.5 9.3 %collective-permute-start.37 = (bf16[128,2,256]{2,1,0:T(2,128)(2,1)S(1)}, bf16[128,2,256]{2,1,0:T(2,128)(2,1)S(1)}, u32[]{:S(2)}, u32[]{:S(2)}) collective-permute-start(bf16[128,2,256]{2,1,0:T(2,128)(2,1)S(1)} %get-tuple-element.157), channel_id=1, source_target_pairs={{0,1},{1,0},{2,3},{3,2},{4,5},{5,4},{6,7},{7,6},{8,9},{9,8},{10,11... | collective-permute-start | bytes 393224 | tf_op jit(solution)/shard_map/ppermute | solution.py:251
  202.2 9.2 %collective-permute-start.38 = (bf16[128,2,256]{2,1,0:T(2,128)(2,1)S(1)}, bf16[128,2,256]{2,1,0:T(2,128)(2,1)S(1)}, u32[]{:S(2)}, u32[]{:S(2)}) collective-permute-start(bf16[128,2,256]{2,1,0:T(2,128)(2,1)S(1)} %get-tuple-element.158), channel_id=1, source_target_pairs={{0,4},{2,6},{4,0},{6,2},{1,5},{3,7},{5,1},{7,3},{8,12},{10,14},{12... | collective-permute-start | bytes 393224 | tf_op jit(solution)/shard_map/ppermute | solution.py:250
  204.0 8.9 %collective-permute-start.39 = (bf16[128,2,256]{2,1,0:T(2,128)(2,1)S(1)}, bf16[128,2,256]{2,1,0:T(2,128)(2,1)S(1)}, u32[]{:S(2)}, u32[]{:S(2)}) collective-permute-start(bf16[128,2,256]{2,1,0:T(2,128)(2,1)S(1)} %get-tuple-element.159), channel_id=1, source_target_pairs={{0,5},{1,4},{2,7},{3,6},{4,1},{5,0},{6,3},{7,2},{8,13},{9,12},{10,... | collective-permute-start | bytes 393224 | tf_op jit(solution)/shard_map/ppermute | solution.py:252
  204.7 9.7 %collective-permute-start.41 = (bf16[128,2,256]{2,1,0:T(2,128)(2,1)S(1)}, bf16[128,2,256]{2,1,0:T(2,128)(2,1)S(1)}, u32[]{:S(2)}, u32[]{:S(2)}) collective-permute-start(bf16[128,2,256]{2,1,0:T(2,128)(2,1)S(1)} %get-tuple-element.166), channel_id=1, source_target_pairs={{0,1},{1,0},{2,3},{3,2},{4,5},{5,4},{6,7},{7,6},{8,9},{9,8},{10,11... | collective-permute-start | bytes 393224 | tf_op jit(solution)/shard_map/ppermute | solution.py:251
  207.2 7.3 %collective-permute-start.42 = (bf16[128,2,256]{2,1,0:T(2,128)(2,1)S(1)}, bf16[128,2,256]{2,1,0:T(2,128)(2,1)S(1)}, u32[]{:S(2)}, u32[]{:S(2)}) collective-permute-start(bf16[128,2,256]{2,1,0:T(2,128)(2,1)S(1)} %get-tuple-element.167), channel_id=1, source_target_pairs={{0,4},{2,6},{4,0},{6,2},{1,5},{3,7},{5,1},{7,3},{8,12},{10,14},{12... | collective-permute-start | bytes 393224 | tf_op jit(solution)/shard_map/ppermute | solution.py:250
  209.8 6.4 %collective-permute-start.43 = (bf16[128,2,256]{2,1,0:T(2,128)(2,1)S(1)}, bf16[128,2,256]{2,1,0:T(2,128)(2,1)S(1)}, u32[]{:S(2)}, u32[]{:S(2)}) collective-permute-start(bf16[128,2,256]{2,1,0:T(2,128)(2,1)S(1)} %get-tuple-element.168), channel_id=1, source_target_pairs={{0,5},{1,4},{2,7},{3,6},{4,1},{5,0},{6,3},{7,2},{8,13},{9,12},{10,... | collective-permute-start | bytes 393224 | tf_op jit(solution)/shard_map/ppermute | solution.py:252
  (14 other events, 59.1 us)
Sparse Core Ops, SparseCore 0:
  109.6 20.7 all-gather.1

commit v3 on v0

--- a/solution.py
+++ b/solution.py
@@ -1,6 +1,8 @@
 import jax
 import jax.numpy as jnp
 from jax import lax
+from jax.experimental import pallas as pl
+from jax.experimental.pallas import tpu as pltpu
 from jax.sharding import PartitionSpec as P
 
 SRC_ST = 2048
@@ -53,7 +55,7 @@
     return (term_real, term_imag)
 
 
-def shards(src_real, src_imag, rcv_real, rcv_imag, src_pos, rcv_pos, freqs):
+def shards_any(src_real, src_imag, rcv_real, rcv_imag, src_pos, rcv_pos, freqs):
     n_time = lax.axis_size("tm")
     n_recv = lax.axis_size("rcv")
     n_source = lax.axis_size("src")
@@ -104,7 +106,487 @@
     )
 
 
+FINE = 32
+CHUNKS = 2
+PLACE_Y, CORE, INNER, SAME, MINE, PLACE_X = range(6)
+VMEM = 48 * 1024 * 1024
+
+
+def waves(freq, slowness, positions):
+    angle = ((TWO_PI * freq) * slowness)[:, None] * positions[None, :]
+    return jnp.cos(angle), jnp.sin(angle)
+
+
+def tables(freq, starts, total, positions):
+    coarse = (2.0 * starts.astype(jnp.float32) + 1.0) / total - 1.0
+    fine = 2.0 * jnp.arange(FINE, dtype=jnp.float32) / total
+    return waves(freq, coarse, positions) + waves(freq, fine, positions)
+
+
+def nt(first, second):
+    return lax.dot_general(first, second, (((1,), (1,)), ((), ())), preferred_element_type=jnp.float32)
+
+
+def steered_kernel(sign, scale, n_parts, n_halves, flags, cos_c, sin_c, cos_f, sin_f, *refs):
+    parts, halves = refs[:n_parts], refs[n_parts : n_parts + n_halves]
+    outs, (steer, spectra) = refs[n_parts + n_halves : -2], refs[-2:]
+    step = pl.program_id(0)
+    group = cos_c.shape[0]
+    rows = group * FINE
+
+    @pl.when(step == 0)
+    def _():
+        first = 0
+        for part in parts:
+            spectra[:, first : first + part.shape[1]] = part[...]
+            first += part.shape[1]
+        for i, part in enumerate(halves):
+            count = part.shape[0] // 2
+            for t in range(2):
+                at = 2 * t * count + (flags[CORE] if i == 0 else 1 - flags[CORE]) * count
+                spectra[pl.ds(pl.multiple_of(at, count), count), first:] = part[t * count : (t + 1) * count, :]
+
+    for i in range(group):
+        cc, sc = cos_c[i : i + 1, :], sin_c[i : i + 1, :]
+        steer[i * FINE : (i + 1) * FINE, :] = (cc * cos_f[...] - sc * sin_f[...]).astype(jnp.bfloat16)
+        steer[rows + i * FINE : rows + (i + 1) * FINE, :] = (sc * cos_f[...] + cc * sin_f[...]).astype(
+            jnp.bfloat16
+        )
+    found = nt(steer[...], spectra[...])
+    half = found.shape[1] // 2
+    real = (found[:rows, :half] + found[rows:, half:]) * scale
+    imag = (found[:rows, half:] - found[rows:, :half]) * (sign * scale)
+    for k, out in enumerate(outs):
+
+        size = out.shape[0]
+        per = rows // size
+
+        @pl.when((step == k // per) | (len(outs) == 1))
+        def _(out=out, at=k % per * size):
+            if out.ndim == 2:
+                out[:, :half] = real[at : at + size].astype(out.dtype)
+                out[:, half:] = imag[at : at + size].astype(out.dtype)
+            else:
+                out[:, 0, :] = real.astype(out.dtype)
+                out[:, 1, :] = imag.astype(out.dtype)
+
+
+def steered(flags, table, parts, steps, halves=(), cuts=1, sign=1.0, scale=1.0, paired=False, joined=False):
+    coarse, depth = table[0].shape
+    wide = parts[0].shape[0]
+    group = coarse // steps
+    rows = group * FINE
+    whole = lambda v: pl.BlockSpec(v.shape, lambda i: (0, 0))
+    if paired:
+        shape, spec = jax.ShapeDtypeStruct((rows, 2, wide // 2), jnp.float32), pl.BlockSpec(
+            (rows, 2, wide // 2), lambda i: (0, 0, 0)
+        )
+    else:
+        shape, spec = jax.ShapeDtypeStruct((rows, wide), jnp.bfloat16), pl.BlockSpec((rows, wide), lambda i: (0, 0))
+    shapes, specs = [shape] * steps, [spec] * steps
+    if paired:
+        shapes[1:] = [jax.ShapeDtypeStruct(shape.shape, jnp.bfloat16)] * (steps - 1)
+    if cuts > 1:
+        shapes = [jax.ShapeDtypeStruct((rows // cuts, wide), jnp.bfloat16)] * (steps * cuts)
+        specs = [pl.BlockSpec((rows // cuts, wide), lambda i: (0, 0))] * (steps * cuts)
+    if joined:
+        shapes = jax.ShapeDtypeStruct((steps * rows, wide), jnp.bfloat16)
+        specs = pl.BlockSpec((rows, wide), lambda i: (i, 0))
+    return pl.pallas_call(
+        lambda *refs: steered_kernel(sign, scale, len(parts), len(halves), *refs),
+        grid=(steps,),
+        in_specs=[pl.BlockSpec(memory_space=pltpu.SMEM)]
+        + [pl.BlockSpec((group, depth), lambda i: (i, 0))] * 2
+        + [whole(v) for v in (*table[2:], *parts, *halves)],
+        out_specs=specs,
+        out_shape=shapes,
+        scratch_shapes=[pltpu.VMEM((2 * rows, depth), jnp.bfloat16), pltpu.VMEM((wide, depth), jnp.bfloat16)],
+        compiler_params=pltpu.CompilerParams(vmem_limit_bytes=VMEM),
+        cost_estimate=pl.CostEstimate(flops=1, bytes_accessed=1, transcendentals=0),
+    )(flags, *table, *parts, *halves)
+
+
+def focus_kernel(scale, flags, slots, others, receiver, out, real, imag, both):
+    n_z, rows, _ = slots.shape
+    half = rows // 2
+    wide = rows
+    part = receiver.shape[1]
+    q = 2 * part
+    for slot in range(n_z):
+        for v, at in ((slots, flags[PLACE_Y] * half), (others, (1 - flags[PLACE_Y]) * half)):
+            to = pl.ds(pl.multiple_of(slot * wide + at, half), half)
+            real[to, :] = v[slot, :half, :]
+            imag[to, :] = v[slot, half:, :]
+        for t in range(2):
+            for i in range(receiver.shape[0]):
+                row, col = t * q + i % 2 * part, slot * wide + i // 2 * half
+                both[row : row + part, col : col + half] = receiver[i, :, (2 * slot + t) * half : (2 * slot + t + 1) * half]
+    one = jnp.dot(both[...], real[...], preferred_element_type=jnp.float32)
+    two = jnp.dot(both[...], imag[...], preferred_element_type=jnp.float32)
+    out[:q, :] = ((one[:q] - two[q:]) * scale).astype(out.dtype)
+    out[q:, :] = ((one[q:] + two[:q]) * scale).astype(out.dtype)
+
+
+def focused(scale, flags, slots, others, receiver):
+    n_z, rows, stations = slots.shape
+    q = 2 * receiver.shape[1]
+    vmem = pl.BlockSpec(memory_space=pltpu.VMEM)
+    return pl.pallas_call(
+        lambda *refs: focus_kernel(scale, *refs),
+        out_shape=jax.ShapeDtypeStruct((2 * q, stations), jnp.bfloat16),
+        in_specs=[pl.BlockSpec(memory_space=pltpu.SMEM)] + [vmem] * 3,
+        out_specs=vmem,
+        scratch_shapes=[pltpu.VMEM((n_z * rows, stations), jnp.bfloat16)] * 2
+        + [pltpu.VMEM((2 * q, n_z * rows), jnp.bfloat16)],
+        compiler_params=pltpu.CompilerParams(vmem_limit_bytes=VMEM),
+        cost_estimate=pl.CostEstimate(flops=1, bytes_accessed=1, transcendentals=0),
+    )(flags, slots, others, receiver)
+
+
+def product_kernel(scale, flags, own, near, one, two, three, four, mine, other, *refs):
+    outs, both = refs[:-1], refs[-1]
+    rows = both.shape[0] // 2
+    wide = own.shape[1]
+    half = wide // 2
+    for slot, part in enumerate((own[...], near[...], one[...] + two[...], three[...] + four[...])):
+        at = slot * wide
+        real, imag = part[:, :half], part[:, half:]
+        both[:rows, at : at + half] = real
+        both[:rows, at + half : at + wide] = -imag
+        both[rows:, at : at + half] = imag
+        both[rows:, at + half : at + wide] = real
+    middle = rows // 2
+    same = flags[SAME] == 1
+    by_mine, by_other = nt(both[...], mine[...]) * scale, nt(both[...], other[...]) * scale
+    for total, one, two in (
+        (jnp.where(same, by_mine, by_other), outs[0], outs[2]),
+        (jnp.where(same, by_other, by_mine), outs[1], outs[3]),
+    ):
+        for t in range(2):
+            one[:, t, :] = total[t * rows : t * rows + middle].astype(one.dtype)
+            two[:, t, :] = total[t * rows + middle : (t + 1) * rows].astype(two.dtype)
+
+
+def product(scale, k, rows, flags, parts, mine, other):
+    shape = (rows // 2, 2, mine.shape[0])
+    return pl.pallas_call(
+        lambda *refs: product_kernel(scale, *refs),
+        grid=(1,),
+        out_shape=[jax.ShapeDtypeStruct(shape, kind) for kind in (jnp.float32,) + (jnp.bfloat16,) * 3],
+        in_specs=[pl.BlockSpec(memory_space=pltpu.SMEM)]
+        + [pl.BlockSpec((rows, v.shape[1]), lambda i: (k, 0)) for v in parts[:-1]]
+        + [pl.BlockSpec(v.shape, lambda i: (0, 0)) for v in (parts[-1], mine, other)],
+        out_specs=[pl.BlockSpec(shape, lambda i: (0, 0, 0))] * 4,
+        scratch_shapes=[pltpu.VMEM((2 * rows, mine.shape[1]), jnp.bfloat16)],
+        compiler_params=pltpu.CompilerParams(vmem_limit_bytes=VMEM),
+        cost_estimate=pl.CostEstimate(flops=1, bytes_accessed=1, transcendentals=0),
+    )(flags, *parts, mine, other)
+
+
+def arranged_kernel(flags, own, one, two, three, out):
+    inner = flags[INNER] == 1
+    second, third = jnp.where(inner, three[...], two[...]), jnp.where(inner, two[...], three[...])
+    wide = own.shape[1]
+    for slot, v in enumerate((own[...], one[...], second, third)):
+        if out.ndim == 3:
+            out[slot] = v
+        else:
+            out[:, slot * wide : (slot + 1) * wide] = v
+
+
+def arranged(flags, got, stacked):
+    rows, wide = got[0].shape
+    vmem = pl.BlockSpec(memory_space=pltpu.VMEM)
+    return pl.pallas_call(
+        arranged_kernel,
+        out_shape=jax.ShapeDtypeStruct((4, rows, wide) if stacked else (rows, 4 * wide), got[0].dtype),
+        in_specs=[pl.BlockSpec(memory_space=pltpu.SMEM)] + [vmem] * 4,
+        out_specs=vmem,
+        compiler_params=pltpu.CompilerParams(vmem_limit_bytes=VMEM),
+        cost_estimate=pl.CostEstimate(flops=1, bytes_accessed=1, transcendentals=0),
+    )(flags, *got)
+
+
+def fill_steering(steer, cos_c, sin_c, cos_f, sin_f, first, count):
+    for i in range(count):
+        cc, sc = cos_c[pl.ds(first + i, 1), :], sin_c[pl.ds(first + i, 1), :]
+        steer[i * FINE : (i + 1) * FINE, :] = (cc * cos_f[...] - sc * sin_f[...]).astype(steer.dtype)
+        steer[(count + i) * FINE : (count + i + 1) * FINE, :] = (sc * cos_f[...] + cc * sin_f[...]).astype(
+            steer.dtype
+        )
+
+
+def conjugated(steer, spectra):
+    found = nt(steer[...], spectra[...])
+    rows, half = found.shape[0] // 2, found.shape[1] // 2
+    return found[:rows, :half] + found[rows:, half:], found[rows:, :half] - found[:rows, half:]
+
+
+def receivers_kernel(flags, *refs):
+    tables, own, own_last, (given, other) = (refs[:4], refs[4:8]), refs[8:10], refs[10:12], refs[12:14]
+    outs, (steer, spectra, steer_last, spectra_last) = refs[14:-4], refs[-4:]
+    step = pl.program_id(0)
+
+    @pl.when(step == 0)
+    def _():
+        first = 0
+        for to, here in ((spectra, own), (spectra_last, own_last)):
+            b_block, count = here[0].shape[2], here[0].shape[1] // 2
+            to[: 2 * count, :b_block] = here[0][0]
+            to[2 * count :, :b_block] = here[1][0]
+            for t in range(2):
+                rows = slice(first + t * count, first + (t + 1) * count)
+                for part, place in ((given, flags[CORE]), (other, 1 - flags[CORE])):
+                    at = pl.multiple_of((2 * t + place) * count, count)
+                    to[pl.ds(at, count), b_block:] = part[rows, :]
+            first += 2 * count
+
+    coarse = tables[0][0].shape[0]
+    fill_steering(steer, *tables[0], 0, coarse)
+    real, imag = conjugated(steer, spectra)
+    coarse_last = tables[1][0].shape[0] // len(outs)
+    fill_steering(steer_last, *tables[1], step * coarse_last, coarse_last)
+    real_last, imag_last = conjugated(steer_last, spectra_last)
+    rows, wide = real.shape
+    half, part = real_last.shape[0] // 2, wide // 2
+    for k, out in enumerate(outs):
+
+        @pl.when(step == k)
+        def _(out=out):
+            out[:rows, :wide] = real.astype(out.dtype)
+            out[:rows, wide:] = imag.astype(out.dtype)
+            for i in range(2):
+                at = slice(i * half, (i + 1) * half)
+                out[rows:, 2 * i * part : (2 * i + 1) * part] = real_last[at].astype(out.dtype)
+                out[rows:, (2 * i + 1) * part : (2 * i + 2) * part] = imag_last[at].astype(out.dtype)
+
+
+def receivers_of(flags, table, table_last, real, imag, given, other):
+    planes = 4
+    bins, wide, b_block = real.shape
+    coarse, depth = table[0].shape
+    rows, rows_last = coarse * FINE // planes, table_last[0].shape[0] * FINE // planes
+    shape = jax.ShapeDtypeStruct((rows + rows_last // 2, 2 * wide), jnp.bfloat16)
+    whole = lambda v: pl.BlockSpec(v.shape, lambda i, f: (0, 0))
+    return pl.pallas_call(
+        receivers_kernel,
+        grid_spec=pltpu.PrefetchScalarGridSpec(
+            num_scalar_prefetch=1,
+            grid=(planes,),
+            in_specs=[pl.BlockSpec((coarse // planes, depth), lambda i, f: (i, 0))] * 2
+            + [whole(v) for v in (*table[2:], *table_last)]
+            + [pl.BlockSpec((1, wide, b_block), lambda i, f: (f[MINE], 0, 0))] * 2
+            + [pl.BlockSpec((1, wide // 2, b_block), lambda i, f: (bins - 1, f[PLACE_X], 0))] * 2
+            + [whole(given), whole(other)],
+            out_specs=[pl.BlockSpec(shape.shape, lambda i, f: (0, 0))] * planes,
+            scratch_shapes=[
+                pltpu.VMEM((2 * rows, depth), jnp.bfloat16),
+                pltpu.VMEM((2 * wide, depth), jnp.bfloat16),
+                pltpu.VMEM((2 * rows_last, depth), jnp.bfloat16),
+                pltpu.VMEM((wide, depth), jnp.bfloat16),
+            ],
+        ),
+        out_shape=[shape] * planes,
+        compiler_params=pltpu.CompilerParams(vmem_limit_bytes=VMEM),
+        cost_estimate=pl.CostEstimate(flops=1, bytes_accessed=1, transcendentals=0),
+    )(flags, *table, *table_last, real, imag, real, imag, given, other)
+
+
+def parted_kernel(flags, own, one, two, three, out, out_last):
+    inner = flags[INNER] == 1
+    second, third = jnp.where(inner, three[...], two[...]), jnp.where(inner, two[...], three[...])
+    wide, half, rows = own.shape[1], own.shape[1] // 2, out.shape[0]
+    rest = own.shape[0] - rows
+    for slot, v in enumerate((own[...], one[...], second, third)):
+        out[:, slot * wide : (slot + 1) * wide] = v[:rows]
+        for i in range(2):
+            out_last[i * rest : (i + 1) * rest, slot * half : (slot + 1) * half] = v[rows:, i * half : (i + 1) * half]
+
+
+def parted(flags, got, rows):
+    vmem = pl.BlockSpec(memory_space=pltpu.VMEM)
+    high, wide = got[0].shape
+    return pl.pallas_call(
+        parted_kernel,
+        out_shape=[
+            jax.ShapeDtypeStruct((rows, 4 * wide), jnp.bfloat16),
+            jax.ShapeDtypeStruct((2 * (high - rows), 2 * wide), jnp.bfloat16),
+        ],
+        in_specs=[pl.BlockSpec(memory_space=pltpu.SMEM)] + [vmem] * 4,
+        out_specs=[vmem] * 2,
+        compiler_params=pltpu.CompilerParams(vmem_limit_bytes=VMEM),
+        cost_estimate=pl.CostEstimate(flops=1, bytes_accessed=1, transcendentals=0),
+    )(flags, *got)
+
+
+def place_kernel(flags, *refs):
+    out, found = refs[-1], refs[-5:-1]
+    for d, part in enumerate(found):
+
+        @pl.when(pl.program_id(0) == d)
+        def _(part=part):
+            out[:, 0] = part[...].astype(out.dtype)
+
+
+def placed(flags, whole, shape, found, k):
+    rows = found[0].shape[0]
+    before = [] if whole is None else [whole]
+    return pl.pallas_call(
+        place_kernel,
+        grid_spec=pltpu.PrefetchScalarGridSpec(
+            num_scalar_prefetch=1,
+            grid=(4,),
+            in_specs=[pl.BlockSpec(memory_space=pl.ANY)] * len(before)
+            + [pl.BlockSpec(v.shape, lambda d, f: (0, 0, 0)) for v in found],
+            out_specs=pl.BlockSpec((rows, 1) + shape[2:], lambda d, f: (k, f[MINE] ^ d, 0, 0)),
+        ),
+        out_shape=jax.ShapeDtypeStruct(shape, jnp.float32),
+        input_output_aliases={1: 0} if before else {},
+        compiler_params=pltpu.CompilerParams(vmem_limit_bytes=VMEM),
+        cost_estimate=pl.CostEstimate(flops=1, bytes_accessed=1, transcendentals=0),
+    )(flags, *before, *found)
+
+
+def place_last_kernel(_, kept, given, out):
+    out[:, 0] = kept[...] + given[...].astype(jnp.float32)
+
+
+def placed_last(whole, kept, given):
+    last = whole.shape[1] - 1
+    block = pl.BlockSpec(given.shape, lambda i: (0, 0, 0))
+    return pl.pallas_call(
+        place_last_kernel,
+        grid=(1,),
+        in_specs=[pl.BlockSpec(memory_space=pl.ANY)] + [block] * 2,
+        out_specs=pl.BlockSpec((given.shape[0], 1) + given.shape[1:], lambda i: (0, last, 0, 0)),
+        out_shape=jax.ShapeDtypeStruct(whole.shape, jnp.float32),
+        input_output_aliases={0: 0},
+        compiler_params=pltpu.CompilerParams(vmem_limit_bytes=VMEM),
+        cost_estimate=pl.CostEstimate(flops=1, bytes_accessed=1, transcendentals=0),
+    )(whole, kept, given)
+
+
+def shards_plane(src_real, src_imag, rcv_real, rcv_imag, src_pos, rcv_pos, freqs):
+    n_z = lax.axis_size("tm")
+    bins, wide, a_block = src_real.shape
+    b_block = rcv_real.shape[2]
+    half = wide // 2
+    p_block = SRC_SL // lax.axis_size("src")
+    q_plane = RCV_SL // n_z
+    q_block = q_plane // 2
+    q_sub = q_block // lax.axis_size("src")
+    z, s, y = (lax.axis_index(name) for name in ("tm", "src", "rcv"))
+    x, c = s // 2, s % 2
+    mine = 2 * x + y
+    last = bins - 1
+    core = lambda v: lax.ppermute(v, "src", [(i, i ^ 1) for i in range(4)])
+    over_x = lambda v: lax.ppermute(v, "src", [(i, i ^ 2) for i in range(4)])
+    over_y = lambda v: lax.ppermute(v, "rcv", [(0, 1), (1, 0)])
+    over_xy = lambda v: lax.ppermute(v, ("src", "rcv"), [(i, i ^ 5) for i in range(8)])
+    over_z = lambda v, d: lax.ppermute(v, "tm", [(i, i ^ d) for i in range(n_z)])
+    ends = lambda v: lax.ppermute(v, "tm", [(1, 0), (2, 3)])
+    middle = lambda v: lax.ppermute(v, "tm", [(1, 2), (2, 1)])
+    flat = lambda v: v.reshape(-1, v.shape[-1])
+    take = lambda v, block, size: lax.dynamic_slice_in_dim(v, block * size, size)
+    turn = [freqs]
+
+    def after(v, *others):
+        return lax.optimization_barrier((v, others))[0]
+
+    def step(v):
+        v = after(v, turn[0])
+        turn[0] = v
+        return v
+
+    def bin_of(real, imag, which):
+        return flat(jnp.stack([lax.dynamic_index_in_dim(part, which, 0, False) for part in (real, imag)]))
+
+    def rows_of(which, first, count):
+        at, size = (which, first, 0), (1, count, b_block)
+        return jnp.concatenate([lax.dynamic_slice(v, at, size)[0] for v in (rcv_real, rcv_imag)], 0)
+
+    spread = lambda got: [got[0]] + [over_z(got[d], d) for d in range(1, n_z)]
+    inner = (z == 1) | (z == 2)
+    flags = jnp.stack([v.astype(jnp.int32) for v in (y, c, inner, c == y, mine, x)])
+
+    x_given = over_x(step(bin_of(src_real, src_imag, 2 * (1 - x) + y)))
+    y_given = [rows_of(2 * x + 1 - y, c * half, half), rows_of(last, x * half + c * (half // 2), half // 2)]
+    y_given = over_y(step(jnp.concatenate(y_given, 0)))
+    raw = lax.dynamic_slice_in_dim(jnp.stack([src_real[last], src_imag[last]]), y * half, half, 1)
+    raw = spread([step(flat(raw))] * n_z)
+    x_own = step(bin_of(src_real, src_imag, mine))
+    x_other = core(x_own)
+
+    at_src = jnp.concatenate([take(src_pos, block, a_block) for block in (s, s ^ 2, s ^ 1, s ^ 3)])
+    at_rcv = jnp.concatenate([take(rcv_pos, block, b_block) for block in (y, 1 - y)])
+    f_mine, f_last = lax.dynamic_index_in_dim(freqs, mine, 0, False), freqs[last]
+    chunk = p_block // CHUNKS
+    here, there = s * p_block, (s ^ 2) * p_block
+    n = jnp.arange(2 * p_block // FINE, dtype=jnp.int32) * FINE
+    starts = jnp.where(n // chunk % 2 == 0, here, there) + n // (2 * chunk) * chunk + n % chunk
+    x_other = step(x_other)
+    t_source = step(tables(f_mine, starts, SRC_SL, at_src))
+    x_given = step(x_given)
+    x_cross = core(x_given)
+    n = jnp.arange(n_z * q_block // FINE, dtype=jnp.int32) * FINE
+    t_receiver = tables(f_mine, (z ^ n // q_block) * q_plane + c * q_block + n % q_block, RCV_SL, at_rcv)
+    q_half = q_block // 2
+    n = jnp.arange(n_z * q_half // FINE, dtype=jnp.int32) * FINE
+    starts = (z ^ n // q_half) * q_plane + y * q_block + c * q_half + n % q_half
+    t_receiver_last = tables(f_last, starts, RCV_SL, at_rcv)
+    n = jnp.arange(2 * p_block // FINE, dtype=jnp.int32) * FINE
+    starts = jnp.where(n < p_block, here, there) + n % p_block
+    at_cores = jnp.concatenate([take(src_pos, block, a_block) for block in (s, s ^ 1)])
+    t_source_last = tables(f_last, starts, SRC_SL, at_cores)
+    t_receiver, t_receiver_last, t_source_last = step((t_receiver, t_receiver_last, t_source_last))
+    y_given = step(y_given)
+    y_other = core(y_given)
+    x_cross, raw = step((x_cross, raw))
+    raw = step(arranged(flags, raw, True))
+    other_raw = over_y(raw)
+    pieces = step(steered(flags, t_source, [x_own, x_given, x_other, x_cross], 4, joined=True))
+    near, one = over_z(pieces, 1), middle(pieces)
+    y_other = step(y_other)
+    yr = receivers_of(flags, t_receiver, t_receiver_last, rcv_real, rcv_imag, y_given, y_other)
+    yr, other_raw = step((yr, other_raw))
+    yr = spread(yr)
+    near, one, yr = step((near, one, yr))
+
+    two, three = middle(near), ends(one)
+    yr_mine, yr_last = step(parted(flags, yr, q_block))
+    yr_other = core(yr_mine)
+    yr_last = lax.all_gather(yr_last, "src", axis=0)
+    focus_scale = 1.0 / float(wide * n_z * RCV_ST) ** 0.5
+    beam_scale = 1.0 / float(SRC_ST) ** 0.5
+    yr_last = step(yr_last)
+    focus = step(focused(focus_scale, flags, raw, other_raw, yr_last))
+    focus = step([focus, core(focus)])
+    kept, given = step(steered(flags, t_source_last, focus, 2, scale=beam_scale, paired=True))
+    two, three, yr_other = step((two, three, yr_other))
+    given = over_x(given)
+    four = [ends(two[k * 2 * chunk : (k + 1) * 2 * chunk]) for k in range(CHUNKS)]
+
+    shape = (p_block, bins, 2, q_block)
+    four[0] = step(four[0])
+    parts = [pieces, near, one, three, two]
+    scale = focus_scale * beam_scale
+    share = lambda found: [found[0], over_y(found[1]), over_x(found[2]), over_xy(found[3])]
+    found = step(product(scale, 0, 2 * chunk, flags, [*parts, four[0]], yr_mine, yr_other))
+    found = share(found)
+    four[1] = step(four[1])
+    later = step(product(scale, 1, 2 * chunk, flags, [*parts, four[1]], yr_mine, yr_other))
+    found = step(found)
+    later = share(later)
+    whole = step(placed(flags, None, shape, found, 0))
+    given = step(given)
+    whole = step(placed_last(whole, kept, given))
+    later = step(later)
+    return placed(flags, whole, shape, later, 1).transpose(0, 2, 1, 3)
+
+
 def solution(mesh):
+    plane = (mesh.shape["tm"], mesh.shape["src"], mesh.shape["rcv"]) == (4, 4, 2)
+    shards = shards_plane if plane else shards_any
     in_specs = (
         P(None, "tm", "src"),
         P(None, "tm", "src"),

time: 1200 us -> 202 us (0.17)
  waiting for transfers between devices: 638 us -> 88.1 us
  matrix products: 355 us -> 0 us
  other arithmetic: 157 us -> 10.5 us
  Pallas kernels: 0 us -> 40.6 us
  starting transfers between devices: 0.46 us -> 33.5 us
  local copies, waits for them, and re-layouts: 26.3 us -> 12.4 us
    reduce_scatter x3 -> x0, waiting for transfers between devices: 501 us -> none  [the longest x1 178 us: shards(): lax.psum_scatter(part_real, 'tm', scatter_dimension=2, tiled=True)]
    dot_general x10 -> x0, matrix products: 355 us -> none  [mixed(): return jnp.einsum(form, first, second, preferred_element_type=jnp.float32)]
    dot_general x4 -> x0, other arithmetic: 143 us -> none  [mixed(): return jnp.einsum(form, first, second, preferred_element_type=jnp.float32)]
    all_gather x2 -> x1, waiting for transfers between devices: 137 us -> 16.6 us  [shards_plane(): yr_last = lax.all_gather(yr_last, 'src', axis=0)]
    ppermute x0 -> x27, waiting for transfers between devices: none -> 71.5 us  [the longest x7 31.6 us: shards_plane(): lax.ppermute(v, 'tm', [(i, i ^ d) for i in range(n_z)])]
    pallas_call x0 -> x11, Pallas kernels: none -> 40.6 us  [the longest x2 11.1 us: steered(): pl.pallas_call(lambda *refs: steered_kernel(sign, scale, len(parts), len(...]
    ppermute x0 -> x27, starting transfers between devices: none -> 33.5 us  [the longest x7 14.1 us: shards_plane(): lax.ppermute(v, 'tm', [(i, i ^ d) for i in range(n_z)])]
  transfers between devices with their start and end apart: 5 -> 28, of which waited for: 4 -> 13; matrix products, arithmetic and copies ran while one was open for 15% -> 5% of each run, Pallas kernels for 0% -> 18%
where the time goes in v3:
time: 202 us
  waiting for transfers between devices  88.1 us (44%)
  Pallas kernels  40.6 us (20%)
  starting transfers between devices  33.5 us (17%)
  between operations  16.4 us (8%)
  local copies, waits for them, and re-layouts  12.4 us (6%)
  other arithmetic  10.5 us (5%)
    ppermute x7, waiting for transfers between devices, shards_plane(): lax.ppermute(v, 'tm', [(i, i ^ d) for i in range(n_z)])  31.6 us
    ppermute x4, waiting for transfers between devices, shards_plane(): over_y = lambda v: lax.ppermute(v, 'rcv', [(0, 1), (1, 0)])  18.8 us
    all_gather x1, waiting for transfers between devices, shards_plane(): yr_last = lax.all_gather(yr_last, 'src', axis=0)  16.6 us
    ppermute x3, waiting for transfers between devices, shards_plane(): ends = lambda v: lax.ppermute(v, 'tm', [(1, 0), (2, 3)])  15.8 us
    ppermute x7, starting transfers between devices, shards_plane(): lax.ppermute(v, 'tm', [(i, i ^ d) for i in range(n_z)])  14.1 us
    pallas_call x2, Pallas kernels, steered(): pl.pallas_call(lambda *refs: steered_kernel(sign, scale, len(parts), len(...  11.1 us
    pallas_call x2, Pallas kernels, product(): pl.pallas_call(lambda *refs: product_kernel(scale, *refs), grid=(1,), out...  9.99 us
    pallas_call x1, Pallas kernels, receivers_of(): pl.pallas_call(receivers_kernel, grid_spec=pltpu.PrefetchScalarGridSpec(n...  9.11 us
  transfers between devices with their start and end apart: 28, of which 13 were waited for; matrix products, arithmetic and copies ran while one was open for 5% of the time, Pallas kernels for 18%

profile of v3, /device:TPU:0, one launch (start us, length us, event | category | flops | bytes accessed | tf_op | source)
XLA Modules:
  0.0 201.5 jit_solution(401713277245848558)
XLA Ops:
  6.5 1.4 constant_dynamic-slice_fusion
  8.8 1.0 dynamic-slice_bitcast_fusion.2
  9.8 1.1 dynamic-slice_bitcast_fusion
  11.9 5.1 %collective-permute-start.5 = (bf16[256,512]{1,0:T(8,128)(2,1)S(1)}, bf16[256,512]{1,0:T(8,128)(2,1)S(1)}, u32[]{:S(2)}, u32[]{:S(2)}) collective-permute-start(bf16[256,512]{1,0:T(8,128)(2,1)S(1)} %bitcast.25), channel_id=1, source_target_pairs={{0,24},{8,16},{16,8},{24,0},{1,25},{9,17},{17,9},{25,1},{2,26},{10... | collective-permute-start | bytes 786440 | tf_op jit(solution)/shard_map/ppermute | solution.py:486
  17.6 1.6 collective-permute-start.1
  23.0 5.6 %multiply_sine_fusion = (f32[32,2048]{1,0:T(8,128)S(1)}, f32[32,2048]{1,0:T(8,128)}, f32[32,2048]{1,0:T(8,128)}, f32[32,2048]{1,0:T(8,128)}, f32[32,2048]{1,0:T(...) fusion(f32[32]{0:T(128)S(1)} %get-tuple-element.236, ...), kind=kLoop, calls=%fused_computation.5 | loop fusion | flops 327680 | bytes 2638336 | tf_op jit(solution)/shard_map/sin | solution.py:117
  28.6 1.6 collective-permute-start.6
  31.0 1.2 multiply_sine_fusion.7
  32.3 1.8 multiply_sine_fusion.5
  34.0 14.8 %collective-permute-done.6.refs_12_ = bf16[384,1024]{1,0:T(8,128)(2,1)} collective-permute-done((bf16[384,1024]{1,0:T(8,128)(2,1)}, bf16[384,1024]{1,0:T(8,128)(2,1)}, u32[]{:S(2)}, u32[]{:S(2)}) %collective-permute-start.6) | collective-permute-done | bytes 786464 | tf_op jit(solution)/shard_map/ppermute | solution.py:484
  48.9 1.1 shard_map.74.refs_1_
  50.1 1.6 collective-permute-start.10
  51.7 1.0 copy-done.13
  52.7 1.0 copy-done.15
  53.7 6.5 %shard_map.73.refs_1_ = bf16[1024,512]{1,0:T(8,128)(2,1)S(1)} custom-call(s32[6]{0:T(128)S(1)} %stack.48.refs_0_.flags, f32[32,2048]{1,0:T(8,128)S(1)} %get-tuple-element.100.refs_1_, f32[32,2048]{1,0:T(8,128)S(1)} %get-tuple-element.101.refs_2_, f32[32,2048]{1,0:T(8,128)S(1)} %get-tuple-element.102.refs_3_, f32[32,2048]{1,0:T(8,128)S(1)} %get-tuple-element.103.refs_4_, ...), custom_call_target="tpu_custom_call" | custom-call | flops 1 | bytes 1 | tf_op jit(solution)/shard_map/pallas_call | solution.py:195
  61.0 4.0 %collective-permute-start.7 = (bf16[1024,512]{1,0:T(8,128)(2,1)S(1)}, bf16[1024,512]{1,0:T(8,128)(2,1)S(1)}, u32[]{:S(2)}, u32[]{:S(2)}) collective-permute-start(bf16[1024,512]{1,0:T(8,128)(2,1)S(1)} %shard_map.73.refs_1_), channel_id=1, source_target_pairs={{0,8},{8,0},{16,24},{24,16},{1,9},{9,1},{17,25},{25,17},{2,10},{10... | collective-permute-start | bytes 3145736 | tf_op jit(solution)/shard_map/ppermute | solution.py:486
  65.0 9.1 %shard_map.75 = (bf16[320,512]{1,0:T(8,128)(2,1)S(1)}, bf16[320,512]{1,0:T(8,128)(2,1)S(1)}, bf16[320,512]{1,0:T(8,128)(2,1)S(1)}, bf16[320,512]{1,0:T(8,128)(2,1)S(1)}) custom-call(s32[6]{0:T(128)S(1)} %stack.48.refs_0_.flags, f32[32,2048]{1,0:T(8,128)S(1)} %copy-done.6, f32[32,2048]{1,0:T(8,128)S(1)} %copy-done.7, f32[32,2048]{1,0:T(8,128)S(1)} %copy-done.4, ...), custom_call_target="tpu_custom_call" | custom-call | flops 1 | bytes 1 | tf_op jit(solution)/shard_map/pallas_call | solution.py:371
  74.9 1.2 collective-permute-start.11
  76.1 2.9 %collective-permute-start.12 = (bf16[320,512]{1,0:T(8,128)(2,1)S(1)}, bf16[320,512]{1,0:T(8,128)(2,1)S(1)}, u32[]{:S(2)}, u32[]{:S(2)}) collective-permute-start(bf16[320,512]{1,0:T(8,128)(2,1)S(1)} %get-tuple-element.132), channel_id=1, source_target_pairs={{0,16},{8,24},{16,0},{24,8},{1,17},{9,25},{17,1},{25,9},{2,18},{10... | collective-permute-start | bytes 983048 | tf_op jit(solution)/shard_map/ppermute | solution.py:486
  79.3 16.6 %collective-permute-done.7.refs_2_ = bf16[1024,512]{1,0:T(8,128)(2,1)S(1)} collective-permute-done((bf16[1024,512]{1,0:T(8,128)(2,1)S(1)}, bf16[1024,512]{1,0:T(8,128)(2,1)S(1)}, u32[]{:S(2)}, u32[]{:S(2)}) %collective-permute-start.7) | collective-permute-done | bytes 1048608 | tf_op jit(solution)/shard_map/ppermute | solution.py:486
  95.9 6.6 %collective-permute-done.11.one = bf16[320,512]{1,0:T(8,128)(2,1)S(1)} collective-permute-done((bf16[320,512]{1,0:T(8,128)(2,1)S(1)}, bf16[320,512]{1,0:T(8,128)(2,1)S(1)}, u32[]{:S(2)}, u32[]{:S(2)}) %collective-permute-start.11) | collective-permute-done | bytes 327712 | tf_op jit(solution)/shard_map/ppermute | solution.py:486
  102.5 8.3 %collective-permute-done.13.three = bf16[320,512]{1,0:T(8,128)(2,1)S(1)} collective-permute-done((bf16[320,512]{1,0:T(8,128)(2,1)S(1)}, bf16[320,512]{1,0:T(8,128)(2,1)S(1)}, u32[]{:S(2)}, u32[]{:S(2)}) %collective-permute-start.13) | collective-permute-done | bytes 327712 | tf_op jit(solution)/shard_map/ppermute | solution.py:486
  110.8 1.3 shard_map.76
  112.2 1.0 copy-done
  113.1 1.7 collective-permute-start.14
  114.8 1.5 collective-permute-start.15
  116.4 16.6 %all-gather.3.cloned.1.call-done = bf16[512,1024]{1,0:T(8,128)(2,1)} async-done(((bf16[128,1024]{1,0:T(8,128)(2,1)}), bf16[512,1024]{1,0:T(8,128)(2,1)}) %all-gather.3.cloned.1.call-update) | async-done | bytes 1048592 | tf_op jit(solution)/shard_map/all_gather | solution.py:558
  132.9 1.2 copy-done.2
  134.2 1.2 copy-done.9
  135.4 1.2 copy-done.10
  136.6 1.9 shard_map.77.refs_5_
  138.8 1.7 collective-permute-done.17.refs_6_
  140.5 4.6 %shard_map.78 = (f32[512,2,256]{2,1,0:T(2,128)S(1)}, bf16[512,2,256]{2,1,0:T(2,128)(2,1)S(1)}) custom-call(s32[6]{0:T(128)S(1)} %stack.48.refs_0_.flags, f32[32,1024]{1,0:T(8,128)S(1)} %copy-done.18, f32[32,1024]{1,0:T(8,128)S(1)} %copy-done.19, f32[32,1024]{1,0:T(8,128)S(1)} %copy-done.17, f32[32,1024]{1,0:T(8,128)S(1)} %copy-done.16, ...), custom_call_target="tpu_custom_call" | custom-call | flops 1 | bytes 1 | tf_op jit(solution)/shard_map/pallas_call | solution.py:195
  145.1 1.8 collective-permute-done.15.refs_4_
  146.9 1.3 fusion.8
  148.2 1.3 collective-permute-start.18
  149.5 1.3 collective-permute-start.22
  151.4 13.5 %collective-permute-done.18.refs_6_ = bf16[512,512]{1,0:T(8,128)(2,1)S(1)} collective-permute-done((bf16[512,512]{1,0:T(8,128)(2,1)S(1)}, bf16[512,512]{1,0:T(8,128)(2,1)S(1)}, u32[]{:S(2)}, u32[]{:S(2)}) %collective-permute-start.18) | collective-permute-done | bytes 524320 | tf_op jit(solution)/shard_map/ppermute | solution.py:487
  165.0 5.0 %shard_map.79 = (f32[256,2,256]{2,1,0:T(2,128)S(1)}, bf16[256,2,256]{2,1,0:T(2,128)(2,1)S(1)}, bf16[256,2,256]{2,1,0:T(2,128)(2,1)S(1)}, bf16[256,2,256]{2,1,0:T(2,128)(2,1)S(1)}) custom-call(s32[6]{0:T(128)S(1)} %stack.48.refs_0_.flags, bf16[1024,512]{1,0:T(8,128)(2,1)S(1)} %shard_map.73.refs_1_, bf16[1024,512]{1,0:T(8,128)(2,1)S(1)} %collective-permute-done.7.refs_2_, ...), custom_call_target="tpu_custom_call" | custom-call | flops 1 | bytes 1 | tf_op jit(solution)/shard_map/pallas_call | solution.py:272
  170.9 2.7 %collective-permute-start.21 = (bf16[256,2,256]{2,1,0:T(2,128)(2,1)S(1)}, bf16[256,2,256]{2,1,0:T(2,128)(2,1)S(1)}, u32[]{:S(2)}, u32[]{:S(2)}) collective-permute-start(bf16[256,2,256]{2,1,0:T(2,128)(2,1)S(1)} %get-tuple-element.164), channel_id=1, source_target_pairs={{0,5},{1,4},{2,7},{3,6},{4,1},{5,0},{6,3},{7,2},{8,13},{9,12},{10,... | collective-permute-start | bytes 786440 | tf_op jit(solution)/shard_map/ppermute | solution.py:485
  174.0 5.0 %shard_map.80 = (f32[256,2,256]{2,1,0:T(2,128)S(1)}, bf16[256,2,256]{2,1,0:T(2,128)(2,1)S(1)}, bf16[256,2,256]{2,1,0:T(2,128)(2,1)S(1)}, bf16[256,2,256]{2,1,0:T(2,128)(2,1)S(1)}) custom-call(s32[6]{0:T(128)S(1)} %stack.48.refs_0_.flags, bf16[1024,512]{1,0:T(8,128)(2,1)S(1)} %shard_map.73.refs_1_, bf16[1024,512]{1,0:T(8,128)(2,1)S(1)} %collective-permute-done.7.refs_2_, ...), custom_call_target="tpu_custom_call" | custom-call | flops 1 | bytes 1 | tf_op jit(solution)/shard_map/pallas_call | solution.py:272
  179.0 1.2 collective-permute-start.24
  180.7 1.8 collective-permute-start.26
  182.6 2.4 %shard_map.81._ = f32[512,5,2,256]{3,2,1,0:T(2,128)} custom-call(s32[6]{0:T(128)S(1)} %stack.48.refs_0_.flags, f32[256,2,256]{2,1,0:T(2,128)S(1)} %get-tuple-element.174.refs_0_, bf16[256,2,256]{2,1,0:T(2,128)(2,1)S(1)} %collective-permute-done.19.refs_1_, bf16[256,2,256]{2,1,0:T(2,128)(2,1)S(1)} %collective-permute-done.20.refs_2_, ...), custom_call_target="tpu_custom_call" | custom-call | flops 1 | bytes 1 | tf_op jit(solution)/shard_map/pallas_call | solution.py:434
  185.0 1.2 shard_map.82.refs_0_
  186.2 3.2 %collective-permute-done.24.refs_2_ = bf16[256,2,256]{2,1,0:T(2,128)(2,1)S(1)} collective-permute-done((bf16[256,2,256]{2,1,0:T(2,128)(2,1)S(1)}, bf16[256,2,256]{2,1,0:T(2,128)(2,1)S(1)}, u32[]{:S(2)}, u32[]{:S(2)}) %collective-permute-start.24) | collective-permute-done | bytes 262176 | tf_op jit(solution)/shard_map/ppermute | solution.py:484
  189.4 2.8 %collective-permute-done.26.refs_4_ = bf16[256,2,256]{2,1,0:T(2,128)(2,1)S(1)} collective-permute-done((bf16[256,2,256]{2,1,0:T(2,128)(2,1)S(1)}, bf16[256,2,256]{2,1,0:T(2,128)(2,1)S(1)}, u32[]{:S(2)}, u32[]{:S(2)}) %collective-permute-start.26) | collective-permute-done | bytes 262176 | tf_op jit(solution)/shard_map/ppermute | solution.py:485
  192.3 2.4 %shard_map.83 = f32[512,5,2,256]{3,2,1,0:T(2,128)} custom-call(s32[6]{0:T(128)S(1)} %stack.48.refs_0_.flags, f32[512,5,2,256]{3,2,1,0:T(2,128)} %shard_map.82.refs_0_, f32[256,2,256]{2,1,0:T(2,128)S(1)} %get-tuple-element.181.refs_1_, bf16[256,2,256]{2,1,0:T(2,128)(2,1)S(1)} %collective-permute-done.24.refs_2_, ...), custom_call_target="tpu_custom_call", output_to_operand_aliasing={{}: (1, {})} | custom-call | flops 1 | bytes 1 | tf_op jit(solution)/shard_map/pallas_call | solution.py:434
  (87 shorter events, 9.1 us)
Async XLA Ops:
  6.5 126.4 %all-gather.3.cloned.1.call-start = ((), (), s32[]{:S(2)}) async-start(), calls=%async_computation | async-start | bytes 1310720 | tf_op jit(solution)/shard_map/all_gather | solution.py:558
  10.9 8.5 %copy-start.22 = (f32[5]{0:T(128)S(1)}, f32[5]{0:T(128)}, u32[]{:S(2)}) copy-start(f32[5]{0:T(128)} %param.13) | copy-start | bytes 64
  10.9 11.9 %copy-start.20 = (f32[2048]{0:T(1024)S(1)}, f32[2048]{0:T(1024)}, u32[]{:S(2)}) copy-start(f32[2048]{0:T(1024)} %param.12) | copy-start | bytes 24580
  10.9 11.9 %copy-start.21 = (f32[2048]{0:T(1024)S(1)}, f32[2048]{0:T(1024)}, u32[]{:S(2)}) copy-start(f32[2048]{0:T(1024)} %param.11) | copy-start | bytes 24580
  11.9 37.0 %collective-permute-start.5 = (bf16[256,512]{1,0:T(8,128)(2,1)S(1)}, bf16[256,512]{1,0:T(8,128)(2,1)S(1)}, u32[]{:S(2)}, u32[]{:S(2)}) collective-permute-start(bf16[256,512]{1,0:T(8,128)(2,1)S(1)} %bitcast.25), channel_id=1, source_target_pairs={{0,24},{8,16},{16,8},{24,0},{1,25},{9,17},{17,9},{25,1},{2,26},{10... | collective-permute-start | bytes 786440 | tf_op jit(solution)/shard_map/ppermute | solution.py:486
  17.0 31.9 %collective-permute-start.4 = (bf16[256,512]{1,0:T(8,128)(2,1)S(1)}, bf16[256,512]{1,0:T(8,128)(2,1)}, u32[]{:S(2)}, u32[]{:S(2)}) collective-permute-start(bf16[256,512]{1,0:T(8,128)(2,1)S(1)} %bitcast.26), channel_id=1, source_target_pairs={{0,16},{8,24},{16,0},{24,8},{1,17},{9,25},{17,1},{25,9},{2,18},{10... | collective-permute-start | bytes 786440 | tf_op jit(solution)/shard_map/ppermute | solution.py:486
  17.0 31.9 %collective-permute-start.3 = (bf16[256,512]{1,0:T(8,128)(2,1)S(1)}, bf16[256,512]{1,0:T(8,128)(2,1)}, u32[]{:S(2)}, u32[]{:S(2)}) collective-permute-start(bf16[256,512]{1,0:T(8,128)(2,1)S(1)} %bitcast.27), channel_id=1, source_target_pairs={{0,8},{8,0},{16,24},{24,16},{1,9},{9,1},{17,25},{25,17},{2,10},{10... | collective-permute-start | bytes 786440 | tf_op jit(solution)/shard_map/ppermute | solution.py:486
  17.6 13.3 %collective-permute-start.1 = (bf16[512,512]{1,0:T(8,128)(2,1)}, bf16[512,512]{1,0:T(8,128)(2,1)S(1)}, u32[]{:S(2)}, u32[]{:S(2)}) collective-permute-start(bf16[512,512]{1,0:T(8,128)(2,1)} %bitcast.14), channel_id=1, source_target_pairs={{0,4},{2,6},{4,0},{6,2},{1,5},{3,7},{5,1},{7,3},{8,12},{10,14},{12... | collective-permute-start | bytes 1572872 | tf_op jit(solution)/shard_map/ppermute | solution.py:483
  19.3 9.2 %collective-permute-start = (bf16[512,512]{1,0:T(8,128)(2,1)S(1)}, bf16[512,512]{1,0:T(8,128)(2,1)S(1)}, u32[]{:S(2)}, u32[]{:S(2)}) collective-permute-start(bf16[512,512]{1,0:T(8,128)(2,1)S(1)} %bitcast.23), channel_id=1, source_target_pairs={{0,2},{2,0},{4,6},{6,4},{1,3},{3,1},{5,7},{7,5},{8,10},{10,8},{12,... | collective-permute-start | bytes 1572872 | tf_op jit(solution)/shard_map/ppermute | solution.py:482
  28.6 23.1 %copy-start.14 = (bf16[512,512]{1,0:T(8,128)(2,1)}, bf16[512,512]{1,0:T(8,128)(2,1)S(1)}, u32[]{:S(2)}) copy-start(bf16[512,512]{1,0:T(8,128)(2,1)S(1)} %collective-permute-done.refs_7_) | copy-start | bytes 1572868
  28.6 20.3 %collective-permute-start.6 = (bf16[384,1024]{1,0:T(8,128)(2,1)}, bf16[384,1024]{1,0:T(8,128)(2,1)}, u32[]{:S(2)}, u32[]{:S(2)}) collective-permute-start(bf16[384,1024]{1,0:T(8,128)(2,1)} %pad_maximum_fusion), channel_id=1, source_target_pairs={{0,1},{1,0},{2,3},{3,2},{4,5},{5,4},{6,7},{7,6},{8,9},{9,8},{10,11... | collective-permute-start | bytes 2359304 | tf_op jit(solution)/shard_map/ppermute | solution.py:484
  31.0 20.7 %copy-start.12 = (bf16[512,512]{1,0:T(8,128)(2,1)}, bf16[512,512]{1,0:T(8,128)(2,1)S(1)}, u32[]{:S(2)}) copy-start(bf16[512,512]{1,0:T(8,128)(2,1)S(1)} %collective-permute-done.1.refs_6_) | copy-start | bytes 1572868
  31.0 17.9 %collective-permute-start.2 = (bf16[512,512]{1,0:T(8,128)(2,1)S(1)}, bf16[512,512]{1,0:T(8,128)(2,1)}, u32[]{:S(2)}, u32[]{:S(2)}) collective-permute-start(bf16[512,512]{1,0:T(8,128)(2,1)S(1)} %collective-permute-done.1.refs_6_), channel_id=1, source_target_pairs={{0,2},{2,0},{4,6},{6,4},{1,3},{3,1},{5,7},{7,5},{8,10},{10,8},{12,... | collective-permute-start | bytes 1572872 | tf_op jit(solution)/shard_map/ppermute | solution.py:482
  50.0 10.2 %copy-start.1 = (bf16[4,256,512]{2,1,0:T(8,128)(2,1)}, bf16[4,256,512]{2,1,0:T(8,128)(2,1)S(1)}, u32[]{:S(2)}) copy-start(bf16[4,256,512]{2,1,0:T(8,128)(2,1)S(1)} %shard_map.74.refs_1_) | copy-start | bytes 3145732
  50.0 14.9 %copy-start.3 = (f32[32,2048]{1,0:T(8,128)S(1)}, f32[32,2048]{1,0:T(8,128)}, u32[]{:S(2)}) copy-start(f32[32,2048]{1,0:T(8,128)} %get-tuple-element.111.refs_6_) | copy-start | bytes 786436
  50.0 14.9 %copy-start.4 = (f32[32,2048]{1,0:T(8,128)S(1)}, f32[32,2048]{1,0:T(8,128)}, u32[]{:S(2)}) copy-start(f32[32,2048]{1,0:T(8,128)} %get-tuple-element.107.refs_2_) | copy-start | bytes 786436
  50.0 14.9 %copy-start.5 = (f32[32,2048]{1,0:T(8,128)S(1)}, f32[32,2048]{1,0:T(8,128)}, u32[]{:S(2)}) copy-start(f32[32,2048]{1,0:T(8,128)} %get-tuple-element.108.refs_3_) | copy-start | bytes 786436
  50.0 14.9 %copy-start.6 = (f32[32,2048]{1,0:T(8,128)S(1)}, f32[32,2048]{1,0:T(8,128)}, u32[]{:S(2)}) copy-start(f32[32,2048]{1,0:T(8,128)} %get-tuple-element.105.refs_0_) | copy-start | bytes 786436
  50.0 14.9 %copy-start.7 = (f32[32,2048]{1,0:T(8,128)S(1)}, f32[32,2048]{1,0:T(8,128)}, u32[]{:S(2)}) copy-start(f32[32,2048]{1,0:T(8,128)} %get-tuple-element.106.refs_1_) | copy-start | bytes 786436
  50.1 14.9 %copy-start.11 = (f32[16,2048]{1,0:T(8,128)S(1)}, f32[16,2048]{1,0:T(8,128)}, u32[]{:S(2)}) copy-start(f32[16,2048]{1,0:T(8,128)} %get-tuple-element.109.refs_4_) | copy-start | bytes 393220
  50.1 24.8 %collective-permute-start.10 = (bf16[4,256,512]{2,1,0:T(8,128)(2,1)S(1)}, bf16[4,256,512]{2,1,0:T(8,128)(2,1)S(1)}, u32[]{:S(2)}, u32[]{:S(2)}) collective-permute-start(bf16[4,256,512]{2,1,0:T(8,128)(2,1)S(1)} %shard_map.74.refs_1_), channel_id=1, source_target_pairs={{0,1},{1,0},{2,3},{3,2},{4,5},{5,4},{6,7},{7,6},{8,9},{9,8},{10,11... | collective-permute-start | bytes 3145736 | tf_op jit(solution)/shard_map/ppermute | solution.py:484
  51.7 13.3 %collective-permute-start.9 = (bf16[384,1024]{1,0:T(8,128)(2,1)}, bf16[384,1024]{1,0:T(8,128)(2,1)S(1)}, u32[]{:S(2)}, u32[]{:S(2)}) collective-permute-start(bf16[384,1024]{1,0:T(8,128)(2,1)} %collective-permute-done.6.refs_12_), channel_id=1, source_target_pairs={{0,2},{2,0},{4,6},{6,4},{1,3},{3,1},{5,7},{7,5},{8,10},{10,8},{12,... | collective-permute-start | bytes 2359304 | tf_op jit(solution)/shard_map/ppermute | solution.py:482
  60.2 19.0 %collective-permute-start.8 = (bf16[1024,512]{1,0:T(8,128)(2,1)S(1)}, bf16[1024,512]{1,0:T(8,128)(2,1)S(1)}, u32[]{:S(2)}, u32[]{:S(2)}) collective-permute-start(bf16[1024,512]{1,0:T(8,128)(2,1)S(1)} %shard_map.73.refs_1_), channel_id=1, source_target_pairs={{8,16},{16,8},{9,17},{17,9},{10,18},{18,10},{11,19},{19,11},{12,20... | collective-permute-start | bytes 3145736 | tf_op jit(solution)/shard_map/ppermute | solution.py:488
  61.0 34.9 %collective-permute-start.7 = (bf16[1024,512]{1,0:T(8,128)(2,1)S(1)}, bf16[1024,512]{1,0:T(8,128)(2,1)S(1)}, u32[]{:S(2)}, u32[]{:S(2)}) collective-permute-start(bf16[1024,512]{1,0:T(8,128)(2,1)S(1)} %shard_map.73.refs_1_), channel_id=1, source_target_pairs={{0,8},{8,0},{16,24},{24,16},{1,9},{9,1},{17,25},{25,17},{2,10},{10... | collective-permute-start | bytes 3145736 | tf_op jit(solution)/shard_map/ppermute | solution.py:486
  74.9 37.3 %copy-start.8 = (bf16[4,256,512]{2,1,0:T(8,128)(2,1)}, bf16[4,256,512]{2,1,0:T(8,128)(2,1)S(1)}, u32[]{:S(2)}) copy-start(bf16[4,256,512]{2,1,0:T(8,128)(2,1)S(1)} %collective-permute-done.10.refs_2_) | copy-start | bytes 3145732
  74.9 27.6 %collective-permute-start.11 = (bf16[320,512]{1,0:T(8,128)(2,1)S(1)}, bf16[320,512]{1,0:T(8,128)(2,1)S(1)}, u32[]{:S(2)}, u32[]{:S(2)}) collective-permute-start(bf16[320,512]{1,0:T(8,128)(2,1)S(1)} %get-tuple-element.131), channel_id=1, source_target_pairs={{0,8},{8,0},{16,24},{24,16},{1,9},{9,1},{17,25},{25,17},{2,10},{10... | collective-permute-start | bytes 983048 | tf_op jit(solution)/shard_map/ppermute | solution.py:486
  76.1 26.4 %collective-permute-start.12 = (bf16[320,512]{1,0:T(8,128)(2,1)S(1)}, bf16[320,512]{1,0:T(8,128)(2,1)S(1)}, u32[]{:S(2)}, u32[]{:S(2)}) collective-permute-start(bf16[320,512]{1,0:T(8,128)(2,1)S(1)} %get-tuple-element.132), channel_id=1, source_target_pairs={{0,16},{8,24},{16,0},{24,8},{1,17},{9,25},{17,1},{25,9},{2,18},{10... | collective-permute-start | bytes 983048 | tf_op jit(solution)/shard_map/ppermute | solution.py:486
  79.0 31.8 %collective-permute-start.13 = (bf16[320,512]{1,0:T(8,128)(2,1)S(1)}, bf16[320,512]{1,0:T(8,128)(2,1)S(1)}, u32[]{:S(2)}, u32[]{:S(2)}) collective-permute-start(bf16[320,512]{1,0:T(8,128)(2,1)S(1)} %get-tuple-element.133), channel_id=1, source_target_pairs={{0,24},{8,16},{16,8},{24,0},{1,25},{9,17},{17,9},{25,1},{2,26},{10... | collective-permute-start | bytes 983048 | tf_op jit(solution)/shard_map/ppermute | solution.py:486
  113.1 32.0 %collective-permute-start.14 = (bf16[1024,512]{1,0:T(8,128)(2,1)S(1)}, bf16[1024,512]{1,0:T(8,128)(2,1)}, u32[]{:S(2)}, u32[]{:S(2)}) collective-permute-start(bf16[1024,512]{1,0:T(8,128)(2,1)S(1)} %collective-permute-done.7.refs_2_), channel_id=1, source_target_pairs={{8,16},{16,8},{9,17},{17,9},{10,18},{18,10},{11,19},{19,11},{12,20... | collective-permute-start | bytes 3145736 | tf_op jit(solution)/shard_map/ppermute | solution.py:488
  114.8 32.1 %collective-permute-start.15 = (bf16[1024,512]{1,0:T(8,128)(2,1)S(1)}, bf16[1024,512]{1,0:T(8,128)(2,1)}, u32[]{:S(2)}, u32[]{:S(2)}) collective-permute-start(bf16[1024,512]{1,0:T(8,128)(2,1)S(1)} %collective-permute-done.8.refs_3_), channel_id=1, source_target_pairs={{8,0},{16,24},{9,1},{17,25},{10,2},{18,26},{11,3},{19,27},{12,4},{... | collective-permute-start | bytes 3145736 | tf_op jit(solution)/shard_map/ppermute | solution.py:487
  116.3 30.7 %collective-permute-start.16 = (bf16[256,2048]{1,0:T(8,128)(2,1)}, bf16[256,2048]{1,0:T(8,128)(2,1)}, u32[]{:S(2)}, u32[]{:S(2)}) collective-permute-start(bf16[256,2048]{1,0:T(8,128)(2,1)} %copy-done), channel_id=1, source_target_pairs={{0,2},{2,0},{4,6},{6,4},{1,3},{3,1},{5,7},{7,5},{8,10},{10,8},{12,... | collective-permute-start | bytes 3145736 | tf_op jit(solution)/shard_map/ppermute | solution.py:482
  132.9 1.2 copy-start.2
  134.2 1.2 copy-start.9
  135.4 1.2 copy-start.10
  136.6 3.9 %copy-start.16 = (f32[32,1024]{1,0:T(8,128)S(1)}, f32[32,1024]{1,0:T(8,128)}, u32[]{:S(2)}) copy-start(f32[32,1024]{1,0:T(8,128)} %get-tuple-element.116.refs_4_) | copy-start | bytes 393220
  136.6 3.9 %copy-start.17 = (f32[32,1024]{1,0:T(8,128)S(1)}, f32[32,1024]{1,0:T(8,128)}, u32[]{:S(2)}) copy-start(f32[32,1024]{1,0:T(8,128)} %get-tuple-element.115.refs_3_) | copy-start | bytes 393220
  136.6 3.9 %copy-start.18 = (f32[32,1024]{1,0:T(8,128)S(1)}, f32[32,1024]{1,0:T(8,128)}, u32[]{:S(2)}) copy-start(f32[32,1024]{1,0:T(8,128)} %get-tuple-element.113.refs_1_) | copy-start | bytes 393220
  136.6 3.9 %copy-start.19 = (f32[32,1024]{1,0:T(8,128)S(1)}, f32[32,1024]{1,0:T(8,128)}, u32[]{:S(2)}) copy-start(f32[32,1024]{1,0:T(8,128)} %get-tuple-element.114.refs_2_) | copy-start | bytes 393220
  138.5 2.0 collective-permute-start.17
  148.2 16.8 %collective-permute-start.18 = (bf16[512,512]{1,0:T(8,128)(2,1)S(1)}, bf16[512,512]{1,0:T(8,128)(2,1)S(1)}, u32[]{:S(2)}, u32[]{:S(2)}) collective-permute-start(bf16[512,512]{1,0:T(8,128)(2,1)S(1)} %get-tuple-element.192), channel_id=1, source_target_pairs={{8,0},{16,24},{9,1},{17,25},{10,2},{18,26},{11,3},{19,27},{12,4},{... | collective-permute-start | bytes 1572872 | tf_op jit(solution)/shard_map/ppermute | solution.py:487
  149.5 24.5 %collective-permute-start.22 = (bf16[512,512]{1,0:T(8,128)(2,1)S(1)}, bf16[512,512]{1,0:T(8,128)(2,1)S(1)}, u32[]{:S(2)}, u32[]{:S(2)}) collective-permute-start(bf16[512,512]{1,0:T(8,128)(2,1)S(1)} %get-tuple-element.191), channel_id=1, source_target_pairs={{8,0},{16,24},{9,1},{17,25},{10,2},{18,26},{11,3},{19,27},{12,4},{... | collective-permute-start | bytes 1572872 | tf_op jit(solution)/shard_map/ppermute | solution.py:487
  150.8 34.2 %collective-permute-start.23 = (bf16[512,2,256]{2,1,0:T(2,128)(2,1)S(1)}, bf16[512,2,256]{2,1,0:T(2,128)(2,1)S(1)}, u32[]{:S(2)}, u32[]{:S(2)}) collective-permute-start(bf16[512,2,256]{2,1,0:T(2,128)(2,1)S(1)} %get-tuple-element.152), channel_id=1, source_target_pairs={{0,4},{2,6},{4,0},{6,2},{1,5},{3,7},{5,1},{7,3},{8,12},{10,14},{12... | collective-permute-start | bytes 1572872 | tf_op jit(solution)/shard_map/ppermute | solution.py:483
  170.0 10.2 %collective-permute-start.19 = (bf16[256,2,256]{2,1,0:T(2,128)(2,1)S(1)}, bf16[256,2,256]{2,1,0:T(2,128)(2,1)S(1)}, u32[]{:S(2)}, u32[]{:S(2)}) collective-permute-start(bf16[256,2,256]{2,1,0:T(2,128)(2,1)S(1)} %get-tuple-element.162), channel_id=1, source_target_pairs={{0,1},{1,0},{2,3},{3,2},{4,5},{5,4},{6,7},{7,6},{8,9},{9,8},{10,11... | collective-permute-start | bytes 786440 | tf_op jit(solution)/shard_map/ppermute | solution.py:484
  170.3 10.4 %collective-permute-start.20 = (bf16[256,2,256]{2,1,0:T(2,128)(2,1)S(1)}, bf16[256,2,256]{2,1,0:T(2,128)(2,1)S(1)}, u32[]{:S(2)}, u32[]{:S(2)}) collective-permute-start(bf16[256,2,256]{2,1,0:T(2,128)(2,1)S(1)} %get-tuple-element.163), channel_id=1, source_target_pairs={{0,4},{2,6},{4,0},{6,2},{1,5},{3,7},{5,1},{7,3},{8,12},{10,14},{12... | collective-permute-start | bytes 786440 | tf_op jit(solution)/shard_map/ppermute | solution.py:483
  170.9 11.7 %collective-permute-start.21 = (bf16[256,2,256]{2,1,0:T(2,128)(2,1)S(1)}, bf16[256,2,256]{2,1,0:T(2,128)(2,1)S(1)}, u32[]{:S(2)}, u32[]{:S(2)}) collective-permute-start(bf16[256,2,256]{2,1,0:T(2,128)(2,1)S(1)} %get-tuple-element.164), channel_id=1, source_target_pairs={{0,5},{1,4},{2,7},{3,6},{4,1},{5,0},{6,3},{7,2},{8,13},{9,12},{10,... | collective-permute-start | bytes 786440 | tf_op jit(solution)/shard_map/ppermute | solution.py:485
  179.0 10.4 %collective-permute-start.24 = (bf16[256,2,256]{2,1,0:T(2,128)(2,1)S(1)}, bf16[256,2,256]{2,1,0:T(2,128)(2,1)S(1)}, u32[]{:S(2)}, u32[]{:S(2)}) collective-permute-start(bf16[256,2,256]{2,1,0:T(2,128)(2,1)S(1)} %get-tuple-element.171), channel_id=1, source_target_pairs={{0,1},{1,0},{2,3},{3,2},{4,5},{5,4},{6,7},{7,6},{8,9},{9,8},{10,11... | collective-permute-start | bytes 786440 | tf_op jit(solution)/shard_map/ppermute | solution.py:484
  180.2 9.3 %collective-permute-start.25 = (bf16[256,2,256]{2,1,0:T(2,128)(2,1)S(1)}, bf16[256,2,256]{2,1,0:T(2,128)(2,1)S(1)}, u32[]{:S(2)}, u32[]{:S(2)}) collective-permute-start(bf16[256,2,256]{2,1,0:T(2,128)(2,1)S(1)} %get-tuple-element.172), channel_id=1, source_target_pairs={{0,4},{2,6},{4,0},{6,2},{1,5},{3,7},{5,1},{7,3},{8,12},{10,14},{12... | collective-permute-start | bytes 786440 | tf_op jit(solution)/shard_map/ppermute | solution.py:483
  180.7 11.5 %collective-permute-start.26 = (bf16[256,2,256]{2,1,0:T(2,128)(2,1)S(1)}, bf16[256,2,256]{2,1,0:T(2,128)(2,1)S(1)}, u32[]{:S(2)}, u32[]{:S(2)}) collective-permute-start(bf16[256,2,256]{2,1,0:T(2,128)(2,1)S(1)} %get-tuple-element.173), channel_id=1, source_target_pairs={{0,5},{1,4},{2,7},{3,6},{4,1},{5,0},{6,3},{7,2},{8,13},{9,12},{10,... | collective-permute-start | bytes 786440 | tf_op jit(solution)/shard_map/ppermute | solution.py:485
  (3 other events, 3.1 us)
Sparse Core Ops, SparseCore 0:
  113.3 19.6 all-gather.2

commit v4 on v3

--- a/solution.py
+++ b/solution.py
@@ -107,7 +107,7 @@
 
 
 FINE = 32
-CHUNKS = 2
+CUTS = (0, 3, 6, 8)
 PLACE_Y, CORE, INNER, SAME, MINE, PLACE_X = range(6)
 VMEM = 48 * 1024 * 1024
 
@@ -515,16 +515,18 @@
     raw = lax.dynamic_slice_in_dim(jnp.stack([src_real[last], src_imag[last]]), y * half, half, 1)
     raw = spread([step(flat(raw))] * n_z)
     x_own = step(bin_of(src_real, src_imag, mine))
+    raw[1], x_own = step((raw[1], x_own))
     x_other = core(x_own)
 
     at_src = jnp.concatenate([take(src_pos, block, a_block) for block in (s, s ^ 2, s ^ 1, s ^ 3)])
     at_rcv = jnp.concatenate([take(rcv_pos, block, b_block) for block in (y, 1 - y)])
     f_mine, f_last = lax.dynamic_index_in_dim(freqs, mine, 0, False), freqs[last]
-    chunk = p_block // CHUNKS
     here, there = s * p_block, (s ^ 2) * p_block
-    n = jnp.arange(2 * p_block // FINE, dtype=jnp.int32) * FINE
-    starts = jnp.where(n // chunk % 2 == 0, here, there) + n // (2 * chunk) * chunk + n % chunk
-    x_other = step(x_other)
+    cuts = [cut * p_block // CUTS[-1] for cut in CUTS]
+    spans = list(zip(cuts, cuts[1:]))
+    runs = [(i, n) for span in spans for i in range(2) for n in range(*span, FINE)]
+    side, first = jnp.array([i for i, _ in runs], jnp.int32), jnp.array([n for _, n in runs], jnp.int32)
+    starts = jnp.where(side == 0, here, there) + first
     t_source = step(tables(f_mine, starts, SRC_SL, at_src))
     x_given = step(x_given)
     x_cross = core(x_given)
@@ -541,7 +543,7 @@
     t_receiver, t_receiver_last, t_source_last = step((t_receiver, t_receiver_last, t_source_last))
     y_given = step(y_given)
     y_other = core(y_given)
-    x_cross, raw = step((x_cross, raw))
+    x_cross, x_other, raw = step((x_cross, x_other, raw))
     raw = step(arranged(flags, raw, True))
     other_raw = over_y(raw)
     pieces = step(steered(flags, t_source, [x_own, x_given, x_other, x_cross], 4, joined=True))
@@ -561,27 +563,29 @@
     yr_last = step(yr_last)
     focus = step(focused(focus_scale, flags, raw, other_raw, yr_last))
     focus = step([focus, core(focus)])
+    two, three, yr_other = step((two, three, yr_other))
+    four = [ends(two[2 * first : 2 * past]) for first, past in spans]
     kept, given = step(steered(flags, t_source_last, focus, 2, scale=beam_scale, paired=True))
-    two, three, yr_other = step((two, three, yr_other))
     given = over_x(given)
-    four = [ends(two[k * 2 * chunk : (k + 1) * 2 * chunk]) for k in range(CHUNKS)]
-
     shape = (p_block, bins, 2, q_block)
-    four[0] = step(four[0])
     parts = [pieces, near, one, three, two]
     scale = focus_scale * beam_scale
-    share = lambda found: [found[0], over_y(found[1]), over_x(found[2]), over_xy(found[3])]
-    found = step(product(scale, 0, 2 * chunk, flags, [*parts, four[0]], yr_mine, yr_other))
-    found = share(found)
-    four[1] = step(four[1])
-    later = step(product(scale, 1, 2 * chunk, flags, [*parts, four[1]], yr_mine, yr_other))
-    found = step(found)
-    later = share(later)
-    whole = step(placed(flags, None, shape, found, 0))
-    given = step(given)
-    whole = step(placed_last(whole, kept, given))
-    later = step(later)
-    return placed(flags, whole, shape, later, 1).transpose(0, 2, 1, 3)
+    sent, whole = [], None
+    for k, (first, past) in enumerate(spans):
+        rows = 2 * (past - first)
+        four[k] = step(four[k])
+        found = step(product(scale, 2 * first // rows, rows, flags, [*parts, four[k]], yr_mine, yr_other))
+        if k == 0:
+            given = step(given)
+        if k > 0:
+            sent[-1] = step(sent[-1])
+        sent.append([found[0], over_y(found[1]), over_x(found[2]), over_xy(found[3])])
+    for k, (first, past) in enumerate(spans):
+        found = step(sent[k]) if k == len(spans) - 1 else sent[k]
+        whole = placed(flags, whole, shape, found, first // (past - first))
+        if k == 0:
+            whole = placed_last(whole, kept, given)
+    return whole.transpose(0, 2, 1, 3)
 
 
 def solution(mesh):

time: 202 us -> 193 us (0.955)
  waiting for transfers between devices: 88.1 us -> 66.7 us
  starting transfers between devices: 33.5 us -> 37.5 us
  Pallas kernels: 40.6 us -> 44.3 us
  local copies, waits for them, and re-layouts: 12.4 us -> 14.9 us
  other arithmetic: 10.5 us -> 12.7 us
    ppermute x4 -> x5, waiting for transfers between devices: 18.8 us -> 1.3 us  [shards_plane(): over_y = lambda v: lax.ppermute(v, 'rcv', [(0, 1), (1, 0)])]
    ppermute x3 -> x4, waiting for transfers between devices: 15.8 us -> 11.4 us  [shards_plane(): ends = lambda v: lax.ppermute(v, 'tm', [(1, 0), (2, 3)])]
    ppermute x7, waiting for transfers between devices: 31.6 us -> 34.7 us  [shards_plane(): lax.ppermute(v, 'tm', [(i, i ^ d) for i in range(n_z)])]
    unnamed x46 -> x52, local copies, waits for them, and re-layouts: 6.79 us -> 9.64 us
    ppermute x2 -> x3, waiting for transfers between devices: 2.82 us -> 0.01 us  [shards_plane(): lax.ppermute(v, ('src', 'rcv'), [(i, i ^ 5) for i in range(8)])]
    ppermute x2 -> x3, starting transfers between devices: 4.48 us -> 6.67 us  [shards_plane(): lax.ppermute(v, ('src', 'rcv'), [(i, i ^ 5) for i in range(8)])]
    ppermute x4 -> x5, starting transfers between devices: 3.34 us -> 5.48 us  [shards_plane(): over_x = lambda v: lax.ppermute(v, 'src', [(i, i ^ 2) for i in range(4)])]
    pallas_call x2 -> x3, Pallas kernels: 4.88 us -> 6.69 us  [placed(): pl.pallas_call(place_kernel, grid_spec=pltpu.PrefetchScalarGridSpec(num_s...]
  transfers between devices with their start and end apart: 28 -> 32, of which waited for: 13 -> 12; matrix products, arithmetic and copies ran while one was open for 5% -> 6% of each run, Pallas kernels for 18% -> 21%
where the time goes in v4:
time: 193 us; the launch traced here: 192 us
  waiting for transfers between devices  66.7 us (35%)
  Pallas kernels  44.3 us (23%)
  starting transfers between devices  37.5 us (19%)
  between operations  16.4 us (8%)
  local copies, waits for them, and re-layouts  14.9 us (8%)
  other arithmetic  12.7 us (7%)
    ppermute x7, waiting for transfers between devices, shards_plane(): lax.ppermute(v, 'tm', [(i, i ^ d) for i in range(n_z)])  34.7 us
    all_gather x1, waiting for transfers between devices, shards_plane(): yr_last = lax.all_gather(yr_last, 'src', axis=0)  17.5 us
    ppermute x7, starting transfers between devices, shards_plane(): lax.ppermute(v, 'tm', [(i, i ^ d) for i in range(n_z)])  12.9 us
    pallas_call x3, Pallas kernels, product(): pl.pallas_call(lambda *refs: product_kernel(scale, *refs), grid=(1,), out...  11.7 us
    ppermute x4, waiting for transfers between devices, shards_plane(): ends = lambda v: lax.ppermute(v, 'tm', [(1, 0), (2, 3)])  11.4 us
    pallas_call x2, Pallas kernels, steered(): pl.pallas_call(lambda *refs: steered_kernel(sign, scale, len(parts), len(...  11.2 us
    unnamed x52, local copies, waits for them, and re-layouts  9.64 us
    sin x3, other arithmetic, waves(): return (jnp.cos(angle), jnp.sin(angle))  9.17 us
  transfers between devices with their start and end apart: 32, of which 12 were waited for; matrix products, arithmetic and copies ran while one was open for 6% of the time, Pallas kernels for 21%

profile of v4, /device:TPU:0, one launch (start us, length us, event | category | flops | bytes accessed | tf_op | source)
XLA Modules:
  0.0 192.4 jit_solution(3120331802396190472)
XLA Ops:
  6.5 2.3 %constant_dynamic-slice_fusion = (bf16[1,256,512]{2,1,0:T(8,128)(2,1)}, bf16[1,256,512]{2,1,0:T(8,128)(2,1)S(1)}, bf16[1,256,512]{2,1,0:T(8,128)(2,1)S(1)}, bf16...) fusion(bf16[5,256,512]{2,1,0:T(8,128)(2,1)} %param.10, ...), kind=kLoop, calls=%fused_computation.29 | loop fusion | bytes 3145736 | tf_op jit(solution)/shard_map/jit(dynamic_index_in_dim)/dynamic_slice | solution.py:502
  9.7 1.0 dynamic-slice_bitcast_fusion.2
  10.7 1.1 dynamic-slice_bitcast_fusion
  12.8 5.1 %collective-permute-start.5 = (bf16[256,512]{1,0:T(8,128)(2,1)S(1)}, bf16[256,512]{1,0:T(8,128)(2,1)S(1)}, u32[]{:S(2)}, u32[]{:S(2)}) collective-permute-start(bf16[256,512]{1,0:T(8,128)(2,1)S(1)} %bitcast.25), channel_id=1, source_target_pairs={{0,24},{8,16},{16,8},{24,0},{1,25},{9,17},{17,9},{25,1},{2,26},{10... | collective-permute-start | bytes 786440 | tf_op jit(solution)/shard_map/ppermute | solution.py:486
  18.5 1.6 collective-permute-start.1
  20.2 1.5 collective-permute-start.6
  25.7 5.6 %multiply_sine_fusion = (f32[32,2048]{1,0:T(8,128)S(1)}, f32[32,2048]{1,0:T(8,128)S(1)}, f32[32,2048]{1,0:T(8,128)S(1)}, f32[32,2048]{1,0:T(8,128)S(1)}, f32[32,...) fusion(f32[32]{0:T(128)S(1)} %get-tuple-element.262, ...), kind=kLoop, calls=%fused_computation.5 | loop fusion | flops 327680 | bytes 2638336 | tf_op jit(solution)/shard_map/sin | solution.py:117
  31.2 1.1 pad_maximum_fusion.2
  32.3 2.4 %collective-permute-done.one = bf16[256,512]{1,0:T(8,128)(2,1)} collective-permute-done((bf16[256,512]{1,0:T(8,128)(2,1)S(1)}, bf16[256,512]{1,0:T(8,128)(2,1)}, u32[]{:S(2)}, u32[]{:S(2)}) %collective-permute-start) | collective-permute-done | bytes 262176 | tf_op jit(solution)/shard_map/ppermute | solution.py:486
  35.3 1.2 multiply_sine_fusion.7
  36.6 2.4 %multiply_sine_fusion.5 = (f32[32,1024]{1,0:T(8,128)}, f32[32,1024]{1,0:T(8,128)}, f32[32,1024]{1,0:T(8,128)}, f32[32,1024]{1,0:T(8,128)}) fusion(f32[32]{0:T(128)} %copy-done.22, f32[1024]{0:T(1024)S(1)} %pad_maximum_fusion.5, f32[32]{0:T(128)} %get-tuple-element.255), kind=kLoop, calls=%fused_computation.18 | loop fusion | flops 65536 | bytes 528640 | tf_op jit(solution)/shard_map/sin | solution.py:117
  39.0 1.3 collective-permute-done.4.two
  40.3 1.1 shard_map.92.refs_1_
  41.5 1.6 collective-permute-start.10
  45.0 1.0 copy-done.15
  46.0 6.6 %shard_map.91.refs_1_ = bf16[1024,512]{1,0:T(8,128)(2,1)S(1)} custom-call(s32[6]{0:T(128)S(1)} %stack.48.refs_0_.flags, f32[32,2048]{1,0:T(8,128)S(1)} %get-tuple-element.114.refs_1_, f32[32,2048]{1,0:T(8,128)S(1)} %get-tuple-element.115.refs_2_, f32[32,2048]{1,0:T(8,128)S(1)} %copy-done.8, f32[32,2048]{1,0:T(8,128)S(1)} %copy-done.9, ...), custom_call_target="tpu_custom_call" | custom-call | flops 1 | bytes 1 | tf_op jit(solution)/shard_map/pallas_call | solution.py:195
  53.4 2.6 %collective-permute-start.7 = (bf16[1024,512]{1,0:T(8,128)(2,1)S(1)}, bf16[1024,512]{1,0:T(8,128)(2,1)S(1)}, u32[]{:S(2)}, u32[]{:S(2)}) collective-permute-start(bf16[1024,512]{1,0:T(8,128)(2,1)S(1)} %shard_map.91.refs_1_), channel_id=1, source_target_pairs={{0,8},{8,0},{16,24},{24,16},{1,9},{9,1},{17,25},{25,17},{2,10},{10... | collective-permute-start | bytes 3145736 | tf_op jit(solution)/shard_map/ppermute | solution.py:486
  56.0 9.1 %shard_map.93 = (bf16[320,512]{1,0:T(8,128)(2,1)S(1)}, bf16[320,512]{1,0:T(8,128)(2,1)S(1)}, bf16[320,512]{1,0:T(8,128)(2,1)S(1)}, bf16[320,512]{1,0:T(8,128)(2,1)S(1)}) custom-call(s32[6]{0:T(128)S(1)} %stack.48.refs_0_.flags, f32[32,2048]{1,0:T(8,128)S(1)} %get-tuple-element.119.refs_0_, f32[32,2048]{1,0:T(8,128)S(1)} %copy-done.7, ...), custom_call_target="tpu_custom_call" | custom-call | flops 1 | bytes 1 | tf_op jit(solution)/shard_map/pallas_call | solution.py:371
  65.8 1.0 copy-done.10
  66.8 2.2 %collective-permute-start.11 = (bf16[320,512]{1,0:T(8,128)(2,1)S(1)}, bf16[320,512]{1,0:T(8,128)(2,1)S(1)}, u32[]{:S(2)}, u32[]{:S(2)}) collective-permute-start(bf16[320,512]{1,0:T(8,128)(2,1)S(1)} %get-tuple-element.146), channel_id=1, source_target_pairs={{0,8},{8,0},{16,24},{24,16},{1,9},{9,1},{17,25},{25,17},{2,10},{10... | collective-permute-start | bytes 983048 | tf_op jit(solution)/shard_map/ppermute | solution.py:486
  69.6 1.7 collective-permute-start.13
  71.4 8.6 %collective-permute-done.7.refs_2_ = bf16[1024,512]{1,0:T(8,128)(2,1)S(1)} collective-permute-done((bf16[1024,512]{1,0:T(8,128)(2,1)S(1)}, bf16[1024,512]{1,0:T(8,128)(2,1)S(1)}, u32[]{:S(2)}, u32[]{:S(2)}) %collective-permute-start.7) | collective-permute-done | bytes 1048608 | tf_op jit(solution)/shard_map/ppermute | solution.py:486
  81.0 12.9 %collective-permute-done.11.one = bf16[320,512]{1,0:T(8,128)(2,1)S(1)} collective-permute-done((bf16[320,512]{1,0:T(8,128)(2,1)S(1)}, bf16[320,512]{1,0:T(8,128)(2,1)S(1)}, u32[]{:S(2)}, u32[]{:S(2)}) %collective-permute-start.11) | collective-permute-done | bytes 327712 | tf_op jit(solution)/shard_map/ppermute | solution.py:486
  93.8 9.5 %collective-permute-done.13.three = bf16[320,512]{1,0:T(8,128)(2,1)S(1)} collective-permute-done((bf16[320,512]{1,0:T(8,128)(2,1)S(1)}, bf16[320,512]{1,0:T(8,128)(2,1)S(1)}, u32[]{:S(2)}, u32[]{:S(2)}) %collective-permute-start.13) | collective-permute-done | bytes 327712 | tf_op jit(solution)/shard_map/ppermute | solution.py:486
  103.3 1.3 shard_map.94
  106.4 1.5 collective-permute-start.15
  107.9 17.5 %all-gather.3.cloned.1.call-done = bf16[512,1024]{1,0:T(8,128)(2,1)} async-done(((bf16[128,1024]{1,0:T(8,128)(2,1)}), bf16[512,1024]{1,0:T(8,128)(2,1)}) %all-gather.3.cloned.1.call-update) | async-done | bytes 1048592 | tf_op jit(solution)/shard_map/all_gather | solution.py:560
  125.5 1.2 copy-done.6
  126.7 1.2 copy-done.11
  127.9 1.2 copy-done.12
  129.1 1.9 shard_map.95.refs_5_
  131.4 1.7 collective-permute-done.17.refs_6_
  133.1 4.6 %shard_map.96 = (f32[512,2,256]{2,1,0:T(2,128)S(1)}, bf16[512,2,256]{2,1,0:T(2,128)(2,1)S(1)}) custom-call(s32[6]{0:T(128)S(1)} %stack.48.refs_0_.flags, f32[32,1024]{1,0:T(8,128)S(1)} %copy-done.18, f32[32,1024]{1,0:T(8,128)S(1)} %copy-done.19, f32[32,1024]{1,0:T(8,128)S(1)} %copy-done.17, f32[32,1024]{1,0:T(8,128)S(1)} %copy-done.16, ...), custom_call_target="tpu_custom_call" | custom-call | flops 1 | bytes 1 | tf_op jit(solution)/shard_map/pallas_call | solution.py:195
  138.4 1.5 collective-permute-start.23
  140.0 1.3 collective-permute-start.18
  141.3 1.3 collective-permute-start.22
  142.6 1.3 collective-permute-start.27
  143.9 10.0 %collective-permute-done.18.refs_6_ = bf16[384,512]{1,0:T(8,128)(2,1)S(1)} collective-permute-done((bf16[384,512]{1,0:T(8,128)(2,1)S(1)}, bf16[384,512]{1,0:T(8,128)(2,1)S(1)}, u32[]{:S(2)}, u32[]{:S(2)}) %collective-permute-start.18) | collective-permute-done | bytes 393248 | tf_op jit(solution)/shard_map/ppermute | solution.py:487
  154.0 4.2 %shard_map.97 = (f32[192,2,256]{2,1,0:T(2,128)S(1)}, bf16[192,2,256]{2,1,0:T(2,128)(2,1)S(1)}, bf16[192,2,256]{2,1,0:T(2,128)(2,1)S(1)}, bf16[192,2,256]{2,1,0:T(2,128)(2,1)S(1)}) custom-call(s32[6]{0:T(128)S(1)} %stack.48.refs_0_.flags, bf16[1024,512]{1,0:T(8,128)(2,1)S(1)} %shard_map.91.refs_1_, bf16[1024,512]{1,0:T(8,128)(2,1)S(1)} %copy-done.3, ...), custom_call_target="tpu_custom_call" | custom-call | flops 1 | bytes 1 | tf_op jit(solution)/shard_map/pallas_call | solution.py:272
  159.5 2.2 %collective-permute-start.21 = (bf16[192,2,256]{2,1,0:T(2,128)(2,1)S(1)}, bf16[192,2,256]{2,1,0:T(2,128)(2,1)S(1)}, u32[]{:S(2)}, u32[]{:S(2)}) collective-permute-start(bf16[192,2,256]{2,1,0:T(2,128)(2,1)S(1)} %get-tuple-element.179), channel_id=1, source_target_pairs={{0,5},{1,4},{2,7},{3,6},{4,1},{5,0},{6,3},{7,2},{8,13},{9,12},{10,... | collective-permute-start | bytes 589832 | tf_op jit(solution)/shard_map/ppermute | solution.py:485
  162.4 4.2 %shard_map.98 = (f32[192,2,256]{2,1,0:T(2,128)S(1)}, bf16[192,2,256]{2,1,0:T(2,128)(2,1)S(1)}, bf16[192,2,256]{2,1,0:T(2,128)(2,1)S(1)}, bf16[192,2,256]{2,1,0:T(2,128)(2,1)S(1)}) custom-call(s32[6]{0:T(128)S(1)} %stack.48.refs_0_.flags, bf16[1024,512]{1,0:T(8,128)(2,1)S(1)} %shard_map.91.refs_1_, bf16[1024,512]{1,0:T(8,128)(2,1)S(1)} %copy-done.3, ...), custom_call_target="tpu_custom_call" | custom-call | flops 1 | bytes 1 | tf_op jit(solution)/shard_map/pallas_call | solution.py:272
  167.9 2.2 %collective-permute-start.26 = (bf16[192,2,256]{2,1,0:T(2,128)(2,1)S(1)}, bf16[192,2,256]{2,1,0:T(2,128)(2,1)S(1)}, u32[]{:S(2)}, u32[]{:S(2)}) collective-permute-start(bf16[192,2,256]{2,1,0:T(2,128)(2,1)S(1)} %get-tuple-element.189), channel_id=1, source_target_pairs={{0,5},{1,4},{2,7},{3,6},{4,1},{5,0},{6,3},{7,2},{8,13},{9,12},{10,... | collective-permute-start | bytes 589832 | tf_op jit(solution)/shard_map/ppermute | solution.py:485
  170.1 3.3 %shard_map.101 = (f32[128,2,256]{2,1,0:T(2,128)S(1)}, bf16[128,2,256]{2,1,0:T(2,128)(2,1)S(1)}, bf16[128,2,256]{2,1,0:T(2,128)(2,1)S(1)}, bf16[128,2,256]{2,1,0:T(2,128)(2,1)S(1)}) custom-call(s32[6]{0:T(128)S(1)} %stack.48.refs_0_.flags, bf16[1024,512]{1,0:T(8,128)(2,1)S(1)} %shard_map.91.refs_1_, bf16[1024,512]{1,0:T(8,128)(2,1)S(1)} %copy-done.3, ...), custom_call_target="tpu_custom_call" | custom-call | flops 1 | bytes 1 | tf_op jit(solution)/shard_map/pallas_call | solution.py:272
  175.4 2.2 %collective-permute-start.30 = (bf16[128,2,256]{2,1,0:T(2,128)(2,1)S(1)}, bf16[128,2,256]{2,1,0:T(2,128)(2,1)S(1)}, u32[]{:S(2)}, u32[]{:S(2)}) collective-permute-start(bf16[128,2,256]{2,1,0:T(2,128)(2,1)S(1)} %get-tuple-element.202), channel_id=1, source_target_pairs={{0,5},{1,4},{2,7},{3,6},{4,1},{5,0},{6,3},{7,2},{8,13},{9,12},{10,... | collective-permute-start | bytes 393224 | tf_op jit(solution)/shard_map/ppermute | solution.py:485
  177.6 2.3 %shard_map.99._ = f32[512,5,2,256]{3,2,1,0:T(2,128)} custom-call(s32[6]{0:T(128)S(1)} %stack.48.refs_0_.flags, f32[192,2,256]{2,1,0:T(2,128)S(1)} %get-tuple-element.190.refs_0_, bf16[192,2,256]{2,1,0:T(2,128)(2,1)S(1)} %collective-permute-done.19.refs_1_, bf16[192,2,256]{2,1,0:T(2,128)(2,1)S(1)} %collective-permute-done.20.refs_2_, ...), custom_call_target="tpu_custom_call" | custom-call | flops 1 | bytes 1 | tf_op jit(solution)/shard_map/pallas_call | solution.py:434
  179.9 1.2 shard_map.100.refs_0_
  181.1 2.3 %shard_map.102.refs_0_ = f32[512,5,2,256]{3,2,1,0:T(2,128)} custom-call(s32[6]{0:T(128)S(1)} %stack.48.refs_0_.flags, f32[512,5,2,256]{3,2,1,0:T(2,128)} %shard_map.100.refs_0_, f32[192,2,256]{2,1,0:T(2,128)S(1)} %get-tuple-element.203.refs_1_, bf16[192,2,256]{2,1,0:T(2,128)(2,1)S(1)} %collective-permute-done.24.refs_2_, ...), custom_call_target="tpu_custom_call", output_to_operand_aliasing={{}: (1, {})} | custom-call | flops 1 | bytes 1 | tf_op jit(solution)/shard_map/pallas_call | solution.py:434
  183.4 2.1 %shard_map.103 = f32[512,5,2,256]{3,2,1,0:T(2,128)} custom-call(s32[6]{0:T(128)S(1)} %stack.48.refs_0_.flags, f32[512,5,2,256]{3,2,1,0:T(2,128)} %shard_map.102.refs_0_, f32[128,2,256]{2,1,0:T(2,128)S(1)} %get-tuple-element.207.refs_1_, bf16[128,2,256]{2,1,0:T(2,128)(2,1)S(1)} %collective-permute-done.28.refs_2_, ...), custom_call_target="tpu_custom_call", output_to_operand_aliasing={{}: (1, {})} | custom-call | flops 1 | bytes 1 | tf_op jit(solution)/shard_map/pallas_call | solution.py:434
  (104 shorter events, 17.6 us)
Async XLA Ops:
  6.5 118.9 %all-gather.3.cloned.1.call-start = ((), (), s32[]{:S(2)}) async-start(), calls=%async_computation | async-start | bytes 1310720 | tf_op jit(solution)/shard_map/all_gather | solution.py:560
  10.7 11.0 %copy-start.23 = (f32[5]{0:T(128)S(1)}, f32[5]{0:T(128)}, u32[]{:S(2)}) copy-start(f32[5]{0:T(128)} %param.15) | copy-start | bytes 64
  10.7 14.3 %copy-start.24 = (pred[32]{0:T(512)(128)(4,1)S(1)}, pred[32]{0:T(512)(128)(4,1)}, u32[]{:S(2)}) copy-start(pred[32]{0:T(512)(128)(4,1)} %constant.166) | copy-start | bytes 100
  10.7 14.3 %copy-start.25 = (s32[32]{0:T(128)S(1)}, s32[32]{0:T(128)}, u32[]{:S(2)}) copy-start(s32[32]{0:T(128)} %constant.165.clone) | copy-start | bytes 388
  10.7 14.9 %copy-start.20 = (f32[2048]{0:T(1024)S(1)}, f32[2048]{0:T(1024)}, u32[]{:S(2)}) copy-start(f32[2048]{0:T(1024)} %param.14) | copy-start | bytes 24580
  10.7 14.8 %copy-start.21 = (f32[2048]{0:T(1024)S(1)}, f32[2048]{0:T(1024)}, u32[]{:S(2)}) copy-start(f32[2048]{0:T(1024)} %param.13) | copy-start | bytes 24580
  12.8 26.2 %collective-permute-start.5 = (bf16[256,512]{1,0:T(8,128)(2,1)S(1)}, bf16[256,512]{1,0:T(8,128)(2,1)S(1)}, u32[]{:S(2)}, u32[]{:S(2)}) collective-permute-start(bf16[256,512]{1,0:T(8,128)(2,1)S(1)} %bitcast.25), channel_id=1, source_target_pairs={{0,24},{8,16},{16,8},{24,0},{1,25},{9,17},{17,9},{25,1},{2,26},{10... | collective-permute-start | bytes 786440 | tf_op jit(solution)/shard_map/ppermute | solution.py:486
  17.9 22.4 %collective-permute-start.4 = (bf16[256,512]{1,0:T(8,128)(2,1)S(1)}, bf16[256,512]{1,0:T(8,128)(2,1)}, u32[]{:S(2)}, u32[]{:S(2)}) collective-permute-start(bf16[256,512]{1,0:T(8,128)(2,1)S(1)} %bitcast.26), channel_id=1, source_target_pairs={{0,16},{8,24},{16,0},{24,8},{1,17},{9,25},{17,1},{25,9},{2,18},{10... | collective-permute-start | bytes 786440 | tf_op jit(solution)/shard_map/ppermute | solution.py:486
  17.9 16.9 %collective-permute-start = (bf16[256,512]{1,0:T(8,128)(2,1)S(1)}, bf16[256,512]{1,0:T(8,128)(2,1)}, u32[]{:S(2)}, u32[]{:S(2)}) collective-permute-start(bf16[256,512]{1,0:T(8,128)(2,1)S(1)} %bitcast.27), channel_id=1, source_target_pairs={{0,8},{8,0},{16,24},{24,16},{1,9},{9,1},{17,25},{25,17},{2,10},{10... | collective-permute-start | bytes 786440 | tf_op jit(solution)/shard_map/ppermute | solution.py:486
  18.5 16.3 %collective-permute-start.1 = (bf16[512,512]{1,0:T(8,128)(2,1)}, bf16[512,512]{1,0:T(8,128)(2,1)S(1)}, u32[]{:S(2)}, u32[]{:S(2)}) collective-permute-start(bf16[512,512]{1,0:T(8,128)(2,1)} %bitcast.13), channel_id=1, source_target_pairs={{0,4},{2,6},{4,0},{6,2},{1,5},{3,7},{5,1},{7,3},{8,12},{10,14},{12... | collective-permute-start | bytes 1572872 | tf_op jit(solution)/shard_map/ppermute | solution.py:483
  20.2 18.8 %collective-permute-start.6 = (bf16[384,1024]{1,0:T(8,128)(2,1)}, bf16[384,1024]{1,0:T(8,128)(2,1)}, u32[]{:S(2)}, u32[]{:S(2)}) collective-permute-start(bf16[384,1024]{1,0:T(8,128)(2,1)} %pad_maximum_fusion), channel_id=1, source_target_pairs={{0,1},{1,0},{2,3},{3,2},{4,5},{5,4},{6,7},{7,6},{8,9},{9,8},{10,11... | collective-permute-start | bytes 2359304 | tf_op jit(solution)/shard_map/ppermute | solution.py:484
  25.0 7.3 %copy-start.22 = (f32[32]{0:T(128)}, f32[32]{0:T(128)S(1)}, u32[]{:S(2)}) copy-start(f32[32]{0:T(128)S(1)} %get-tuple-element.262) | copy-start | bytes 388
  34.8 5.5 %collective-permute-start.3 = (bf16[512,512]{1,0:T(8,128)(2,1)S(1)}, bf16[512,512]{1,0:T(8,128)(2,1)}, u32[]{:S(2)}, u32[]{:S(2)}) collective-permute-start(bf16[512,512]{1,0:T(8,128)(2,1)S(1)} %bitcast.23), channel_id=1, source_target_pairs={{0,2},{2,0},{4,6},{6,4},{1,3},{3,1},{5,7},{7,5},{8,10},{10,8},{12,... | collective-permute-start | bytes 1572872 | tf_op jit(solution)/shard_map/ppermute | solution.py:482
  34.8 8.3 %copy-start.14 = (bf16[512,512]{1,0:T(8,128)(2,1)}, bf16[512,512]{1,0:T(8,128)(2,1)S(1)}, u32[]{:S(2)}) copy-start(bf16[512,512]{1,0:T(8,128)(2,1)S(1)} %collective-permute-done.1.refs_6_) | copy-start | bytes 1572868
  34.8 5.5 %collective-permute-start.2 = (bf16[512,512]{1,0:T(8,128)(2,1)S(1)}, bf16[512,512]{1,0:T(8,128)(2,1)}, u32[]{:S(2)}, u32[]{:S(2)}) collective-permute-start(bf16[512,512]{1,0:T(8,128)(2,1)S(1)} %collective-permute-done.1.refs_6_), channel_id=1, source_target_pairs={{0,2},{2,0},{4,6},{6,4},{1,3},{3,1},{5,7},{7,5},{8,10},{10,8},{12,... | collective-permute-start | bytes 1572872 | tf_op jit(solution)/shard_map/ppermute | solution.py:482
  40.3 15.7 %copy-start.13 = (f32[16,2048]{1,0:T(8,128)S(1)}, f32[16,2048]{1,0:T(8,128)}, u32[]{:S(2)}) copy-start(f32[16,2048]{1,0:T(8,128)} %get-tuple-element.123.refs_4_) | copy-start | bytes 393220
  41.5 11.2 %copy-start.5 = (bf16[4,256,512]{2,1,0:T(8,128)(2,1)}, bf16[4,256,512]{2,1,0:T(8,128)(2,1)S(1)}, u32[]{:S(2)}) copy-start(bf16[4,256,512]{2,1,0:T(8,128)(2,1)S(1)} %shard_map.92.refs_1_) | copy-start | bytes 3145732
  41.5 14.5 %copy-start.7 = (f32[32,2048]{1,0:T(8,128)S(1)}, f32[32,2048]{1,0:T(8,128)}, u32[]{:S(2)}) copy-start(f32[32,2048]{1,0:T(8,128)} %get-tuple-element.120.refs_1_) | copy-start | bytes 786436
  41.5 24.3 %collective-permute-start.10 = (bf16[4,256,512]{2,1,0:T(8,128)(2,1)S(1)}, bf16[4,256,512]{2,1,0:T(8,128)(2,1)S(1)}, u32[]{:S(2)}, u32[]{:S(2)}) collective-permute-start(bf16[4,256,512]{2,1,0:T(8,128)(2,1)S(1)} %shard_map.92.refs_1_), channel_id=1, source_target_pairs={{0,1},{1,0},{2,3},{3,2},{4,5},{5,4},{6,7},{7,6},{8,9},{9,8},{10,11... | collective-permute-start | bytes 3145736 | tf_op jit(solution)/shard_map/ppermute | solution.py:484
  43.1 12.9 %collective-permute-start.9 = (bf16[384,1024]{1,0:T(8,128)(2,1)}, bf16[384,1024]{1,0:T(8,128)(2,1)S(1)}, u32[]{:S(2)}, u32[]{:S(2)}) collective-permute-start(bf16[384,1024]{1,0:T(8,128)(2,1)} %collective-permute-done.6.refs_12_), channel_id=1, source_target_pairs={{0,2},{2,0},{4,6},{6,4},{1,3},{3,1},{5,7},{7,5},{8,10},{10,8},{12,... | collective-permute-start | bytes 2359304 | tf_op jit(solution)/shard_map/ppermute | solution.py:482
  52.6 18.7 %collective-permute-start.8 = (bf16[1024,512]{1,0:T(8,128)(2,1)S(1)}, bf16[1024,512]{1,0:T(8,128)(2,1)S(1)}, u32[]{:S(2)}, u32[]{:S(2)}) collective-permute-start(bf16[1024,512]{1,0:T(8,128)(2,1)S(1)} %shard_map.91.refs_1_), channel_id=1, source_target_pairs={{8,16},{16,8},{9,17},{17,9},{10,18},{18,10},{11,19},{19,11},{12,20... | collective-permute-start | bytes 3145736 | tf_op jit(solution)/shard_map/ppermute | solution.py:488
  53.4 26.6 %collective-permute-start.7 = (bf16[1024,512]{1,0:T(8,128)(2,1)S(1)}, bf16[1024,512]{1,0:T(8,128)(2,1)S(1)}, u32[]{:S(2)}, u32[]{:S(2)}) collective-permute-start(bf16[1024,512]{1,0:T(8,128)(2,1)S(1)} %shard_map.91.refs_1_), channel_id=1, source_target_pairs={{0,8},{8,0},{16,24},{24,16},{1,9},{9,1},{17,25},{25,17},{2,10},{10... | collective-permute-start | bytes 3145736 | tf_op jit(solution)/shard_map/ppermute | solution.py:486
  66.8 27.1 %collective-permute-start.11 = (bf16[320,512]{1,0:T(8,128)(2,1)S(1)}, bf16[320,512]{1,0:T(8,128)(2,1)S(1)}, u32[]{:S(2)}, u32[]{:S(2)}) collective-permute-start(bf16[320,512]{1,0:T(8,128)(2,1)S(1)} %get-tuple-element.146), channel_id=1, source_target_pairs={{0,8},{8,0},{16,24},{24,16},{1,9},{9,1},{17,25},{25,17},{2,10},{10... | collective-permute-start | bytes 983048 | tf_op jit(solution)/shard_map/ppermute | solution.py:486
  69.0 24.8 %collective-permute-start.12 = (bf16[320,512]{1,0:T(8,128)(2,1)S(1)}, bf16[320,512]{1,0:T(8,128)(2,1)S(1)}, u32[]{:S(2)}, u32[]{:S(2)}) collective-permute-start(bf16[320,512]{1,0:T(8,128)(2,1)S(1)} %get-tuple-element.147), channel_id=1, source_target_pairs={{0,16},{8,24},{16,0},{24,8},{1,17},{9,25},{17,1},{25,9},{2,18},{10... | collective-permute-start | bytes 983048 | tf_op jit(solution)/shard_map/ppermute | solution.py:486
  69.6 33.7 %collective-permute-start.13 = (bf16[320,512]{1,0:T(8,128)(2,1)S(1)}, bf16[320,512]{1,0:T(8,128)(2,1)S(1)}, u32[]{:S(2)}, u32[]{:S(2)}) collective-permute-start(bf16[320,512]{1,0:T(8,128)(2,1)S(1)} %get-tuple-element.148), channel_id=1, source_target_pairs={{0,24},{8,16},{16,8},{24,0},{1,25},{9,17},{17,9},{25,1},{2,26},{10... | collective-permute-start | bytes 983048 | tf_op jit(solution)/shard_map/ppermute | solution.py:486
  105.6 32.0 %collective-permute-start.14 = (bf16[1024,512]{1,0:T(8,128)(2,1)}, bf16[1024,512]{1,0:T(8,128)(2,1)S(1)}, u32[]{:S(2)}, u32[]{:S(2)}) collective-permute-start(bf16[1024,512]{1,0:T(8,128)(2,1)} %copy-done.2), channel_id=1, source_target_pairs={{8,16},{16,8},{9,17},{17,9},{10,18},{18,10},{11,19},{19,11},{12,20... | collective-permute-start | bytes 3145736 | tf_op jit(solution)/shard_map/ppermute | solution.py:488
  106.4 32.1 %collective-permute-start.15 = (bf16[1024,512]{1,0:T(8,128)(2,1)S(1)}, bf16[1024,512]{1,0:T(8,128)(2,1)}, u32[]{:S(2)}, u32[]{:S(2)}) collective-permute-start(bf16[1024,512]{1,0:T(8,128)(2,1)S(1)} %collective-permute-done.8.refs_3_), channel_id=1, source_target_pairs={{8,0},{16,24},{9,1},{17,25},{10,2},{18,26},{11,3},{19,27},{12,4},{... | collective-permute-start | bytes 3145736 | tf_op jit(solution)/shard_map/ppermute | solution.py:487
  107.8 30.6 %collective-permute-start.16 = (bf16[256,2048]{1,0:T(8,128)(2,1)}, bf16[256,2048]{1,0:T(8,128)(2,1)}, u32[]{:S(2)}, u32[]{:S(2)}) collective-permute-start(bf16[256,2048]{1,0:T(8,128)(2,1)} %copy-done.4), channel_id=1, source_target_pairs={{0,2},{2,0},{4,6},{6,4},{1,3},{3,1},{5,7},{7,5},{8,10},{10,8},{12,... | collective-permute-start | bytes 3145736 | tf_op jit(solution)/shard_map/ppermute | solution.py:482
  129.1 3.9 %copy-start.17 = (f32[32,1024]{1,0:T(8,128)S(1)}, f32[32,1024]{1,0:T(8,128)}, u32[]{:S(2)}) copy-start(f32[32,1024]{1,0:T(8,128)} %get-tuple-element.129.refs_3_) | copy-start | bytes 393220
  129.1 3.9 %copy-start.18 = (f32[32,1024]{1,0:T(8,128)S(1)}, f32[32,1024]{1,0:T(8,128)}, u32[]{:S(2)}) copy-start(f32[32,1024]{1,0:T(8,128)} %get-tuple-element.127.refs_1_) | copy-start | bytes 393220
  129.1 3.9 %copy-start.19 = (f32[32,1024]{1,0:T(8,128)S(1)}, f32[32,1024]{1,0:T(8,128)}, u32[]{:S(2)}) copy-start(f32[32,1024]{1,0:T(8,128)} %get-tuple-element.128.refs_2_) | copy-start | bytes 393220
  131.1 22.9 %copy-start.3 = (bf16[1024,512]{1,0:T(8,128)(2,1)S(1)}, bf16[1024,512]{1,0:T(8,128)(2,1)}, u32[]{:S(2)}) copy-start(bf16[1024,512]{1,0:T(8,128)(2,1)} %copy-done.2) | copy-start | bytes 3145732
  131.1 2.0 %collective-permute-start.17 = (bf16[512,512]{1,0:T(8,128)(2,1)S(1)}, bf16[512,512]{1,0:T(8,128)(2,1)S(1)}, u32[]{:S(2)}, u32[]{:S(2)}) collective-permute-start(bf16[512,512]{1,0:T(8,128)(2,1)S(1)} %shard_map.95.refs_5_), channel_id=1, source_target_pairs={{0,2},{2,0},{4,6},{6,4},{1,3},{3,1},{5,7},{7,5},{8,10},{10,8},{12,... | collective-permute-start | bytes 1572872 | tf_op jit(solution)/shard_map/ppermute | solution.py:482
  137.7 16.3 %copy-start = (bf16[1024,512]{1,0:T(8,128)(2,1)}, bf16[1024,512]{1,0:T(8,128)(2,1)S(1)}, u32[]{:S(2)}) copy-start(bf16[1024,512]{1,0:T(8,128)(2,1)S(1)} %collective-permute-done.14.refs_5_) | copy-start | bytes 3145732
  138.4 21.1 %collective-permute-start.23 = (bf16[512,2,256]{2,1,0:T(2,128)(2,1)S(1)}, bf16[512,2,256]{2,1,0:T(2,128)(2,1)S(1)}, u32[]{:S(2)}, u32[]{:S(2)}) collective-permute-start(bf16[512,2,256]{2,1,0:T(2,128)(2,1)S(1)} %get-tuple-element.170), channel_id=1, source_target_pairs={{0,4},{2,6},{4,0},{6,2},{1,5},{3,7},{5,1},{7,3},{8,12},{10,14},{12... | collective-permute-start | bytes 1572872 | tf_op jit(solution)/shard_map/ppermute | solution.py:483
  140.0 13.9 %collective-permute-start.18 = (bf16[384,512]{1,0:T(8,128)(2,1)S(1)}, bf16[384,512]{1,0:T(8,128)(2,1)S(1)}, u32[]{:S(2)}, u32[]{:S(2)}) collective-permute-start(bf16[384,512]{1,0:T(8,128)(2,1)S(1)} %get-tuple-element.218), channel_id=1, source_target_pairs={{8,0},{16,24},{9,1},{17,25},{10,2},{18,26},{11,3},{19,27},{12,4},{... | collective-permute-start | bytes 1179656 | tf_op jit(solution)/shard_map/ppermute | solution.py:487
  141.3 21.1 %collective-permute-start.22 = (bf16[384,512]{1,0:T(8,128)(2,1)S(1)}, bf16[384,512]{1,0:T(8,128)(2,1)S(1)}, u32[]{:S(2)}, u32[]{:S(2)}) collective-permute-start(bf16[384,512]{1,0:T(8,128)(2,1)S(1)} %get-tuple-element.217), channel_id=1, source_target_pairs={{8,0},{16,24},{9,1},{17,25},{10,2},{18,26},{11,3},{19,27},{12,4},{... | collective-permute-start | bytes 1179656 | tf_op jit(solution)/shard_map/ppermute | solution.py:487
  142.6 27.5 %collective-permute-start.27 = (bf16[256,512]{1,0:T(8,128)(2,1)S(1)}, bf16[256,512]{1,0:T(8,128)(2,1)S(1)}, u32[]{:S(2)}, u32[]{:S(2)}) collective-permute-start(bf16[256,512]{1,0:T(8,128)(2,1)S(1)} %slice.23), channel_id=1, source_target_pairs={{8,0},{16,24},{9,1},{17,25},{10,2},{18,26},{11,3},{19,27},{12,4},{... | collective-permute-start | bytes 786440 | tf_op jit(solution)/shard_map/ppermute | solution.py:487
  158.2 12.0 %copy-start.1 = (bf16[1024,512]{1,0:T(8,128)(2,1)S(1)}, bf16[1024,512]{1,0:T(8,128)(2,1)}, u32[]{:S(2)}) copy-start(bf16[1024,512]{1,0:T(8,128)(2,1)} %copy-done) | copy-start | bytes 3145732
  158.2 9.0 %collective-permute-start.19 = (bf16[192,2,256]{2,1,0:T(2,128)(2,1)S(1)}, bf16[192,2,256]{2,1,0:T(2,128)(2,1)S(1)}, u32[]{:S(2)}, u32[]{:S(2)}) collective-permute-start(bf16[192,2,256]{2,1,0:T(2,128)(2,1)S(1)} %get-tuple-element.177), channel_id=1, source_target_pairs={{0,1},{1,0},{2,3},{3,2},{4,5},{5,4},{6,7},{7,6},{8,9},{9,8},{10,11... | collective-permute-start | bytes 589832 | tf_op jit(solution)/shard_map/ppermute | solution.py:484
  158.7 9.2 %collective-permute-start.20 = (bf16[192,2,256]{2,1,0:T(2,128)(2,1)S(1)}, bf16[192,2,256]{2,1,0:T(2,128)(2,1)S(1)}, u32[]{:S(2)}, u32[]{:S(2)}) collective-permute-start(bf16[192,2,256]{2,1,0:T(2,128)(2,1)S(1)} %get-tuple-element.178), channel_id=1, source_target_pairs={{0,4},{2,6},{4,0},{6,2},{1,5},{3,7},{5,1},{7,3},{8,12},{10,14},{12... | collective-permute-start | bytes 589832 | tf_op jit(solution)/shard_map/ppermute | solution.py:483
  159.5 10.6 %collective-permute-start.21 = (bf16[192,2,256]{2,1,0:T(2,128)(2,1)S(1)}, bf16[192,2,256]{2,1,0:T(2,128)(2,1)S(1)}, u32[]{:S(2)}, u32[]{:S(2)}) collective-permute-start(bf16[192,2,256]{2,1,0:T(2,128)(2,1)S(1)} %get-tuple-element.179), channel_id=1, source_target_pairs={{0,5},{1,4},{2,7},{3,6},{4,1},{5,0},{6,3},{7,2},{8,13},{9,12},{10,... | collective-permute-start | bytes 589832 | tf_op jit(solution)/shard_map/ppermute | solution.py:485
  166.6 8.8 %collective-permute-start.24 = (bf16[192,2,256]{2,1,0:T(2,128)(2,1)S(1)}, bf16[192,2,256]{2,1,0:T(2,128)(2,1)S(1)}, u32[]{:S(2)}, u32[]{:S(2)}) collective-permute-start(bf16[192,2,256]{2,1,0:T(2,128)(2,1)S(1)} %get-tuple-element.187), channel_id=1, source_target_pairs={{0,1},{1,0},{2,3},{3,2},{4,5},{5,4},{6,7},{7,6},{8,9},{9,8},{10,11... | collective-permute-start | bytes 589832 | tf_op jit(solution)/shard_map/ppermute | solution.py:484
  167.1 14.0 %collective-permute-start.25 = (bf16[192,2,256]{2,1,0:T(2,128)(2,1)S(1)}, bf16[192,2,256]{2,1,0:T(2,128)(2,1)S(1)}, u32[]{:S(2)}, u32[]{:S(2)}) collective-permute-start(bf16[192,2,256]{2,1,0:T(2,128)(2,1)S(1)} %get-tuple-element.188), channel_id=1, source_target_pairs={{0,4},{2,6},{4,0},{6,2},{1,5},{3,7},{5,1},{7,3},{8,12},{10,14},{12... | collective-permute-start | bytes 589832 | tf_op jit(solution)/shard_map/ppermute | solution.py:483
  167.9 13.2 %collective-permute-start.26 = (bf16[192,2,256]{2,1,0:T(2,128)(2,1)S(1)}, bf16[192,2,256]{2,1,0:T(2,128)(2,1)S(1)}, u32[]{:S(2)}, u32[]{:S(2)}) collective-permute-start(bf16[192,2,256]{2,1,0:T(2,128)(2,1)S(1)} %get-tuple-element.189), channel_id=1, source_target_pairs={{0,5},{1,4},{2,7},{3,6},{4,1},{5,0},{6,3},{7,2},{8,13},{9,12},{10,... | collective-permute-start | bytes 589832 | tf_op jit(solution)/shard_map/ppermute | solution.py:485
  173.4 10.0 %collective-permute-start.28 = (bf16[128,2,256]{2,1,0:T(2,128)(2,1)S(1)}, bf16[128,2,256]{2,1,0:T(2,128)(2,1)S(1)}, u32[]{:S(2)}, u32[]{:S(2)}) collective-permute-start(bf16[128,2,256]{2,1,0:T(2,128)(2,1)S(1)} %get-tuple-element.200), channel_id=1, source_target_pairs={{0,1},{1,0},{2,3},{3,2},{4,5},{5,4},{6,7},{7,6},{8,9},{9,8},{10,11... | collective-permute-start | bytes 393224 | tf_op jit(solution)/shard_map/ppermute | solution.py:484
  174.0 9.4 %collective-permute-start.29 = (bf16[128,2,256]{2,1,0:T(2,128)(2,1)S(1)}, bf16[128,2,256]{2,1,0:T(2,128)(2,1)S(1)}, u32[]{:S(2)}, u32[]{:S(2)}) collective-permute-start(bf16[128,2,256]{2,1,0:T(2,128)(2,1)S(1)} %get-tuple-element.201), channel_id=1, source_target_pairs={{0,4},{2,6},{4,0},{6,2},{1,5},{3,7},{5,1},{7,3},{8,12},{10,14},{12... | collective-permute-start | bytes 393224 | tf_op jit(solution)/shard_map/ppermute | solution.py:483
  175.4 8.0 %collective-permute-start.30 = (bf16[128,2,256]{2,1,0:T(2,128)(2,1)S(1)}, bf16[128,2,256]{2,1,0:T(2,128)(2,1)S(1)}, u32[]{:S(2)}, u32[]{:S(2)}) collective-permute-start(bf16[128,2,256]{2,1,0:T(2,128)(2,1)S(1)} %get-tuple-element.202), channel_id=1, source_target_pairs={{0,5},{1,4},{2,7},{3,6},{4,1},{5,0},{6,3},{7,2},{8,13},{9,12},{10,... | collective-permute-start | bytes 393224 | tf_op jit(solution)/shard_map/ppermute | solution.py:485
  (10 other events, 13.5 us)
Sparse Core Ops, SparseCore 0:
  105.7 19.6 all-gather.2

commit v5 on v4

--- a/solution.py
+++ b/solution.py
@@ -536,11 +536,7 @@
     n = jnp.arange(n_z * q_half // FINE, dtype=jnp.int32) * FINE
     starts = (z ^ n // q_half) * q_plane + y * q_block + c * q_half + n % q_half
     t_receiver_last = tables(f_last, starts, RCV_SL, at_rcv)
-    n = jnp.arange(2 * p_block // FINE, dtype=jnp.int32) * FINE
-    starts = jnp.where(n < p_block, here, there) + n % p_block
-    at_cores = jnp.concatenate([take(src_pos, block, a_block) for block in (s, s ^ 1)])
-    t_source_last = tables(f_last, starts, SRC_SL, at_cores)
-    t_receiver, t_receiver_last, t_source_last = step((t_receiver, t_receiver_last, t_source_last))
+    t_receiver, t_receiver_last = step((t_receiver, t_receiver_last))
     y_given = step(y_given)
     y_other = core(y_given)
     x_cross, x_other, raw = step((x_cross, x_other, raw))
@@ -560,7 +556,12 @@
     yr_last = lax.all_gather(yr_last, "src", axis=0)
     focus_scale = 1.0 / float(wide * n_z * RCV_ST) ** 0.5
     beam_scale = 1.0 / float(SRC_ST) ** 0.5
-    yr_last = step(yr_last)
+    f_last = after(f_last, yr_mine)
+    n = jnp.arange(2 * p_block // FINE, dtype=jnp.int32) * FINE
+    starts = jnp.where(n < p_block, here, there) + n % p_block
+    at_cores = jnp.concatenate([take(src_pos, block, a_block) for block in (s, s ^ 1)])
+    t_source_last = tables(f_last, starts, SRC_SL, at_cores)
+    yr_last, t_source_last = step((yr_last, t_source_last))
     focus = step(focused(focus_scale, flags, raw, other_raw, yr_last))
     focus = step([focus, core(focus)])
     two, three, yr_other = step((two, three, yr_other))

time: 193 us -> 191 us (0.990)
    ppermute x5, waiting for transfers between devices: 1.3 us -> 4.44 us  [shards_plane(): over_y = lambda v: lax.ppermute(v, 'rcv', [(0, 1), (1, 0)])]
    all_gather x1, waiting for transfers between devices: 17.5 us -> 14.5 us  [shards_plane(): yr_last = lax.all_gather(yr_last, 'src', axis=0)]
    ppermute x3, starting transfers between devices: 6.67 us -> 4.41 us  [shards_plane(): lax.ppermute(v, ('src', 'rcv'), [(i, i ^ 5) for i in range(8)])]
    unnamed x52 -> x42, local copies, waits for them, and re-layouts: 9.64 us -> 9.62 us
  transfers between devices with their start and end apart: 32 -> 32, of which waited for: 12 -> 13; matrix products, arithmetic and copies ran while one was open for 6% -> 5% of each run, Pallas kernels for 21% -> 21%
where the time goes in v5:
time: 191 us; the launch traced here: 190 us
  waiting for transfers between devices  66.8 us (35%)
  Pallas kernels  43.7 us (23%)
  starting transfers between devices  36.3 us (19%)
  between operations  17.4 us (9%)
  local copies, waits for them, and re-layouts  14.8 us (8%)
  other arithmetic  10.8 us (6%)
    ppermute x7, waiting for transfers between devices, shards_plane(): lax.ppermute(v, 'tm', [(i, i ^ d) for i in range(n_z)])  33.8 us
    all_gather x1, waiting for transfers between devices, shards_plane(): yr_last = lax.all_gather(yr_last, 'src', axis=0)  14.5 us
    ppermute x7, starting transfers between devices, shards_plane(): lax.ppermute(v, 'tm', [(i, i ^ d) for i in range(n_z)])  12.7 us
    ppermute x4, waiting for transfers between devices, shards_plane(): ends = lambda v: lax.ppermute(v, 'tm', [(1, 0), (2, 3)])  12.5 us
    pallas_call x3, Pallas kernels, product(): pl.pallas_call(lambda *refs: product_kernel(scale, *refs), grid=(1,), out...  11.7 us
    pallas_call x2, Pallas kernels, steered(): pl.pallas_call(lambda *refs: steered_kernel(sign, scale, len(parts), len(...  10.5 us
    unnamed x42, local copies, waits for them, and re-layouts  9.62 us
    pallas_call x1, Pallas kernels, receivers_of(): pl.pallas_call(receivers_kernel, grid_spec=pltpu.PrefetchScalarGridSpec(n...  9.2 us
  transfers between devices with their start and end apart: 32, of which 13 were waited for; matrix products, arithmetic and copies ran while one was open for 5% of the time, Pallas kernels for 21%

profile of v5, /device:TPU:0, one launch (start us, length us, event | category | flops | bytes accessed | tf_op | source)
XLA Modules:
  0.0 189.8 jit_solution(1111101577291172812)
XLA Ops:
  6.5 2.2 %constant_dynamic-slice_fusion = (bf16[1,256,512]{2,1,0:T(8,128)(2,1)}, bf16[1,256,512]{2,1,0:T(8,128)(2,1)S(1)}, bf16[1,256,512]{2,1,0:T(8,128)(2,1)S(1)}, bf16...) fusion(bf16[5,256,512]{2,1,0:T(8,128)(2,1)} %param.10, ...), kind=kLoop, calls=%fused_computation.29 | loop fusion | bytes 3145736 | tf_op jit(solution)/shard_map/jit(dynamic_index_in_dim)/dynamic_slice | solution.py:502
  10.7 1.1 dynamic-slice_bitcast_fusion
  12.7 5.1 %collective-permute-start.5 = (bf16[256,512]{1,0:T(8,128)(2,1)S(1)}, bf16[256,512]{1,0:T(8,128)(2,1)S(1)}, u32[]{:S(2)}, u32[]{:S(2)}) collective-permute-start(bf16[256,512]{1,0:T(8,128)(2,1)S(1)} %bitcast.24), channel_id=1, source_target_pairs={{0,24},{8,16},{16,8},{24,0},{1,25},{9,17},{17,9},{25,1},{2,26},{10... | collective-permute-start | bytes 786440 | tf_op jit(solution)/shard_map/ppermute | solution.py:486
  18.5 1.6 collective-permute-start.1
  20.1 1.5 collective-permute-start.6
  24.2 5.6 %multiply_sine_fusion = (f32[32,2048]{1,0:T(8,128)S(1)}, f32[32,2048]{1,0:T(8,128)S(1)}, f32[32,2048]{1,0:T(8,128)S(1)}, f32[32,2048]{1,0:T(8,128)S(1)}, f32[32,...) fusion(f32[32]{0:T(128)S(1)} %get-tuple-element.264, ...), kind=kLoop, calls=%fused_computation.5 | loop fusion | flops 327680 | bytes 2638336 | tf_op jit(solution)/shard_map/sin | solution.py:117
  31.6 3.2 %collective-permute-done.one = bf16[256,512]{1,0:T(8,128)(2,1)} collective-permute-done((bf16[256,512]{1,0:T(8,128)(2,1)S(1)}, bf16[256,512]{1,0:T(8,128)(2,1)}, u32[]{:S(2)}, u32[]{:S(2)}) %collective-permute-start) | collective-permute-done | bytes 262176 | tf_op jit(solution)/shard_map/ppermute | solution.py:486
  35.8 2.9 %collective-permute-done.6.refs_12_ = bf16[384,1024]{1,0:T(8,128)(2,1)} collective-permute-done((bf16[384,1024]{1,0:T(8,128)(2,1)}, bf16[384,1024]{1,0:T(8,128)(2,1)}, u32[]{:S(2)}, u32[]{:S(2)}) %collective-permute-start.6) | collective-permute-done | bytes 786464 | tf_op jit(solution)/shard_map/ppermute | solution.py:484
  38.7 1.5 collective-permute-done.4.two
  40.3 1.1 shard_map.92.refs_1_
  41.4 1.6 collective-permute-start.10
  45.9 5.9 %shard_map.91.refs_1_ = bf16[1024,512]{1,0:T(8,128)(2,1)S(1)} custom-call(s32[6]{0:T(128)S(1)} %stack.48.refs_0_.flags, f32[32,2048]{1,0:T(8,128)S(1)} %get-tuple-element.115.refs_1_, f32[32,2048]{1,0:T(8,128)S(1)} %get-tuple-element.116.refs_2_, f32[32,2048]{1,0:T(8,128)S(1)} %copy-done.8, f32[32,2048]{1,0:T(8,128)S(1)} %copy-done.9, ...), custom_call_target="tpu_custom_call" | custom-call | flops 1 | bytes 1 | tf_op jit(solution)/shard_map/pallas_call | solution.py:195
  52.6 2.6 %collective-permute-start.7 = (bf16[1024,512]{1,0:T(8,128)(2,1)S(1)}, bf16[1024,512]{1,0:T(8,128)(2,1)S(1)}, u32[]{:S(2)}, u32[]{:S(2)}) collective-permute-start(bf16[1024,512]{1,0:T(8,128)(2,1)S(1)} %shard_map.91.refs_1_), channel_id=1, source_target_pairs={{0,8},{8,0},{16,24},{24,16},{1,9},{9,1},{17,25},{25,17},{2,10},{10... | collective-permute-start | bytes 3145736 | tf_op jit(solution)/shard_map/ppermute | solution.py:486
  55.2 9.2 %shard_map.93 = (bf16[320,512]{1,0:T(8,128)(2,1)S(1)}, bf16[320,512]{1,0:T(8,128)(2,1)S(1)}, bf16[320,512]{1,0:T(8,128)(2,1)S(1)}, bf16[320,512]{1,0:T(8,128)(2,1)S(1)}) custom-call(s32[6]{0:T(128)S(1)} %stack.48.refs_0_.flags, f32[32,2048]{1,0:T(8,128)S(1)} %get-tuple-element.120.refs_0_, f32[32,2048]{1,0:T(8,128)S(1)} %copy-done.7, ...), custom_call_target="tpu_custom_call" | custom-call | flops 1 | bytes 1 | tf_op jit(solution)/shard_map/pallas_call | solution.py:371
  64.4 1.2 collective-permute-done.10.refs_2_
  67.4 2.2 %collective-permute-start.12 = (bf16[320,512]{1,0:T(8,128)(2,1)S(1)}, bf16[320,512]{1,0:T(8,128)(2,1)S(1)}, u32[]{:S(2)}, u32[]{:S(2)}) collective-permute-start(bf16[320,512]{1,0:T(8,128)(2,1)S(1)} %get-tuple-element.144), channel_id=1, source_target_pairs={{0,16},{8,24},{16,0},{24,8},{1,17},{9,25},{17,1},{25,9},{2,18},{10... | collective-permute-start | bytes 983048 | tf_op jit(solution)/shard_map/ppermute | solution.py:486
  69.5 1.5 collective-permute-start.13
  71.1 15.1 %collective-permute-done.7.refs_2_ = bf16[1024,512]{1,0:T(8,128)(2,1)S(1)} collective-permute-done((bf16[1024,512]{1,0:T(8,128)(2,1)S(1)}, bf16[1024,512]{1,0:T(8,128)(2,1)S(1)}, u32[]{:S(2)}, u32[]{:S(2)}) %collective-permute-start.7) | collective-permute-done | bytes 1048608 | tf_op jit(solution)/shard_map/ppermute | solution.py:486
  87.1 5.7 %collective-permute-done.11.one = bf16[320,512]{1,0:T(8,128)(2,1)S(1)} collective-permute-done((bf16[320,512]{1,0:T(8,128)(2,1)S(1)}, bf16[320,512]{1,0:T(8,128)(2,1)S(1)}, u32[]{:S(2)}, u32[]{:S(2)}) %collective-permute-start.11) | collective-permute-done | bytes 327712 | tf_op jit(solution)/shard_map/ppermute | solution.py:486
  92.8 8.3 %collective-permute-done.13.three = bf16[320,512]{1,0:T(8,128)(2,1)S(1)} collective-permute-done((bf16[320,512]{1,0:T(8,128)(2,1)S(1)}, bf16[320,512]{1,0:T(8,128)(2,1)S(1)}, u32[]{:S(2)}, u32[]{:S(2)}) %collective-permute-start.13) | collective-permute-done | bytes 327712 | tf_op jit(solution)/shard_map/ppermute | solution.py:486
  101.1 1.3 shard_map.94
  104.2 1.5 collective-permute-start.15
  107.1 1.7 multiply_sine_fusion.5
  108.8 14.5 %all-gather.3.cloned.1.call-done = bf16[512,1024]{1,0:T(8,128)(2,1)} async-done(((bf16[128,1024]{1,0:T(8,128)(2,1)}), bf16[512,1024]{1,0:T(8,128)(2,1)}) %all-gather.3.cloned.1.call-update) | async-done | bytes 1048592 | tf_op jit(solution)/shard_map/all_gather | solution.py:556
  123.2 1.2 copy-done.6
  124.5 1.2 copy-done.11
  125.7 1.2 copy-done.12
  126.9 1.9 %shard_map.95.refs_5_ = bf16[512,512]{1,0:T(8,128)(2,1)S(1)} custom-call(s32[6]{0:T(128)S(1)} %stack.48.refs_0_.flags, bf16[4,256,512]{2,1,0:T(8,128)(2,1)S(1)} %copy-done.6, bf16[4,256,512]{2,1,0:T(8,128)(2,1)S(1)} %copy-done.11, bf16[4,128,1024]{2,1,0:T(8,128)(2,1)S(1)} %bitcast.28), custom_call_target="tpu_custom_call" | custom-call | flops 1 | bytes 1 | tf_op jit(solution)/shard_map/pallas_call | solution.py:234
  129.1 1.7 collective-permute-done.17.refs_6_
  130.8 4.6 %shard_map.96 = (f32[512,2,256]{2,1,0:T(2,128)S(1)}, bf16[512,2,256]{2,1,0:T(2,128)(2,1)S(1)}) custom-call(s32[6]{0:T(128)S(1)} %stack.48.refs_0_.flags, f32[32,1024]{1,0:T(8,128)S(1)} %get-tuple-element.159.refs_1_, f32[32,1024]{1,0:T(8,128)S(1)} %copy-done.15, f32[32,1024]{1,0:T(8,128)S(1)} %get-tuple-element.161.refs_3_, ...), custom_call_target="tpu_custom_call" | custom-call | flops 1 | bytes 1 | tf_op jit(solution)/shard_map/pallas_call | solution.py:195
  135.4 1.8 collective-permute-done.15.refs_4_
  137.8 1.3 collective-permute-start.18
  139.1 1.3 collective-permute-start.22
  140.5 1.3 collective-permute-start.27
  141.8 10.0 %collective-permute-done.18.refs_6_ = bf16[384,512]{1,0:T(8,128)(2,1)S(1)} collective-permute-done((bf16[384,512]{1,0:T(8,128)(2,1)S(1)}, bf16[384,512]{1,0:T(8,128)(2,1)S(1)}, u32[]{:S(2)}, u32[]{:S(2)}) %collective-permute-start.18) | collective-permute-done | bytes 393248 | tf_op jit(solution)/shard_map/ppermute | solution.py:487
  151.8 4.2 %shard_map.97 = (f32[192,2,256]{2,1,0:T(2,128)S(1)}, bf16[192,2,256]{2,1,0:T(2,128)(2,1)S(1)}, bf16[192,2,256]{2,1,0:T(2,128)(2,1)S(1)}, bf16[192,2,256]{2,1,0:T(2,128)(2,1)S(1)}) custom-call(s32[6]{0:T(128)S(1)} %stack.48.refs_0_.flags, bf16[1024,512]{1,0:T(8,128)(2,1)S(1)} %shard_map.91.refs_1_, bf16[1024,512]{1,0:T(8,128)(2,1)S(1)} %copy-done.3, ...), custom_call_target="tpu_custom_call" | custom-call | flops 1 | bytes 1 | tf_op jit(solution)/shard_map/pallas_call | solution.py:272
  156.6 1.5 collective-permute-start.20
  158.1 1.5 collective-permute-start.21
  160.2 4.2 %shard_map.98 = (f32[192,2,256]{2,1,0:T(2,128)S(1)}, bf16[192,2,256]{2,1,0:T(2,128)(2,1)S(1)}, bf16[192,2,256]{2,1,0:T(2,128)(2,1)S(1)}, bf16[192,2,256]{2,1,0:T(2,128)(2,1)S(1)}) custom-call(s32[6]{0:T(128)S(1)} %stack.48.refs_0_.flags, bf16[1024,512]{1,0:T(8,128)(2,1)S(1)} %shard_map.91.refs_1_, bf16[1024,512]{1,0:T(8,128)(2,1)S(1)} %copy-done.3, ...), custom_call_target="tpu_custom_call" | custom-call | flops 1 | bytes 1 | tf_op jit(solution)/shard_map/pallas_call | solution.py:272
  165.0 1.5 collective-permute-start.25
  166.5 1.5 collective-permute-start.26
  168.0 3.3 %shard_map.101 = (f32[128,2,256]{2,1,0:T(2,128)S(1)}, bf16[128,2,256]{2,1,0:T(2,128)(2,1)S(1)}, bf16[128,2,256]{2,1,0:T(2,128)(2,1)S(1)}, bf16[128,2,256]{2,1,0:T(2,128)(2,1)S(1)}) custom-call(s32[6]{0:T(128)S(1)} %stack.48.refs_0_.flags, bf16[1024,512]{1,0:T(8,128)(2,1)S(1)} %shard_map.91.refs_1_, bf16[1024,512]{1,0:T(8,128)(2,1)S(1)} %copy-done.3, ...), custom_call_target="tpu_custom_call" | custom-call | flops 1 | bytes 1 | tf_op jit(solution)/shard_map/pallas_call | solution.py:272
  171.9 1.5 collective-permute-start.29
  173.6 1.4 collective-permute-start.30
  175.0 2.3 %shard_map.99._ = f32[512,5,2,256]{3,2,1,0:T(2,128)} custom-call(s32[6]{0:T(128)S(1)} %stack.48.refs_0_.flags, f32[192,2,256]{2,1,0:T(2,128)S(1)} %get-tuple-element.192.refs_0_, bf16[192,2,256]{2,1,0:T(2,128)(2,1)S(1)} %collective-permute-done.19.refs_1_, bf16[192,2,256]{2,1,0:T(2,128)(2,1)S(1)} %collective-permute-done.20.refs_2_, ...), custom_call_target="tpu_custom_call" | custom-call | flops 1 | bytes 1 | tf_op jit(solution)/shard_map/pallas_call | solution.py:434
  177.3 1.2 shard_map.100.refs_0_
  178.5 2.3 %shard_map.102.refs_0_ = f32[512,5,2,256]{3,2,1,0:T(2,128)} custom-call(s32[6]{0:T(128)S(1)} %stack.48.refs_0_.flags, f32[512,5,2,256]{3,2,1,0:T(2,128)} %shard_map.100.refs_0_, f32[192,2,256]{2,1,0:T(2,128)S(1)} %get-tuple-element.205.refs_1_, bf16[192,2,256]{2,1,0:T(2,128)(2,1)S(1)} %collective-permute-done.24.refs_2_, ...), custom_call_target="tpu_custom_call", output_to_operand_aliasing={{}: (1, {})} | custom-call | flops 1 | bytes 1 | tf_op jit(solution)/shard_map/pallas_call | solution.py:434
  180.8 2.1 %shard_map.103 = f32[512,5,2,256]{3,2,1,0:T(2,128)} custom-call(s32[6]{0:T(128)S(1)} %stack.48.refs_0_.flags, f32[512,5,2,256]{3,2,1,0:T(2,128)} %shard_map.102.refs_0_, f32[128,2,256]{2,1,0:T(2,128)S(1)} %get-tuple-element.209.refs_1_, bf16[128,2,256]{2,1,0:T(2,128)(2,1)S(1)} %collective-permute-done.28.refs_2_, ...), custom_call_target="tpu_custom_call", output_to_operand_aliasing={{}: (1, {})} | custom-call | flops 1 | bytes 1 | tf_op jit(solution)/shard_map/pallas_call | solution.py:434
  (95 shorter events, 18.3 us)
Async XLA Ops:
  6.5 116.7 %all-gather.3.cloned.1.call-start = ((), (), s32[]{:S(2)}) async-start(), calls=%async_computation | async-start | bytes 1310720 | tf_op jit(solution)/shard_map/all_gather | solution.py:556
  10.6 11.0 %copy-start.18 = (f32[5]{0:T(128)S(1)}, f32[5]{0:T(128)}, u32[]{:S(2)}) copy-start(f32[5]{0:T(128)} %param.15) | copy-start | bytes 64
  10.6 13.4 %copy-start.16 = (f32[2048]{0:T(1024)S(1)}, f32[2048]{0:T(1024)}, u32[]{:S(2)}) copy-start(f32[2048]{0:T(1024)} %param.14) | copy-start | bytes 24580
  10.7 13.4 %copy-start.19 = (pred[32]{0:T(512)(128)(4,1)S(1)}, pred[32]{0:T(512)(128)(4,1)}, u32[]{:S(2)}) copy-start(pred[32]{0:T(512)(128)(4,1)} %constant.167) | copy-start | bytes 100
  10.7 13.4 %copy-start.20 = (s32[32]{0:T(128)S(1)}, s32[32]{0:T(128)}, u32[]{:S(2)}) copy-start(s32[32]{0:T(128)} %constant.166.clone) | copy-start | bytes 388
  10.7 13.4 %copy-start.17 = (f32[2048]{0:T(1024)S(1)}, f32[2048]{0:T(1024)}, u32[]{:S(2)}) copy-start(f32[2048]{0:T(1024)} %param.13) | copy-start | bytes 24580
  12.7 26.0 %collective-permute-start.5 = (bf16[256,512]{1,0:T(8,128)(2,1)S(1)}, bf16[256,512]{1,0:T(8,128)(2,1)S(1)}, u32[]{:S(2)}, u32[]{:S(2)}) collective-permute-start(bf16[256,512]{1,0:T(8,128)(2,1)S(1)} %bitcast.24), channel_id=1, source_target_pairs={{0,24},{8,16},{16,8},{24,0},{1,25},{9,17},{17,9},{25,1},{2,26},{10... | collective-permute-start | bytes 786440 | tf_op jit(solution)/shard_map/ppermute | solution.py:486
  17.9 22.4 %collective-permute-start.4 = (bf16[256,512]{1,0:T(8,128)(2,1)S(1)}, bf16[256,512]{1,0:T(8,128)(2,1)}, u32[]{:S(2)}, u32[]{:S(2)}) collective-permute-start(bf16[256,512]{1,0:T(8,128)(2,1)S(1)} %bitcast.25), channel_id=1, source_target_pairs={{0,16},{8,24},{16,0},{24,8},{1,17},{9,25},{17,1},{25,9},{2,18},{10... | collective-permute-start | bytes 786440 | tf_op jit(solution)/shard_map/ppermute | solution.py:486
  17.9 16.9 %collective-permute-start = (bf16[256,512]{1,0:T(8,128)(2,1)S(1)}, bf16[256,512]{1,0:T(8,128)(2,1)}, u32[]{:S(2)}, u32[]{:S(2)}) collective-permute-start(bf16[256,512]{1,0:T(8,128)(2,1)S(1)} %bitcast.26), channel_id=1, source_target_pairs={{0,8},{8,0},{16,24},{24,16},{1,9},{9,1},{17,25},{25,17},{2,10},{10... | collective-permute-start | bytes 786440 | tf_op jit(solution)/shard_map/ppermute | solution.py:486
  18.5 16.3 %collective-permute-start.1 = (bf16[512,512]{1,0:T(8,128)(2,1)}, bf16[512,512]{1,0:T(8,128)(2,1)S(1)}, u32[]{:S(2)}, u32[]{:S(2)}) collective-permute-start(bf16[512,512]{1,0:T(8,128)(2,1)} %bitcast.13), channel_id=1, source_target_pairs={{0,4},{2,6},{4,0},{6,2},{1,5},{3,7},{5,1},{7,3},{8,12},{10,14},{12... | collective-permute-start | bytes 1572872 | tf_op jit(solution)/shard_map/ppermute | solution.py:483
  20.1 18.6 %collective-permute-start.6 = (bf16[384,1024]{1,0:T(8,128)(2,1)}, bf16[384,1024]{1,0:T(8,128)(2,1)}, u32[]{:S(2)}, u32[]{:S(2)}) collective-permute-start(bf16[384,1024]{1,0:T(8,128)(2,1)} %pad_maximum_fusion), channel_id=1, source_target_pairs={{0,1},{1,0},{2,3},{3,2},{4,5},{5,4},{6,7},{7,6},{8,9},{9,8},{10,11... | collective-permute-start | bytes 2359304 | tf_op jit(solution)/shard_map/ppermute | solution.py:484
  34.7 5.5 %collective-permute-start.3 = (bf16[512,512]{1,0:T(8,128)(2,1)S(1)}, bf16[512,512]{1,0:T(8,128)(2,1)S(1)}, u32[]{:S(2)}, u32[]{:S(2)}) collective-permute-start(bf16[512,512]{1,0:T(8,128)(2,1)S(1)} %bitcast.22), channel_id=1, source_target_pairs={{0,2},{2,0},{4,6},{6,4},{1,3},{3,1},{5,7},{7,5},{8,10},{10,8},{12,... | collective-permute-start | bytes 1572872 | tf_op jit(solution)/shard_map/ppermute | solution.py:482
  34.7 8.2 %copy-start.13 = (bf16[512,512]{1,0:T(8,128)(2,1)}, bf16[512,512]{1,0:T(8,128)(2,1)S(1)}, u32[]{:S(2)}) copy-start(bf16[512,512]{1,0:T(8,128)(2,1)S(1)} %collective-permute-done.1.refs_6_) | copy-start | bytes 1572868
  34.7 5.5 %collective-permute-start.2 = (bf16[512,512]{1,0:T(8,128)(2,1)S(1)}, bf16[512,512]{1,0:T(8,128)(2,1)S(1)}, u32[]{:S(2)}, u32[]{:S(2)}) collective-permute-start(bf16[512,512]{1,0:T(8,128)(2,1)S(1)} %collective-permute-done.1.refs_6_), channel_id=1, source_target_pairs={{0,2},{2,0},{4,6},{6,4},{1,3},{3,1},{5,7},{7,5},{8,10},{10,8},{12,... | collective-permute-start | bytes 1572872 | tf_op jit(solution)/shard_map/ppermute | solution.py:482
  41.4 10.5 %copy-start.5 = (bf16[4,256,512]{2,1,0:T(8,128)(2,1)}, bf16[4,256,512]{2,1,0:T(8,128)(2,1)S(1)}, u32[]{:S(2)}) copy-start(bf16[4,256,512]{2,1,0:T(8,128)(2,1)S(1)} %shard_map.92.refs_1_) | copy-start | bytes 3145732
  41.4 13.8 %copy-start.7 = (f32[32,2048]{1,0:T(8,128)S(1)}, f32[32,2048]{1,0:T(8,128)}, u32[]{:S(2)}) copy-start(f32[32,2048]{1,0:T(8,128)} %get-tuple-element.121.refs_1_) | copy-start | bytes 786436
  41.4 24.3 %collective-permute-start.10 = (bf16[4,256,512]{2,1,0:T(8,128)(2,1)S(1)}, bf16[4,256,512]{2,1,0:T(8,128)(2,1)S(1)}, u32[]{:S(2)}, u32[]{:S(2)}) collective-permute-start(bf16[4,256,512]{2,1,0:T(8,128)(2,1)S(1)} %shard_map.92.refs_1_), channel_id=1, source_target_pairs={{0,1},{1,0},{2,3},{3,2},{4,5},{5,4},{6,7},{7,6},{8,9},{9,8},{10,11... | collective-permute-start | bytes 3145736 | tf_op jit(solution)/shard_map/ppermute | solution.py:484
  43.0 12.2 %collective-permute-start.9 = (bf16[384,1024]{1,0:T(8,128)(2,1)}, bf16[384,1024]{1,0:T(8,128)(2,1)S(1)}, u32[]{:S(2)}, u32[]{:S(2)}) collective-permute-start(bf16[384,1024]{1,0:T(8,128)(2,1)} %collective-permute-done.6.refs_12_), channel_id=1, source_target_pairs={{0,2},{2,0},{4,6},{6,4},{1,3},{3,1},{5,7},{7,5},{8,10},{10,8},{12,... | collective-permute-start | bytes 2359304 | tf_op jit(solution)/shard_map/ppermute | solution.py:482
  44.9 1.0 copy-start.14
  51.9 19.2 %collective-permute-start.8 = (bf16[1024,512]{1,0:T(8,128)(2,1)S(1)}, bf16[1024,512]{1,0:T(8,128)(2,1)S(1)}, u32[]{:S(2)}, u32[]{:S(2)}) collective-permute-start(bf16[1024,512]{1,0:T(8,128)(2,1)S(1)} %shard_map.91.refs_1_), channel_id=1, source_target_pairs={{8,16},{16,8},{9,17},{17,9},{10,18},{18,10},{11,19},{19,11},{12,20... | collective-permute-start | bytes 3145736 | tf_op jit(solution)/shard_map/ppermute | solution.py:488
  52.6 33.5 %collective-permute-start.7 = (bf16[1024,512]{1,0:T(8,128)(2,1)S(1)}, bf16[1024,512]{1,0:T(8,128)(2,1)S(1)}, u32[]{:S(2)}, u32[]{:S(2)}) collective-permute-start(bf16[1024,512]{1,0:T(8,128)(2,1)S(1)} %shard_map.91.refs_1_), channel_id=1, source_target_pairs={{0,8},{8,0},{16,24},{24,16},{1,9},{9,1},{17,25},{25,17},{2,10},{10... | collective-permute-start | bytes 3145736 | tf_op jit(solution)/shard_map/ppermute | solution.py:486
  66.7 26.1 %collective-permute-start.11 = (bf16[320,512]{1,0:T(8,128)(2,1)S(1)}, bf16[320,512]{1,0:T(8,128)(2,1)S(1)}, u32[]{:S(2)}, u32[]{:S(2)}) collective-permute-start(bf16[320,512]{1,0:T(8,128)(2,1)S(1)} %get-tuple-element.143), channel_id=1, source_target_pairs={{0,8},{8,0},{16,24},{24,16},{1,9},{9,1},{17,25},{25,17},{2,10},{10... | collective-permute-start | bytes 983048 | tf_op jit(solution)/shard_map/ppermute | solution.py:486
  67.4 25.4 %collective-permute-start.12 = (bf16[320,512]{1,0:T(8,128)(2,1)S(1)}, bf16[320,512]{1,0:T(8,128)(2,1)S(1)}, u32[]{:S(2)}, u32[]{:S(2)}) collective-permute-start(bf16[320,512]{1,0:T(8,128)(2,1)S(1)} %get-tuple-element.144), channel_id=1, source_target_pairs={{0,16},{8,24},{16,0},{24,8},{1,17},{9,25},{17,1},{25,9},{2,18},{10... | collective-permute-start | bytes 983048 | tf_op jit(solution)/shard_map/ppermute | solution.py:486
  69.5 31.6 %collective-permute-start.13 = (bf16[320,512]{1,0:T(8,128)(2,1)S(1)}, bf16[320,512]{1,0:T(8,128)(2,1)S(1)}, u32[]{:S(2)}, u32[]{:S(2)}) collective-permute-start(bf16[320,512]{1,0:T(8,128)(2,1)S(1)} %get-tuple-element.145), channel_id=1, source_target_pairs={{0,24},{8,16},{16,8},{24,0},{1,25},{9,17},{17,9},{25,1},{2,26},{10... | collective-permute-start | bytes 983048 | tf_op jit(solution)/shard_map/ppermute | solution.py:486
  103.4 32.0 %collective-permute-start.14 = (bf16[1024,512]{1,0:T(8,128)(2,1)}, bf16[1024,512]{1,0:T(8,128)(2,1)S(1)}, u32[]{:S(2)}, u32[]{:S(2)}) collective-permute-start(bf16[1024,512]{1,0:T(8,128)(2,1)} %copy-done.2), channel_id=1, source_target_pairs={{8,16},{16,8},{9,17},{17,9},{10,18},{18,10},{11,19},{19,11},{12,20... | collective-permute-start | bytes 3145736 | tf_op jit(solution)/shard_map/ppermute | solution.py:488
  104.2 33.0 %collective-permute-start.15 = (bf16[1024,512]{1,0:T(8,128)(2,1)S(1)}, bf16[1024,512]{1,0:T(8,128)(2,1)}, u32[]{:S(2)}, u32[]{:S(2)}) collective-permute-start(bf16[1024,512]{1,0:T(8,128)(2,1)S(1)} %collective-permute-done.8.refs_3_), channel_id=1, source_target_pairs={{8,0},{16,24},{9,1},{17,25},{10,2},{18,26},{11,3},{19,27},{12,4},{... | collective-permute-start | bytes 3145736 | tf_op jit(solution)/shard_map/ppermute | solution.py:487
  105.7 31.6 %collective-permute-start.16 = (bf16[256,2048]{1,0:T(8,128)(2,1)}, bf16[256,2048]{1,0:T(8,128)(2,1)}, u32[]{:S(2)}, u32[]{:S(2)}) collective-permute-start(bf16[256,2048]{1,0:T(8,128)(2,1)} %copy-done.4), channel_id=1, source_target_pairs={{0,2},{2,0},{4,6},{6,4},{1,3},{3,1},{5,7},{7,5},{8,10},{10,8},{12,... | collective-permute-start | bytes 3145736 | tf_op jit(solution)/shard_map/ppermute | solution.py:482
  123.2 1.2 copy-start.6
  124.5 1.2 copy-start.11
  125.7 1.2 copy-start.12
  126.9 3.9 %copy-start.15 = (f32[32,1024]{1,0:T(8,128)S(1)}, f32[32,1024]{1,0:T(8,128)}, u32[]{:S(2)}) copy-start(f32[32,1024]{1,0:T(8,128)} %get-tuple-element.160.refs_2_) | copy-start | bytes 393220
  128.8 22.9 %copy-start.3 = (bf16[1024,512]{1,0:T(8,128)(2,1)S(1)}, bf16[1024,512]{1,0:T(8,128)(2,1)}, u32[]{:S(2)}) copy-start(bf16[1024,512]{1,0:T(8,128)(2,1)} %copy-done.2) | copy-start | bytes 3145732
  128.8 2.0 %collective-permute-start.17 = (bf16[512,512]{1,0:T(8,128)(2,1)S(1)}, bf16[512,512]{1,0:T(8,128)(2,1)S(1)}, u32[]{:S(2)}, u32[]{:S(2)}) collective-permute-start(bf16[512,512]{1,0:T(8,128)(2,1)S(1)} %shard_map.95.refs_5_), channel_id=1, source_target_pairs={{0,2},{2,0},{4,6},{6,4},{1,3},{3,1},{5,7},{7,5},{8,10},{10,8},{12,... | collective-permute-start | bytes 1572872 | tf_op jit(solution)/shard_map/ppermute | solution.py:482
  135.4 16.4 %copy-start = (bf16[1024,512]{1,0:T(8,128)(2,1)}, bf16[1024,512]{1,0:T(8,128)(2,1)S(1)}, u32[]{:S(2)}) copy-start(bf16[1024,512]{1,0:T(8,128)(2,1)S(1)} %collective-permute-done.14.refs_5_) | copy-start | bytes 3145732
  137.2 20.8 %collective-permute-start.23 = (bf16[512,2,256]{2,1,0:T(2,128)(2,1)S(1)}, bf16[512,2,256]{2,1,0:T(2,128)(2,1)S(1)}, u32[]{:S(2)}, u32[]{:S(2)}) collective-permute-start(bf16[512,2,256]{2,1,0:T(2,128)(2,1)S(1)} %get-tuple-element.172), channel_id=1, source_target_pairs={{0,4},{2,6},{4,0},{6,2},{1,5},{3,7},{5,1},{7,3},{8,12},{10,14},{12... | collective-permute-start | bytes 1572872 | tf_op jit(solution)/shard_map/ppermute | solution.py:483
  137.8 13.9 %collective-permute-start.18 = (bf16[384,512]{1,0:T(8,128)(2,1)S(1)}, bf16[384,512]{1,0:T(8,128)(2,1)S(1)}, u32[]{:S(2)}, u32[]{:S(2)}) collective-permute-start(bf16[384,512]{1,0:T(8,128)(2,1)S(1)} %get-tuple-element.220), channel_id=1, source_target_pairs={{8,0},{16,24},{9,1},{17,25},{10,2},{18,26},{11,3},{19,27},{12,4},{... | collective-permute-start | bytes 1179656 | tf_op jit(solution)/shard_map/ppermute | solution.py:487
  139.1 21.1 %collective-permute-start.22 = (bf16[384,512]{1,0:T(8,128)(2,1)S(1)}, bf16[384,512]{1,0:T(8,128)(2,1)S(1)}, u32[]{:S(2)}, u32[]{:S(2)}) collective-permute-start(bf16[384,512]{1,0:T(8,128)(2,1)S(1)} %get-tuple-element.219), channel_id=1, source_target_pairs={{8,0},{16,24},{9,1},{17,25},{10,2},{18,26},{11,3},{19,27},{12,4},{... | collective-permute-start | bytes 1179656 | tf_op jit(solution)/shard_map/ppermute | solution.py:487
  140.5 27.5 %collective-permute-start.27 = (bf16[256,512]{1,0:T(8,128)(2,1)S(1)}, bf16[256,512]{1,0:T(8,128)(2,1)S(1)}, u32[]{:S(2)}, u32[]{:S(2)}) collective-permute-start(bf16[256,512]{1,0:T(8,128)(2,1)S(1)} %slice.23), channel_id=1, source_target_pairs={{8,0},{16,24},{9,1},{17,25},{10,2},{18,26},{11,3},{19,27},{12,4},{... | collective-permute-start | bytes 786440 | tf_op jit(solution)/shard_map/ppermute | solution.py:487
  156.0 12.0 %copy-start.1 = (bf16[1024,512]{1,0:T(8,128)(2,1)S(1)}, bf16[1024,512]{1,0:T(8,128)(2,1)}, u32[]{:S(2)}) copy-start(bf16[1024,512]{1,0:T(8,128)(2,1)} %copy-done) | copy-start | bytes 3145732
  156.0 9.0 %collective-permute-start.19 = (bf16[192,2,256]{2,1,0:T(2,128)(2,1)S(1)}, bf16[192,2,256]{2,1,0:T(2,128)(2,1)S(1)}, u32[]{:S(2)}, u32[]{:S(2)}) collective-permute-start(bf16[192,2,256]{2,1,0:T(2,128)(2,1)S(1)} %get-tuple-element.179), channel_id=1, source_target_pairs={{0,1},{1,0},{2,3},{3,2},{4,5},{5,4},{6,7},{7,6},{8,9},{9,8},{10,11... | collective-permute-start | bytes 589832 | tf_op jit(solution)/shard_map/ppermute | solution.py:484
  156.6 9.9 %collective-permute-start.20 = (bf16[192,2,256]{2,1,0:T(2,128)(2,1)S(1)}, bf16[192,2,256]{2,1,0:T(2,128)(2,1)S(1)}, u32[]{:S(2)}, u32[]{:S(2)}) collective-permute-start(bf16[192,2,256]{2,1,0:T(2,128)(2,1)S(1)} %get-tuple-element.180), channel_id=1, source_target_pairs={{0,4},{2,6},{4,0},{6,2},{1,5},{3,7},{5,1},{7,3},{8,12},{10,14},{12... | collective-permute-start | bytes 589832 | tf_op jit(solution)/shard_map/ppermute | solution.py:483
  158.1 9.9 %collective-permute-start.21 = (bf16[192,2,256]{2,1,0:T(2,128)(2,1)S(1)}, bf16[192,2,256]{2,1,0:T(2,128)(2,1)S(1)}, u32[]{:S(2)}, u32[]{:S(2)}) collective-permute-start(bf16[192,2,256]{2,1,0:T(2,128)(2,1)S(1)} %get-tuple-element.181), channel_id=1, source_target_pairs={{0,5},{1,4},{2,7},{3,6},{4,1},{5,0},{6,3},{7,2},{8,13},{9,12},{10,... | collective-permute-start | bytes 589832 | tf_op jit(solution)/shard_map/ppermute | solution.py:485
  164.4 9.2 %collective-permute-start.24 = (bf16[192,2,256]{2,1,0:T(2,128)(2,1)S(1)}, bf16[192,2,256]{2,1,0:T(2,128)(2,1)S(1)}, u32[]{:S(2)}, u32[]{:S(2)}) collective-permute-start(bf16[192,2,256]{2,1,0:T(2,128)(2,1)S(1)} %get-tuple-element.189), channel_id=1, source_target_pairs={{0,1},{1,0},{2,3},{3,2},{4,5},{5,4},{6,7},{7,6},{8,9},{9,8},{10,11... | collective-permute-start | bytes 589832 | tf_op jit(solution)/shard_map/ppermute | solution.py:484
  165.0 13.6 %collective-permute-start.25 = (bf16[192,2,256]{2,1,0:T(2,128)(2,1)S(1)}, bf16[192,2,256]{2,1,0:T(2,128)(2,1)S(1)}, u32[]{:S(2)}, u32[]{:S(2)}) collective-permute-start(bf16[192,2,256]{2,1,0:T(2,128)(2,1)S(1)} %get-tuple-element.190), channel_id=1, source_target_pairs={{0,4},{2,6},{4,0},{6,2},{1,5},{3,7},{5,1},{7,3},{8,12},{10,14},{12... | collective-permute-start | bytes 589832 | tf_op jit(solution)/shard_map/ppermute | solution.py:483
  166.5 12.1 %collective-permute-start.26 = (bf16[192,2,256]{2,1,0:T(2,128)(2,1)S(1)}, bf16[192,2,256]{2,1,0:T(2,128)(2,1)S(1)}, u32[]{:S(2)}, u32[]{:S(2)}) collective-permute-start(bf16[192,2,256]{2,1,0:T(2,128)(2,1)S(1)} %get-tuple-element.191), channel_id=1, source_target_pairs={{0,5},{1,4},{2,7},{3,6},{4,1},{5,0},{6,3},{7,2},{8,13},{9,12},{10,... | collective-permute-start | bytes 589832 | tf_op jit(solution)/shard_map/ppermute | solution.py:485
  171.3 9.5 %collective-permute-start.28 = (bf16[128,2,256]{2,1,0:T(2,128)(2,1)S(1)}, bf16[128,2,256]{2,1,0:T(2,128)(2,1)S(1)}, u32[]{:S(2)}, u32[]{:S(2)}) collective-permute-start(bf16[128,2,256]{2,1,0:T(2,128)(2,1)S(1)} %get-tuple-element.202), channel_id=1, source_target_pairs={{0,1},{1,0},{2,3},{3,2},{4,5},{5,4},{6,7},{7,6},{8,9},{9,8},{10,11... | collective-permute-start | bytes 393224 | tf_op jit(solution)/shard_map/ppermute | solution.py:484
  171.9 9.0 %collective-permute-start.29 = (bf16[128,2,256]{2,1,0:T(2,128)(2,1)S(1)}, bf16[128,2,256]{2,1,0:T(2,128)(2,1)S(1)}, u32[]{:S(2)}, u32[]{:S(2)}) collective-permute-start(bf16[128,2,256]{2,1,0:T(2,128)(2,1)S(1)} %get-tuple-element.203), channel_id=1, source_target_pairs={{0,4},{2,6},{4,0},{6,2},{1,5},{3,7},{5,1},{7,3},{8,12},{10,14},{12... | collective-permute-start | bytes 393224 | tf_op jit(solution)/shard_map/ppermute | solution.py:483
  173.6 7.2 %collective-permute-start.30 = (bf16[128,2,256]{2,1,0:T(2,128)(2,1)S(1)}, bf16[128,2,256]{2,1,0:T(2,128)(2,1)S(1)}, u32[]{:S(2)}, u32[]{:S(2)}) collective-permute-start(bf16[128,2,256]{2,1,0:T(2,128)(2,1)S(1)} %get-tuple-element.204), channel_id=1, source_target_pairs={{0,5},{1,4},{2,7},{3,6},{4,1},{5,0},{6,3},{7,2},{8,13},{9,12},{10,... | collective-permute-start | bytes 393224 | tf_op jit(solution)/shard_map/ppermute | solution.py:485
  (5 other events, 4.8 us)
Sparse Core Ops, SparseCore 0:
  103.6 19.6 all-gather.2

commit v6 on v4

--- a/solution.py
+++ b/solution.py
@@ -230,12 +230,13 @@
 def focused(scale, flags, slots, others, receiver):
     n_z, rows, stations = slots.shape
     q = 2 * receiver.shape[1]
-    vmem = pl.BlockSpec(memory_space=pltpu.VMEM)
     return pl.pallas_call(
         lambda *refs: focus_kernel(scale, *refs),
         out_shape=jax.ShapeDtypeStruct((2 * q, stations), jnp.bfloat16),
-        in_specs=[pl.BlockSpec(memory_space=pltpu.SMEM)] + [vmem] * 3,
-        out_specs=vmem,
+        grid=(1,),
+        in_specs=[pl.BlockSpec(memory_space=pltpu.SMEM)]
+        + [pl.BlockSpec(v.shape, lambda i: (0, 0, 0)) for v in (slots, others, receiver)],
+        out_specs=pl.BlockSpec((2 * q, stations), lambda i: (0, 0)),
         scratch_shapes=[pltpu.VMEM((n_z * rows, stations), jnp.bfloat16)] * 2
         + [pltpu.VMEM((2 * q, n_z * rows), jnp.bfloat16)],
         compiler_params=pltpu.CompilerParams(vmem_limit_bytes=VMEM),
@@ -536,11 +537,7 @@
     n = jnp.arange(n_z * q_half // FINE, dtype=jnp.int32) * FINE
     starts = (z ^ n // q_half) * q_plane + y * q_block + c * q_half + n % q_half
     t_receiver_last = tables(f_last, starts, RCV_SL, at_rcv)
-    n = jnp.arange(2 * p_block // FINE, dtype=jnp.int32) * FINE
-    starts = jnp.where(n < p_block, here, there) + n % p_block
-    at_cores = jnp.concatenate([take(src_pos, block, a_block) for block in (s, s ^ 1)])
-    t_source_last = tables(f_last, starts, SRC_SL, at_cores)
-    t_receiver, t_receiver_last, t_source_last = step((t_receiver, t_receiver_last, t_source_last))
+    t_receiver, t_receiver_last = step((t_receiver, t_receiver_last))
     y_given = step(y_given)
     y_other = core(y_given)
     x_cross, x_other, raw = step((x_cross, x_other, raw))
@@ -551,8 +548,13 @@
     y_other = step(y_other)
     yr = receivers_of(flags, t_receiver, t_receiver_last, rcv_real, rcv_imag, y_given, y_other)
     yr, other_raw = step((yr, other_raw))
+    f_last = after(f_last, yr)
+    n = jnp.arange(2 * p_block // FINE, dtype=jnp.int32) * FINE
+    starts = jnp.where(n < p_block, here, there) + n % p_block
+    at_cores = jnp.concatenate([take(src_pos, block, a_block) for block in (s, s ^ 1)])
+    t_source_last = tables(f_last, starts, SRC_SL, at_cores)
     yr = spread(yr)
-    near, one, yr = step((near, one, yr))
+    near, one, yr, t_source_last = step((near, one, yr, t_source_last))
 
     two, three = middle(near), ends(one)
     yr_mine, yr_last = step(parted(flags, yr, q_block))

time: 193 us -> 189 us (0.979)
    ppermute x7, waiting for transfers between devices: 34.7 us -> 29.7 us  [shards_plane(): lax.ppermute(v, 'tm', [(i, i ^ d) for i in range(n_z)])]
    ppermute x5, waiting for transfers between devices: 1.3 us -> 3.34 us  [shards_plane(): over_y = lambda v: lax.ppermute(v, 'rcv', [(0, 1), (1, 0)])]
    unnamed x52 -> x58, local copies, waits for them, and re-layouts: 9.64 us -> 11.3 us
  transfers between devices with their start and end apart: 32 -> 32, of which waited for: 12 -> 14; matrix products, arithmetic and copies ran while one was open for 6% -> 5% of each run, Pallas kernels for 21% -> 21%
where the time goes in v6:
time: 189 us
  waiting for transfers between devices  64.8 us (34%)
  Pallas kernels  42.4 us (22%)
  starting transfers between devices  36.7 us (19%)
  between operations  17.5 us (9%)
  local copies, waits for them, and re-layouts  16.6 us (9%)
  other arithmetic  10.8 us (6%)
    ppermute x7, waiting for transfers between devices, shards_plane(): lax.ppermute(v, 'tm', [(i, i ^ d) for i in range(n_z)])  29.7 us
    all_gather x1, waiting for transfers between devices, shards_plane(): yr_last = lax.all_gather(yr_last, 'src', axis=0)  17.5 us
    ppermute x7, starting transfers between devices, shards_plane(): lax.ppermute(v, 'tm', [(i, i ^ d) for i in range(n_z)])  12.9 us
    ppermute x4, waiting for transfers between devices, shards_plane(): ends = lambda v: lax.ppermute(v, 'tm', [(1, 0), (2, 3)])  12.5 us
    pallas_call x3, Pallas kernels, product(): pl.pallas_call(lambda *refs: product_kernel(scale, *refs), grid=(1,), out...  11.7 us
    unnamed x58, local copies, waits for them, and re-layouts  11.3 us
    pallas_call x2, Pallas kernels, steered(): pl.pallas_call(lambda *refs: steered_kernel(sign, scale, len(parts), len(...  10.5 us
    pallas_call x1, Pallas kernels, receivers_of(): pl.pallas_call(receivers_kernel, grid_spec=pltpu.PrefetchScalarGridSpec(n...  9.11 us
  transfers between devices with their start and end apart: 32, of which 14 were waited for; matrix products, arithmetic and copies ran while one was open for 5% of the time, Pallas kernels for 21%

profile of v6, /device:TPU:0, one launch (start us, length us, event | category | flops | bytes accessed | tf_op | source)
XLA Modules:
  0.0 188.7 jit_solution(3399763955070720527)
XLA Ops:
  6.5 2.3 %constant_dynamic-slice_fusion = (bf16[1,256,512]{2,1,0:T(8,128)(2,1)}, bf16[1,256,512]{2,1,0:T(8,128)(2,1)S(1)}, bf16[1,256,512]{2,1,0:T(8,128)(2,1)S(1)}, bf16...) fusion(bf16[5,256,512]{2,1,0:T(8,128)(2,1)} %param.10, ...), kind=kLoop, calls=%fused_computation.29 | loop fusion | bytes 3145736 | tf_op jit(solution)/shard_map/jit(dynamic_index_in_dim)/dynamic_slice | solution.py:503
  10.7 1.1 dynamic-slice_bitcast_fusion
  12.8 5.1 %collective-permute-start.5 = (bf16[256,512]{1,0:T(8,128)(2,1)S(1)}, bf16[256,512]{1,0:T(8,128)(2,1)S(1)}, u32[]{:S(2)}, u32[]{:S(2)}) collective-permute-start(bf16[256,512]{1,0:T(8,128)(2,1)S(1)} %bitcast.24), channel_id=1, source_target_pairs={{0,24},{8,16},{16,8},{24,0},{1,25},{9,17},{17,9},{25,1},{2,26},{10... | collective-permute-start | bytes 786440 | tf_op jit(solution)/shard_map/ppermute | solution.py:487
  18.5 1.6 collective-permute-start.1
  20.2 1.5 collective-permute-start.6
  24.5 5.6 %multiply_sine_fusion = (f32[32,2048]{1,0:T(8,128)S(1)}, f32[32,2048]{1,0:T(8,128)}, f32[32,2048]{1,0:T(8,128)}, f32[32,2048]{1,0:T(8,128)}, f32[32,2048]{1,0:T(...) fusion(f32[32]{0:T(128)S(1)} %get-tuple-element.264, ...), kind=kLoop, calls=%fused_computation.5 | loop fusion | flops 327680 | bytes 2638336 | tf_op jit(solution)/shard_map/sin | solution.py:117
  30.6 1.1 pad_maximum_fusion.2
  31.8 3.0 %collective-permute-done.one = bf16[256,512]{1,0:T(8,128)(2,1)S(1)} collective-permute-done((bf16[256,512]{1,0:T(8,128)(2,1)S(1)}, bf16[256,512]{1,0:T(8,128)(2,1)S(1)}, u32[]{:S(2)}, u32[]{:S(2)}) %collective-permute-start) | collective-permute-done | bytes 262176 | tf_op jit(solution)/shard_map/ppermute | solution.py:487
  35.8 2.9 %collective-permute-done.6.refs_12_ = bf16[384,1024]{1,0:T(8,128)(2,1)} collective-permute-done((bf16[384,1024]{1,0:T(8,128)(2,1)}, bf16[384,1024]{1,0:T(8,128)(2,1)}, u32[]{:S(2)}, u32[]{:S(2)}) %collective-permute-start.6) | collective-permute-done | bytes 786464 | tf_op jit(solution)/shard_map/ppermute | solution.py:485
  38.8 1.4 collective-permute-done.4.two
  40.9 1.6 collective-permute-start.10
  42.5 1.0 copy-done.16
  43.5 5.9 %shard_map.91.refs_1_ = bf16[1024,512]{1,0:T(8,128)(2,1)S(1)} custom-call(s32[6]{0:T(128)S(1)} %stack.48.refs_0_.flags, f32[32,2048]{1,0:T(8,128)S(1)} %get-tuple-element.115.refs_1_, f32[32,2048]{1,0:T(8,128)S(1)} %get-tuple-element.116.refs_2_, f32[32,2048]{1,0:T(8,128)S(1)} %get-tuple-element.117.refs_3_, f32[32,2048]{1,0:T(8,128)S(1)} %get-tuple-element.118.refs_4_, ...), custom_call_target="tpu_custom_call" | custom-call | flops 1 | bytes 1 | tf_op jit(solution)/shard_map/pallas_call | solution.py:195
  50.2 2.7 %collective-permute-start.7 = (bf16[1024,512]{1,0:T(8,128)(2,1)S(1)}, bf16[1024,512]{1,0:T(8,128)(2,1)S(1)}, u32[]{:S(2)}, u32[]{:S(2)}) collective-permute-start(bf16[1024,512]{1,0:T(8,128)(2,1)S(1)} %shard_map.91.refs_1_), channel_id=1, source_target_pairs={{0,8},{8,0},{16,24},{24,16},{1,9},{9,1},{17,25},{25,17},{2,10},{10... | collective-permute-start | bytes 3145736 | tf_op jit(solution)/shard_map/ppermute | solution.py:487
  53.0 9.1 %shard_map.93 = (bf16[320,512]{1,0:T(8,128)(2,1)S(1)}, bf16[320,512]{1,0:T(8,128)(2,1)S(1)}, bf16[320,512]{1,0:T(8,128)(2,1)S(1)}, bf16[320,512]{1,0:T(8,128)(2,1)S(1)}) custom-call(s32[6]{0:T(128)S(1)} %stack.48.refs_0_.flags, f32[32,2048]{1,0:T(8,128)S(1)} %copy-done.10, f32[32,2048]{1,0:T(8,128)S(1)} %copy-done.11, f32[32,2048]{1,0:T(8,128)S(1)} %copy-done.8, ...), custom_call_target="tpu_custom_call" | custom-call | flops 1 | bytes 1 | tf_op jit(solution)/shard_map/pallas_call | solution.py:372
  68.0 2.2 %collective-permute-start.12 = (bf16[320,512]{1,0:T(8,128)(2,1)}, bf16[320,512]{1,0:T(8,128)(2,1)S(1)}, u32[]{:S(2)}, u32[]{:S(2)}) collective-permute-start(bf16[320,512]{1,0:T(8,128)(2,1)} %copy-done.22), channel_id=1, source_target_pairs={{0,16},{8,24},{16,0},{24,8},{1,17},{9,25},{17,1},{25,9},{2,18},{10... | collective-permute-start | bytes 983048 | tf_op jit(solution)/shard_map/ppermute | solution.py:487
  70.2 1.5 collective-permute-start.13
  71.7 1.7 multiply_sine_fusion.5
  73.4 10.4 %collective-permute-done.7.refs_2_ = bf16[1024,512]{1,0:T(8,128)(2,1)S(1)} collective-permute-done((bf16[1024,512]{1,0:T(8,128)(2,1)S(1)}, bf16[1024,512]{1,0:T(8,128)(2,1)S(1)}, u32[]{:S(2)}, u32[]{:S(2)}) %collective-permute-start.7) | collective-permute-done | bytes 1048608 | tf_op jit(solution)/shard_map/ppermute | solution.py:487
  83.9 6.6 %collective-permute-done.11.one = bf16[320,512]{1,0:T(8,128)(2,1)S(1)} collective-permute-done((bf16[320,512]{1,0:T(8,128)(2,1)}, bf16[320,512]{1,0:T(8,128)(2,1)S(1)}, u32[]{:S(2)}, u32[]{:S(2)}) %collective-permute-start.11) | collective-permute-done | bytes 327712 | tf_op jit(solution)/shard_map/ppermute | solution.py:487
  90.6 8.2 %collective-permute-done.13.three = bf16[320,512]{1,0:T(8,128)(2,1)S(1)} collective-permute-done((bf16[320,512]{1,0:T(8,128)(2,1)}, bf16[320,512]{1,0:T(8,128)(2,1)S(1)}, u32[]{:S(2)}, u32[]{:S(2)}) %collective-permute-start.13) | collective-permute-done | bytes 327712 | tf_op jit(solution)/shard_map/ppermute | solution.py:487
  100.4 1.0 copy-done.4
  102.9 1.5 collective-permute-start.15
  104.4 17.5 %all-gather.3.cloned.1.call-done = bf16[512,1024]{1,0:T(8,128)(2,1)} async-done(((bf16[128,1024]{1,0:T(8,128)(2,1)}), bf16[512,1024]{1,0:T(8,128)(2,1)}) %all-gather.3.cloned.1.call-update) | async-done | bytes 1048592 | tf_op jit(solution)/shard_map/all_gather | solution.py:562
  121.9 1.2 copy-done.6
  123.2 1.2 copy-done.13
  124.4 1.2 copy-done.14
  125.6 1.9 %shard_map.95.refs_5_ = bf16[512,512]{1,0:T(8,128)(2,1)S(1)} custom-call(s32[6]{0:T(128)S(1)} %stack.48.refs_0_.flags, bf16[4,256,512]{2,1,0:T(8,128)(2,1)S(1)} %copy-done.6, bf16[4,256,512]{2,1,0:T(8,128)(2,1)S(1)} %copy-done.13, bf16[4,128,1024]{2,1,0:T(8,128)(2,1)S(1)} %bitcast.28), custom_call_target="tpu_custom_call" | custom-call | flops 1 | bytes 1 | tf_op jit(solution)/shard_map/pallas_call | solution.py:233
  127.8 1.7 collective-permute-done.17.refs_6_
  129.5 4.6 %shard_map.96 = (f32[512,2,256]{2,1,0:T(2,128)S(1)}, bf16[512,2,256]{2,1,0:T(2,128)(2,1)S(1)}) custom-call(s32[6]{0:T(128)S(1)} %stack.48.refs_0_.flags, f32[32,1024]{1,0:T(8,128)S(1)} %get-tuple-element.156.refs_1_, f32[32,1024]{1,0:T(8,128)S(1)} %copy-done.17, f32[32,1024]{1,0:T(8,128)S(1)} %get-tuple-element.158.refs_3_, ...), custom_call_target="tpu_custom_call" | custom-call | flops 1 | bytes 1 | tf_op jit(solution)/shard_map/pallas_call | solution.py:195
  134.1 1.8 collective-permute-done.15.refs_4_
  136.5 1.3 collective-permute-start.18
  137.8 1.3 collective-permute-start.22
  139.2 1.3 collective-permute-start.27
  140.5 10.0 %collective-permute-done.18.refs_6_ = bf16[384,512]{1,0:T(8,128)(2,1)S(1)} collective-permute-done((bf16[384,512]{1,0:T(8,128)(2,1)S(1)}, bf16[384,512]{1,0:T(8,128)(2,1)S(1)}, u32[]{:S(2)}, u32[]{:S(2)}) %collective-permute-start.18) | collective-permute-done | bytes 393248 | tf_op jit(solution)/shard_map/ppermute | solution.py:488
  150.5 4.2 %shard_map.97 = (f32[192,2,256]{2,1,0:T(2,128)S(1)}, bf16[192,2,256]{2,1,0:T(2,128)(2,1)S(1)}, bf16[192,2,256]{2,1,0:T(2,128)(2,1)S(1)}, bf16[192,2,256]{2,1,0:T(2,128)(2,1)S(1)}) custom-call(s32[6]{0:T(128)S(1)} %stack.48.refs_0_.flags, bf16[1024,512]{1,0:T(8,128)(2,1)S(1)} %shard_map.91.refs_1_, bf16[1024,512]{1,0:T(8,128)(2,1)S(1)} %copy-done.3, ...), custom_call_target="tpu_custom_call" | custom-call | flops 1 | bytes 1 | tf_op jit(solution)/shard_map/pallas_call | solution.py:273
  155.1 1.5 collective-permute-start.20
  156.6 1.7 collective-permute-start.21
  158.9 4.2 %shard_map.98 = (f32[192,2,256]{2,1,0:T(2,128)S(1)}, bf16[192,2,256]{2,1,0:T(2,128)(2,1)S(1)}, bf16[192,2,256]{2,1,0:T(2,128)(2,1)S(1)}, bf16[192,2,256]{2,1,0:T(2,128)(2,1)S(1)}) custom-call(s32[6]{0:T(128)S(1)} %stack.48.refs_0_.flags, bf16[1024,512]{1,0:T(8,128)(2,1)S(1)} %shard_map.91.refs_1_, bf16[1024,512]{1,0:T(8,128)(2,1)S(1)} %copy-done.3, ...), custom_call_target="tpu_custom_call" | custom-call | flops 1 | bytes 1 | tf_op jit(solution)/shard_map/pallas_call | solution.py:273
  163.5 1.5 collective-permute-start.25
  165.0 1.7 collective-permute-start.26
  166.7 3.3 %shard_map.101 = (f32[128,2,256]{2,1,0:T(2,128)S(1)}, bf16[128,2,256]{2,1,0:T(2,128)(2,1)S(1)}, bf16[128,2,256]{2,1,0:T(2,128)(2,1)S(1)}, bf16[128,2,256]{2,1,0:T(2,128)(2,1)S(1)}) custom-call(s32[6]{0:T(128)S(1)} %stack.48.refs_0_.flags, bf16[1024,512]{1,0:T(8,128)(2,1)S(1)} %shard_map.91.refs_1_, bf16[1024,512]{1,0:T(8,128)(2,1)S(1)} %copy-done.3, ...), custom_call_target="tpu_custom_call" | custom-call | flops 1 | bytes 1 | tf_op jit(solution)/shard_map/pallas_call | solution.py:273
  170.4 1.5 collective-permute-start.29
  172.1 1.8 collective-permute-start.30
  173.9 2.3 %shard_map.99._ = f32[512,5,2,256]{3,2,1,0:T(2,128)} custom-call(s32[6]{0:T(128)S(1)} %stack.48.refs_0_.flags, f32[192,2,256]{2,1,0:T(2,128)S(1)} %get-tuple-element.192.refs_0_, bf16[192,2,256]{2,1,0:T(2,128)(2,1)S(1)} %collective-permute-done.19.refs_1_, bf16[192,2,256]{2,1,0:T(2,128)(2,1)S(1)} %collective-permute-done.20.refs_2_, ...), custom_call_target="tpu_custom_call" | custom-call | flops 1 | bytes 1 | tf_op jit(solution)/shard_map/pallas_call | solution.py:435
  176.2 1.2 shard_map.100.refs_0_
  177.5 2.3 %shard_map.102.refs_0_ = f32[512,5,2,256]{3,2,1,0:T(2,128)} custom-call(s32[6]{0:T(128)S(1)} %stack.48.refs_0_.flags, f32[512,5,2,256]{3,2,1,0:T(2,128)} %shard_map.100.refs_0_, f32[192,2,256]{2,1,0:T(2,128)S(1)} %get-tuple-element.205.refs_1_, bf16[192,2,256]{2,1,0:T(2,128)(2,1)S(1)} %collective-permute-done.24.refs_2_, ...), custom_call_target="tpu_custom_call", output_to_operand_aliasing={{}: (1, {})} | custom-call | flops 1 | bytes 1 | tf_op jit(solution)/shard_map/pallas_call | solution.py:435
  179.7 2.1 %shard_map.103 = f32[512,5,2,256]{3,2,1,0:T(2,128)} custom-call(s32[6]{0:T(128)S(1)} %stack.48.refs_0_.flags, f32[512,5,2,256]{3,2,1,0:T(2,128)} %shard_map.102.refs_0_, f32[128,2,256]{2,1,0:T(2,128)S(1)} %get-tuple-element.209.refs_1_, bf16[128,2,256]{2,1,0:T(2,128)(2,1)S(1)} %collective-permute-done.28.refs_2_, ...), custom_call_target="tpu_custom_call", output_to_operand_aliasing={{}: (1, {})} | custom-call | flops 1 | bytes 1 | tf_op jit(solution)/shard_map/pallas_call | solution.py:435
  (111 shorter events, 17.9 us)
Async XLA Ops:
  6.5 115.4 %all-gather.3.cloned.1.call-start = ((), (), s32[]{:S(2)}) async-start(), calls=%async_computation | async-start | bytes 1310720 | tf_op jit(solution)/shard_map/all_gather | solution.py:562
  10.7 11.0 %copy-start.26 = (f32[5]{0:T(128)S(1)}, f32[5]{0:T(128)}, u32[]{:S(2)}) copy-start(f32[5]{0:T(128)} %param.15) | copy-start | bytes 64
  10.7 13.6 %copy-start.24 = (f32[2048]{0:T(1024)S(1)}, f32[2048]{0:T(1024)}, u32[]{:S(2)}) copy-start(f32[2048]{0:T(1024)} %param.14) | copy-start | bytes 24580
  10.7 13.6 %copy-start.27 = (pred[32]{0:T(512)(128)(4,1)S(1)}, pred[32]{0:T(512)(128)(4,1)}, u32[]{:S(2)}) copy-start(pred[32]{0:T(512)(128)(4,1)} %constant.167) | copy-start | bytes 100
  10.7 13.6 %copy-start.28 = (s32[32]{0:T(128)S(1)}, s32[32]{0:T(128)}, u32[]{:S(2)}) copy-start(s32[32]{0:T(128)} %constant.166.clone) | copy-start | bytes 388
  10.7 13.7 %copy-start.25 = (f32[2048]{0:T(1024)S(1)}, f32[2048]{0:T(1024)}, u32[]{:S(2)}) copy-start(f32[2048]{0:T(1024)} %param.13) | copy-start | bytes 24580
  12.8 26.0 %collective-permute-start.5 = (bf16[256,512]{1,0:T(8,128)(2,1)S(1)}, bf16[256,512]{1,0:T(8,128)(2,1)S(1)}, u32[]{:S(2)}, u32[]{:S(2)}) collective-permute-start(bf16[256,512]{1,0:T(8,128)(2,1)S(1)} %bitcast.24), channel_id=1, source_target_pairs={{0,24},{8,16},{16,8},{24,0},{1,25},{9,17},{17,9},{25,1},{2,26},{10... | collective-permute-start | bytes 786440 | tf_op jit(solution)/shard_map/ppermute | solution.py:487
  17.9 22.3 %collective-permute-start.4 = (bf16[256,512]{1,0:T(8,128)(2,1)S(1)}, bf16[256,512]{1,0:T(8,128)(2,1)S(1)}, u32[]{:S(2)}, u32[]{:S(2)}) collective-permute-start(bf16[256,512]{1,0:T(8,128)(2,1)S(1)} %bitcast.25), channel_id=1, source_target_pairs={{0,16},{8,24},{16,0},{24,8},{1,17},{9,25},{17,1},{25,9},{2,18},{10... | collective-permute-start | bytes 786440 | tf_op jit(solution)/shard_map/ppermute | solution.py:487
  17.9 16.9 %collective-permute-start = (bf16[256,512]{1,0:T(8,128)(2,1)S(1)}, bf16[256,512]{1,0:T(8,128)(2,1)S(1)}, u32[]{:S(2)}, u32[]{:S(2)}) collective-permute-start(bf16[256,512]{1,0:T(8,128)(2,1)S(1)} %bitcast.26), channel_id=1, source_target_pairs={{0,8},{8,0},{16,24},{24,16},{1,9},{9,1},{17,25},{25,17},{2,10},{10... | collective-permute-start | bytes 786440 | tf_op jit(solution)/shard_map/ppermute | solution.py:487
  18.5 16.3 %collective-permute-start.1 = (bf16[512,512]{1,0:T(8,128)(2,1)}, bf16[512,512]{1,0:T(8,128)(2,1)S(1)}, u32[]{:S(2)}, u32[]{:S(2)}) collective-permute-start(bf16[512,512]{1,0:T(8,128)(2,1)} %bitcast.13), channel_id=1, source_target_pairs={{0,4},{2,6},{4,0},{6,2},{1,5},{3,7},{5,1},{7,3},{8,12},{10,14},{12... | collective-permute-start | bytes 1572872 | tf_op jit(solution)/shard_map/ppermute | solution.py:484
  20.2 18.6 %collective-permute-start.6 = (bf16[384,1024]{1,0:T(8,128)(2,1)}, bf16[384,1024]{1,0:T(8,128)(2,1)}, u32[]{:S(2)}, u32[]{:S(2)}) collective-permute-start(bf16[384,1024]{1,0:T(8,128)(2,1)} %pad_maximum_fusion), channel_id=1, source_target_pairs={{0,1},{1,0},{2,3},{3,2},{4,5},{5,4},{6,7},{7,6},{8,9},{9,8},{10,11... | collective-permute-start | bytes 2359304 | tf_op jit(solution)/shard_map/ppermute | solution.py:485
  34.8 5.4 %collective-permute-start.3 = (bf16[512,512]{1,0:T(8,128)(2,1)S(1)}, bf16[512,512]{1,0:T(8,128)(2,1)S(1)}, u32[]{:S(2)}, u32[]{:S(2)}) collective-permute-start(bf16[512,512]{1,0:T(8,128)(2,1)S(1)} %bitcast.22), channel_id=1, source_target_pairs={{0,2},{2,0},{4,6},{6,4},{1,3},{3,1},{5,7},{7,5},{8,10},{10,8},{12,... | collective-permute-start | bytes 1572872 | tf_op jit(solution)/shard_map/ppermute | solution.py:483
  34.8 7.7 %copy-start.15 = (bf16[512,512]{1,0:T(8,128)(2,1)}, bf16[512,512]{1,0:T(8,128)(2,1)S(1)}, u32[]{:S(2)}) copy-start(bf16[512,512]{1,0:T(8,128)(2,1)S(1)} %collective-permute-done.1.refs_6_) | copy-start | bytes 1572868
  34.8 5.4 %collective-permute-start.2 = (bf16[512,512]{1,0:T(8,128)(2,1)S(1)}, bf16[512,512]{1,0:T(8,128)(2,1)S(1)}, u32[]{:S(2)}, u32[]{:S(2)}) collective-permute-start(bf16[512,512]{1,0:T(8,128)(2,1)S(1)} %collective-permute-done.1.refs_6_), channel_id=1, source_target_pairs={{0,2},{2,0},{4,6},{6,4},{1,3},{3,1},{5,7},{7,5},{8,10},{10,8},{12,... | collective-permute-start | bytes 1572872 | tf_op jit(solution)/shard_map/ppermute | solution.py:483
  40.8 8.7 %copy-start.5 = (bf16[4,256,512]{2,1,0:T(8,128)(2,1)}, bf16[4,256,512]{2,1,0:T(8,128)(2,1)S(1)}, u32[]{:S(2)}) copy-start(bf16[4,256,512]{2,1,0:T(8,128)(2,1)S(1)} %shard_map.92.refs_1_) | copy-start | bytes 3145732
  40.8 12.1 %copy-start.7 = (f32[32,2048]{1,0:T(8,128)S(1)}, f32[32,2048]{1,0:T(8,128)}, u32[]{:S(2)}) copy-start(f32[32,2048]{1,0:T(8,128)} %get-tuple-element.126.refs_6_) | copy-start | bytes 786436
  40.8 12.1 %copy-start.8 = (f32[32,2048]{1,0:T(8,128)S(1)}, f32[32,2048]{1,0:T(8,128)}, u32[]{:S(2)}) copy-start(f32[32,2048]{1,0:T(8,128)} %get-tuple-element.122.refs_2_) | copy-start | bytes 786436
  40.8 12.1 %copy-start.9 = (f32[32,2048]{1,0:T(8,128)S(1)}, f32[32,2048]{1,0:T(8,128)}, u32[]{:S(2)}) copy-start(f32[32,2048]{1,0:T(8,128)} %get-tuple-element.123.refs_3_) | copy-start | bytes 786436
  40.8 12.1 %copy-start.10 = (f32[32,2048]{1,0:T(8,128)S(1)}, f32[32,2048]{1,0:T(8,128)}, u32[]{:S(2)}) copy-start(f32[32,2048]{1,0:T(8,128)} %get-tuple-element.120.refs_0_) | copy-start | bytes 786436
  40.9 12.1 %copy-start.11 = (f32[32,2048]{1,0:T(8,128)S(1)}, f32[32,2048]{1,0:T(8,128)}, u32[]{:S(2)}) copy-start(f32[32,2048]{1,0:T(8,128)} %get-tuple-element.121.refs_1_) | copy-start | bytes 786436
  40.9 24.3 %collective-permute-start.10 = (bf16[4,256,512]{2,1,0:T(8,128)(2,1)S(1)}, bf16[4,256,512]{2,1,0:T(8,128)(2,1)S(1)}, u32[]{:S(2)}, u32[]{:S(2)}) collective-permute-start(bf16[4,256,512]{2,1,0:T(8,128)(2,1)S(1)} %shard_map.92.refs_1_), channel_id=1, source_target_pairs={{0,1},{1,0},{2,3},{3,2},{4,5},{5,4},{6,7},{7,6},{8,9},{9,8},{10,11... | collective-permute-start | bytes 3145736 | tf_op jit(solution)/shard_map/ppermute | solution.py:485
  42.5 10.5 %collective-permute-start.9 = (bf16[384,1024]{1,0:T(8,128)(2,1)}, bf16[384,1024]{1,0:T(8,128)(2,1)S(1)}, u32[]{:S(2)}, u32[]{:S(2)}) collective-permute-start(bf16[384,1024]{1,0:T(8,128)(2,1)} %collective-permute-done.6.refs_12_), channel_id=1, source_target_pairs={{0,2},{2,0},{4,6},{6,4},{1,3},{3,1},{5,7},{7,5},{8,10},{10,8},{12,... | collective-permute-start | bytes 2359304 | tf_op jit(solution)/shard_map/ppermute | solution.py:483
  49.5 24.0 %collective-permute-start.8 = (bf16[1024,512]{1,0:T(8,128)(2,1)S(1)}, bf16[1024,512]{1,0:T(8,128)(2,1)S(1)}, u32[]{:S(2)}, u32[]{:S(2)}) collective-permute-start(bf16[1024,512]{1,0:T(8,128)(2,1)S(1)} %shard_map.91.refs_1_), channel_id=1, source_target_pairs={{8,16},{16,8},{9,17},{17,9},{10,18},{18,10},{11,19},{19,11},{12,20... | collective-permute-start | bytes 3145736 | tf_op jit(solution)/shard_map/ppermute | solution.py:489
  50.2 33.7 %collective-permute-start.7 = (bf16[1024,512]{1,0:T(8,128)(2,1)S(1)}, bf16[1024,512]{1,0:T(8,128)(2,1)S(1)}, u32[]{:S(2)}, u32[]{:S(2)}) collective-permute-start(bf16[1024,512]{1,0:T(8,128)(2,1)S(1)} %shard_map.91.refs_1_), channel_id=1, source_target_pairs={{0,8},{8,0},{16,24},{24,16},{1,9},{9,1},{17,25},{25,17},{2,10},{10... | collective-permute-start | bytes 3145736 | tf_op jit(solution)/shard_map/ppermute | solution.py:487
  67.2 23.3 %collective-permute-start.11 = (bf16[320,512]{1,0:T(8,128)(2,1)}, bf16[320,512]{1,0:T(8,128)(2,1)S(1)}, u32[]{:S(2)}, u32[]{:S(2)}) collective-permute-start(bf16[320,512]{1,0:T(8,128)(2,1)} %copy-done.23), channel_id=1, source_target_pairs={{0,8},{8,0},{16,24},{24,16},{1,9},{9,1},{17,25},{25,17},{2,10},{10... | collective-permute-start | bytes 983048 | tf_op jit(solution)/shard_map/ppermute | solution.py:487
  68.0 22.6 %collective-permute-start.12 = (bf16[320,512]{1,0:T(8,128)(2,1)}, bf16[320,512]{1,0:T(8,128)(2,1)S(1)}, u32[]{:S(2)}, u32[]{:S(2)}) collective-permute-start(bf16[320,512]{1,0:T(8,128)(2,1)} %copy-done.22), channel_id=1, source_target_pairs={{0,16},{8,24},{16,0},{24,8},{1,17},{9,25},{17,1},{25,9},{2,18},{10... | collective-permute-start | bytes 983048 | tf_op jit(solution)/shard_map/ppermute | solution.py:487
  70.2 28.6 %collective-permute-start.13 = (bf16[320,512]{1,0:T(8,128)(2,1)}, bf16[320,512]{1,0:T(8,128)(2,1)S(1)}, u32[]{:S(2)}, u32[]{:S(2)}) collective-permute-start(bf16[320,512]{1,0:T(8,128)(2,1)} %copy-done.21), channel_id=1, source_target_pairs={{0,24},{8,16},{16,8},{24,0},{1,25},{9,17},{17,9},{25,1},{2,26},{10... | collective-permute-start | bytes 983048 | tf_op jit(solution)/shard_map/ppermute | solution.py:487
  83.9 18.3 %copy-start.2 = (bf16[1024,512]{1,0:T(8,128)(2,1)}, bf16[1024,512]{1,0:T(8,128)(2,1)S(1)}, u32[]{:S(2)}) copy-start(bf16[1024,512]{1,0:T(8,128)(2,1)S(1)} %collective-permute-done.7.refs_2_) | copy-start | bytes 3145732
  102.1 32.0 %collective-permute-start.14 = (bf16[1024,512]{1,0:T(8,128)(2,1)}, bf16[1024,512]{1,0:T(8,128)(2,1)S(1)}, u32[]{:S(2)}, u32[]{:S(2)}) collective-permute-start(bf16[1024,512]{1,0:T(8,128)(2,1)} %copy-done.2), channel_id=1, source_target_pairs={{8,16},{16,8},{9,17},{17,9},{10,18},{18,10},{11,19},{19,11},{12,20... | collective-permute-start | bytes 3145736 | tf_op jit(solution)/shard_map/ppermute | solution.py:489
  102.9 33.0 %collective-permute-start.15 = (bf16[1024,512]{1,0:T(8,128)(2,1)S(1)}, bf16[1024,512]{1,0:T(8,128)(2,1)}, u32[]{:S(2)}, u32[]{:S(2)}) collective-permute-start(bf16[1024,512]{1,0:T(8,128)(2,1)S(1)} %collective-permute-done.8.refs_3_), channel_id=1, source_target_pairs={{8,0},{16,24},{9,1},{17,25},{10,2},{18,26},{11,3},{19,27},{12,4},{... | collective-permute-start | bytes 3145736 | tf_op jit(solution)/shard_map/ppermute | solution.py:488
  104.4 31.6 %collective-permute-start.16 = (bf16[256,2048]{1,0:T(8,128)(2,1)}, bf16[256,2048]{1,0:T(8,128)(2,1)}, u32[]{:S(2)}, u32[]{:S(2)}) collective-permute-start(bf16[256,2048]{1,0:T(8,128)(2,1)} %copy-done.4), channel_id=1, source_target_pairs={{0,2},{2,0},{4,6},{6,4},{1,3},{3,1},{5,7},{7,5},{8,10},{10,8},{12,... | collective-permute-start | bytes 3145736 | tf_op jit(solution)/shard_map/ppermute | solution.py:483
  127.5 22.9 %copy-start.3 = (bf16[1024,512]{1,0:T(8,128)(2,1)S(1)}, bf16[1024,512]{1,0:T(8,128)(2,1)}, u32[]{:S(2)}) copy-start(bf16[1024,512]{1,0:T(8,128)(2,1)} %copy-done.2) | copy-start | bytes 3145732
  127.5 2.0 %collective-permute-start.17 = (bf16[512,512]{1,0:T(8,128)(2,1)S(1)}, bf16[512,512]{1,0:T(8,128)(2,1)S(1)}, u32[]{:S(2)}, u32[]{:S(2)}) collective-permute-start(bf16[512,512]{1,0:T(8,128)(2,1)S(1)} %shard_map.95.refs_5_), channel_id=1, source_target_pairs={{0,2},{2,0},{4,6},{6,4},{1,3},{3,1},{5,7},{7,5},{8,10},{10,8},{12,... | collective-permute-start | bytes 1572872 | tf_op jit(solution)/shard_map/ppermute | solution.py:483
  134.1 16.3 %copy-start = (bf16[1024,512]{1,0:T(8,128)(2,1)}, bf16[1024,512]{1,0:T(8,128)(2,1)S(1)}, u32[]{:S(2)}) copy-start(bf16[1024,512]{1,0:T(8,128)(2,1)S(1)} %collective-permute-done.14.refs_5_) | copy-start | bytes 3145732
  135.9 20.7 %collective-permute-start.23 = (bf16[512,2,256]{2,1,0:T(2,128)(2,1)S(1)}, bf16[512,2,256]{2,1,0:T(2,128)(2,1)S(1)}, u32[]{:S(2)}, u32[]{:S(2)}) collective-permute-start(bf16[512,2,256]{2,1,0:T(2,128)(2,1)S(1)} %get-tuple-element.172), channel_id=1, source_target_pairs={{0,4},{2,6},{4,0},{6,2},{1,5},{3,7},{5,1},{7,3},{8,12},{10,14},{12... | collective-permute-start | bytes 1572872 | tf_op jit(solution)/shard_map/ppermute | solution.py:484
  136.5 13.9 %collective-permute-start.18 = (bf16[384,512]{1,0:T(8,128)(2,1)S(1)}, bf16[384,512]{1,0:T(8,128)(2,1)S(1)}, u32[]{:S(2)}, u32[]{:S(2)}) collective-permute-start(bf16[384,512]{1,0:T(8,128)(2,1)S(1)} %get-tuple-element.220), channel_id=1, source_target_pairs={{8,0},{16,24},{9,1},{17,25},{10,2},{18,26},{11,3},{19,27},{12,4},{... | collective-permute-start | bytes 1179656 | tf_op jit(solution)/shard_map/ppermute | solution.py:488
  137.8 21.1 %collective-permute-start.22 = (bf16[384,512]{1,0:T(8,128)(2,1)S(1)}, bf16[384,512]{1,0:T(8,128)(2,1)S(1)}, u32[]{:S(2)}, u32[]{:S(2)}) collective-permute-start(bf16[384,512]{1,0:T(8,128)(2,1)S(1)} %get-tuple-element.219), channel_id=1, source_target_pairs={{8,0},{16,24},{9,1},{17,25},{10,2},{18,26},{11,3},{19,27},{12,4},{... | collective-permute-start | bytes 1179656 | tf_op jit(solution)/shard_map/ppermute | solution.py:488
  139.2 27.5 %collective-permute-start.27 = (bf16[256,512]{1,0:T(8,128)(2,1)S(1)}, bf16[256,512]{1,0:T(8,128)(2,1)S(1)}, u32[]{:S(2)}, u32[]{:S(2)}) collective-permute-start(bf16[256,512]{1,0:T(8,128)(2,1)S(1)} %slice.23), channel_id=1, source_target_pairs={{8,0},{16,24},{9,1},{17,25},{10,2},{18,26},{11,3},{19,27},{12,4},{... | collective-permute-start | bytes 786440 | tf_op jit(solution)/shard_map/ppermute | solution.py:488
  154.7 12.0 %copy-start.1 = (bf16[1024,512]{1,0:T(8,128)(2,1)S(1)}, bf16[1024,512]{1,0:T(8,128)(2,1)}, u32[]{:S(2)}) copy-start(bf16[1024,512]{1,0:T(8,128)(2,1)} %copy-done) | copy-start | bytes 3145732
  154.7 8.8 %collective-permute-start.19 = (bf16[192,2,256]{2,1,0:T(2,128)(2,1)S(1)}, bf16[192,2,256]{2,1,0:T(2,128)(2,1)S(1)}, u32[]{:S(2)}, u32[]{:S(2)}) collective-permute-start(bf16[192,2,256]{2,1,0:T(2,128)(2,1)S(1)} %get-tuple-element.179), channel_id=1, source_target_pairs={{0,1},{1,0},{2,3},{3,2},{4,5},{5,4},{6,7},{7,6},{8,9},{9,8},{10,11... | collective-permute-start | bytes 589832 | tf_op jit(solution)/shard_map/ppermute | solution.py:485
  155.1 9.9 %collective-permute-start.20 = (bf16[192,2,256]{2,1,0:T(2,128)(2,1)S(1)}, bf16[192,2,256]{2,1,0:T(2,128)(2,1)S(1)}, u32[]{:S(2)}, u32[]{:S(2)}) collective-permute-start(bf16[192,2,256]{2,1,0:T(2,128)(2,1)S(1)} %get-tuple-element.180), channel_id=1, source_target_pairs={{0,4},{2,6},{4,0},{6,2},{1,5},{3,7},{5,1},{7,3},{8,12},{10,14},{12... | collective-permute-start | bytes 589832 | tf_op jit(solution)/shard_map/ppermute | solution.py:484
  156.6 10.1 %collective-permute-start.21 = (bf16[192,2,256]{2,1,0:T(2,128)(2,1)S(1)}, bf16[192,2,256]{2,1,0:T(2,128)(2,1)S(1)}, u32[]{:S(2)}, u32[]{:S(2)}) collective-permute-start(bf16[192,2,256]{2,1,0:T(2,128)(2,1)S(1)} %get-tuple-element.181), channel_id=1, source_target_pairs={{0,5},{1,4},{2,7},{3,6},{4,1},{5,0},{6,3},{7,2},{8,13},{9,12},{10,... | collective-permute-start | bytes 589832 | tf_op jit(solution)/shard_map/ppermute | solution.py:486
  163.1 9.0 %collective-permute-start.24 = (bf16[192,2,256]{2,1,0:T(2,128)(2,1)S(1)}, bf16[192,2,256]{2,1,0:T(2,128)(2,1)S(1)}, u32[]{:S(2)}, u32[]{:S(2)}) collective-permute-start(bf16[192,2,256]{2,1,0:T(2,128)(2,1)S(1)} %get-tuple-element.189), channel_id=1, source_target_pairs={{0,1},{1,0},{2,3},{3,2},{4,5},{5,4},{6,7},{7,6},{8,9},{9,8},{10,11... | collective-permute-start | bytes 589832 | tf_op jit(solution)/shard_map/ppermute | solution.py:485
  163.5 14.0 %collective-permute-start.25 = (bf16[192,2,256]{2,1,0:T(2,128)(2,1)S(1)}, bf16[192,2,256]{2,1,0:T(2,128)(2,1)S(1)}, u32[]{:S(2)}, u32[]{:S(2)}) collective-permute-start(bf16[192,2,256]{2,1,0:T(2,128)(2,1)S(1)} %get-tuple-element.190), channel_id=1, source_target_pairs={{0,4},{2,6},{4,0},{6,2},{1,5},{3,7},{5,1},{7,3},{8,12},{10,14},{12... | collective-permute-start | bytes 589832 | tf_op jit(solution)/shard_map/ppermute | solution.py:484
  165.0 12.5 %collective-permute-start.26 = (bf16[192,2,256]{2,1,0:T(2,128)(2,1)S(1)}, bf16[192,2,256]{2,1,0:T(2,128)(2,1)S(1)}, u32[]{:S(2)}, u32[]{:S(2)}) collective-permute-start(bf16[192,2,256]{2,1,0:T(2,128)(2,1)S(1)} %get-tuple-element.191), channel_id=1, source_target_pairs={{0,5},{1,4},{2,7},{3,6},{4,1},{5,0},{6,3},{7,2},{8,13},{9,12},{10,... | collective-permute-start | bytes 589832 | tf_op jit(solution)/shard_map/ppermute | solution.py:486
  170.0 9.8 %collective-permute-start.28 = (bf16[128,2,256]{2,1,0:T(2,128)(2,1)S(1)}, bf16[128,2,256]{2,1,0:T(2,128)(2,1)S(1)}, u32[]{:S(2)}, u32[]{:S(2)}) collective-permute-start(bf16[128,2,256]{2,1,0:T(2,128)(2,1)S(1)} %get-tuple-element.202), channel_id=1, source_target_pairs={{0,1},{1,0},{2,3},{3,2},{4,5},{5,4},{6,7},{7,6},{8,9},{9,8},{10,11... | collective-permute-start | bytes 393224 | tf_op jit(solution)/shard_map/ppermute | solution.py:485
  170.4 9.4 %collective-permute-start.29 = (bf16[128,2,256]{2,1,0:T(2,128)(2,1)S(1)}, bf16[128,2,256]{2,1,0:T(2,128)(2,1)S(1)}, u32[]{:S(2)}, u32[]{:S(2)}) collective-permute-start(bf16[128,2,256]{2,1,0:T(2,128)(2,1)S(1)} %get-tuple-element.203), channel_id=1, source_target_pairs={{0,4},{2,6},{4,0},{6,2},{1,5},{3,7},{5,1},{7,3},{8,12},{10,14},{12... | collective-permute-start | bytes 393224 | tf_op jit(solution)/shard_map/ppermute | solution.py:484
  172.1 7.6 %collective-permute-start.30 = (bf16[128,2,256]{2,1,0:T(2,128)(2,1)S(1)}, bf16[128,2,256]{2,1,0:T(2,128)(2,1)S(1)}, u32[]{:S(2)}, u32[]{:S(2)}) collective-permute-start(bf16[128,2,256]{2,1,0:T(2,128)(2,1)S(1)} %get-tuple-element.204), channel_id=1, source_target_pairs={{0,5},{1,4},{2,7},{3,6},{4,1},{5,0},{6,3},{7,2},{8,13},{9,12},{10,... | collective-permute-start | bytes 393224 | tf_op jit(solution)/shard_map/ppermute | solution.py:486
  (13 other events, 15.2 us)
Sparse Core Ops, SparseCore 0:
  102.3 19.6 all-gather.2
